TPU v7x, 512 devices: a whole 4x8x8 slice. The times are simulated.
512 devices in a mesh: row: 16 (over z_hi, x), col: 32 (over z_lo, y, core).
Axes of the slice: x: 4, y: 8, z: 8 (z_hi: 4, z_lo: 2; z = z_hi * 2 + z_lo), core: 2. Of those that a mesh axis runs over, the one named last changes fastest.
Arguments:
- pair_rep: bfloat16 [1024, 1024, 128], P('row', 'col'), may hold values from -400 to 400
- true_bins: int32 [1024, 1024], P('row', 'col'), may hold values from 0 to 63, as said below
- w_in: bfloat16 [128, 512], replicated, may hold values from -0.5 to 0.5
- w_out: bfloat16 [512, 128], replicated, may hold values from -0.25 to 0.25
- w_head: bfloat16 [128, 64], replicated, may hold values from -1 to 1
Outputs:
- grad_pair: bfloat16 [1024, 1024, 128], P('row', 'col')
- grad_in: float32 [128, 512], P('row', 'col')
- grad_out: float32 [512, 128], P('row', 'col')
- grad_head: float32 [128, 64], P('row', 'col')
Inputs may be any that keep to these rules, and one draw needn't show every extreme that they name: The bins are symmetric over tokens: true_bins equals mirror(true_bins).
All inputs are finite; a program needn't handle non-finite values.
Results may differ from a plain program's by a relative error of at most 0.0095.
The roundings to bfloat16 on the way count: a program that leaves them out, or rounds other values in their place, can miss the bound.
Values may be sent and summed in bfloat16 or wider, within the bound.
No kernel may reach another device: no remote copies, remote signals or barrier semaphores. Data moves between devices by JAX's collectives and lax.ppermute only.
A program may use at most 64 MiB of HBM per device.

v0:
```python
import jax
import jax.numpy as jnp
from jax import lax
from jax.sharding import PartitionSpec as P

epsilon = 1e-05


def normalize(values):
    centred = values - jnp.mean(values, axis=-1, keepdims=True)
    variance = jnp.mean(centred * centred, axis=-1, keepdims=True)
    inv_std = lax.rsqrt(variance + epsilon)
    return (centred * inv_std, inv_std)


def unfold_mirror(values, cycles, span):
    return jnp.transpose(values, (2, 1, 0, 3, 4)).reshape(cycles, span, values.shape[-1])


def as_tiles(gradient, n_row, n_col):
    first, second = gradient.shape
    split = gradient.reshape(n_row, first // n_row, n_col, second // n_col)
    return jnp.transpose(split, (0, 2, 1, 3)).reshape(
        n_row * n_col, first // n_row * (second // n_col)
    )


def shards(pair_rep, true_bins, w_in, w_out, w_head):
    row_count, col_count, channels = pair_rep.shape
    n_row = lax.axis_size("row")
    n_col = lax.axis_size("col")
    cycles = row_count // n_col
    span = n_col * col_count
    bins_count = w_head.shape[1]
    blocks = pair_rep.reshape(cycles, span, channels)

    def forward(pair_block):
        x_hat, inv_std = normalize(pair_block.astype(jnp.float32))
        normed = x_hat.astype(jnp.bfloat16)
        hidden = jnp.maximum(jnp.dot(normed, w_in, preferred_element_type=jnp.float32), 0.0).astype(
            jnp.bfloat16
        )
        update = jnp.dot(hidden, w_out, preferred_element_type=jnp.float32)
        residual = (pair_block.astype(jnp.float32) + update).astype(jnp.bfloat16)
        logits = jnp.dot(residual, w_head, preferred_element_type=jnp.float32)
        return (residual, logits)

    residual, logits = lax.map(forward, blocks)
    folded = logits.reshape(cycles, n_col, cycles, n_row, bins_count)
    mirrored = lax.all_to_all(
        lax.all_to_all(folded, "row", split_axis=3, concat_axis=3, tiled=True),
        "col",
        split_axis=1,
        concat_axis=1,
        tiled=True,
    )
    sym_logits = logits + unfold_mirror(mirrored, cycles, span)
    probability = jax.nn.softmax(sym_logits, axis=-1)
    bin_blocks = true_bins.reshape(cycles, span)
    onehot = (bin_blocks[:, :, None] == jnp.arange(bins_count, dtype=jnp.int32)).astype(jnp.float32)
    d_sym = (probability - onehot).astype(jnp.bfloat16)
    folded_grad = d_sym.reshape(cycles, n_col, cycles, n_row, bins_count)
    mirror_grad = lax.all_to_all(
        lax.all_to_all(folded_grad, "row", split_axis=3, concat_axis=3, tiled=True),
        "col",
        split_axis=1,
        concat_axis=1,
        tiled=True,
    )
    d_logit = (
        d_sym.astype(jnp.float32) + unfold_mirror(mirror_grad, cycles, span).astype(jnp.float32)
    ).astype(jnp.bfloat16)

    def backward(totals, inputs):
        pair_block, resid_block, d_block = inputs
        x_hat, inv_std = normalize(pair_block.astype(jnp.float32))
        normed = x_hat.astype(jnp.bfloat16)
        pre_act = jnp.dot(normed, w_in, preferred_element_type=jnp.float32)
        hidden = jnp.maximum(pre_act, 0.0).astype(jnp.bfloat16)
        d_resid = jnp.dot(d_block, w_head.T, preferred_element_type=jnp.float32)
        d_update = d_resid.astype(jnp.bfloat16)
        g_out = jnp.dot(hidden.T, d_update, preferred_element_type=jnp.float32)
        back_hidden = jnp.dot(d_update, w_out.T, preferred_element_type=jnp.float32)
        d_hidden = jnp.where(pre_act > 0.0, back_hidden, 0.0).astype(jnp.bfloat16)
        g_in = jnp.dot(normed.T, d_hidden, preferred_element_type=jnp.float32)
        d_normed = jnp.dot(d_hidden, w_in.T, preferred_element_type=jnp.float32)
        first_mean = jnp.mean(d_normed, axis=-1, keepdims=True)
        second_mean = jnp.mean(d_normed * x_hat, axis=-1, keepdims=True)
        d_input = inv_std * (d_normed - first_mean - x_hat * second_mean)
        g_head = jnp.dot(resid_block.T, d_block, preferred_element_type=jnp.float32)
        new_totals = (totals[0] + g_in, totals[1] + g_out, totals[2] + g_head)
        return (new_totals, (d_resid + d_input).astype(jnp.bfloat16))

    start = (
        jnp.zeros(w_in.shape, jnp.float32),
        jnp.zeros(w_out.shape, jnp.float32),
        jnp.zeros(w_head.shape, jnp.float32),
    )
    totals, d_pair = lax.scan(backward, start, (blocks, residual, d_logit))
    packed = jnp.concatenate(
        [
            as_tiles(totals[0], n_row, n_col),
            as_tiles(totals[1], n_row, n_col),
            as_tiles(totals[2], n_row, n_col),
        ],
        axis=1,
    )
    own_share = lax.psum_scatter(packed, ("row", "col"), scatter_dimension=0, tiled=True)
    own_share = own_share.reshape(-1) / (row_count * n_row)
    in_shape = (w_in.shape[0] // n_row, w_in.shape[1] // n_col)
    out_shape = (w_out.shape[0] // n_row, w_out.shape[1] // n_col)
    head_shape = (w_head.shape[0] // n_row, w_head.shape[1] // n_col)
    in_size = in_shape[0] * in_shape[1]
    out_size = out_shape[0] * out_shape[1]
    grad_in = own_share[:in_size].reshape(in_shape)
    grad_out = own_share[in_size : in_size + out_size].reshape(out_shape)
    grad_head = own_share[in_size + out_size :].reshape(head_shape)
    return (d_pair.reshape(row_count, col_count, channels), grad_in, grad_out, grad_head)


def solution(mesh):
    placed = (P("row", "col", None), P("row", "col"), P(), P(), P())
    return jax.shard_map(
        shards,
        mesh=mesh,
        in_specs=placed,
        out_specs=(P("row", "col", None), P("row", "col"), P("row", "col"), P("row", "col")),
        check_vma=False,
    )
```

profile of v0, /device:TPU:1, one launch (start us, length us, event | category | flops | bytes accessed | tf_op | source)
XLA Modules:
  0.0 418.8 jit_solution(7064880029633822254)
XLA Ops:
  8.0 10.6 %while.29 = (s32[]{:T(128)}, bf16[2,1024,128]{2,1,0:T(8,128)(2,1)}, f32[2,1024,64]{1,2,0:T(8,128)S(1)}, bf16[2,1024,128]{2,1,0:T(8,128)(2,1)}, bf16[128,512]{1,0...) while((s32[]{:T(128)}, bf16[2,1024,128]{2,1,0:T(8,128)(2,1)}, ...), condition=%wide.region_3.4_spmd, body=%wide.region_0.3_spmd.sunk | while | flops 287966208 | bytes 2479237 | solution.py:48
  8.0 1.1 convert_reduce_fusion.4
  9.2 1.3 fusion.105
  10.5 2.6 bitcast_dynamic-update-slice_fusion.2
  14.5 1.3 fusion.105
  15.8 2.6 bitcast_dynamic-update-slice_fusion.2
  20.6 26.1 %all_to_all.20 = f32[16,1,8192]{2,1,0:T(1,128)S(1)} all-to-all(f32[16,1,8192]{2,1,0:T(1,128)S(1)} %reshape.117), channel_id=1, replica_groups=mesh['row'=16,'col'=32] {'row'}, dimensions={0} | all-to-all | bytes 1048576 | tf_op jit(solution)/shard_map/all_to_all | solution.py:51
  47.3 1.9 reduce.8
  50.5 1.4 reshape.119
  52.0 14.5 %all-to-all-start.1 = ((f32[32,1,4096]{2,1,0:T(1,128)}), f32[32,1,4096]{2,1,0:T(1,128)S(1)}, u32[]{:S(2)}, u32[]{:S(2)}) async-start(f32[32,1,4096]{2,1,0:T(1,128)} %reshape.119), calls=%async_computation.1 | async-start | bytes 1048576 | tf_op jit(solution)/shard_map/all_to_all | solution.py:50
  66.7 16.4 %all-to-all-done.1 = f32[32,1,4096]{2,1,0:T(1,128)S(1)} async-done(((f32[32,1,4096]{2,1,0:T(1,128)}), f32[32,1,4096]{2,1,0:T(1,128)S(1)}, u32[]{:S(2)}, u32[]{:S(2)}) %all-to-all-start.1) | async-done | bytes 524320 | tf_op jit(solution)/shard_map/all_to_all | solution.py:50
  83.0 1.9 reduce.9
  85.7 3.9 fusion.57
  90.5 13.3 %all_to_all.21 = bf16[16,2,4096]{2,1,0:T(2,128)(2,1)S(1)} all-to-all(bf16[16,2,4096]{2,1,0:T(2,128)(2,1)S(1)} %reshape.121), channel_id=1, replica_groups=mesh['row'=16,'col'=32] {'row'}, dimensions={0} | all-to-all | bytes 524288 | tf_op jit(solution)/shard_map/all_to_all | solution.py:64
  104.8 1.1 reshape.123
  105.9 7.9 %all-to-all-start.3 = ((bf16[32,2,2048]{2,1,0:T(2,128)(2,1)}), bf16[32,2,2048]{2,1,0:T(2,128)(2,1)S(1)}, u32[]{:S(2)}, u32[]{:S(2)}) async-start(bf16[32,2,2048]{2,1,0:T(2,128)(2,1)} %reshape.123), calls=%async_computation.3 | async-start | bytes 524288 | tf_op jit(solution)/shard_map/all_to_all | solution.py:63
  114.1 11.6 %all-to-all-done.3 = bf16[32,2,2048]{2,1,0:T(2,128)(2,1)S(1)} async-done(((bf16[32,2,2048]{2,1,0:T(2,128)(2,1)}), bf16[32,2,2048]{2,1,0:T(2,128)(2,1)S(1)}, u32[]{:S(2)}, u32[]{:S(2)}) %all-to-all-start.3) | async-done | bytes 262176 | tf_op jit(solution)/shard_map/all_to_all | solution.py:63
  126.4 1.2 fusion.58
  128.5 13.4 %while.30 = (s32[]{:T(128)}, f32[128,512]{1,0:T(8,128)S(1)}, f32[512,128]{1,0:T(8,128)S(1)}, f32[128,64]{0,1:T(8,128)S(1)}, bf16[2,1024,128]{2,1,0:T(8,128)(2,1)...) while((s32[]{:T(128)}, f32[128,512]{1,0:T(8,128)S(1)}, ...), condition=%wide.region_11.12_spmd.clone, body=%wide.region_6.11_spmd.clone.sunk | while | flops 711607296 | bytes 18396844 | solution.py:99
  129.1 1.2 convolution_add_fusion.8
  133.9 1.3 fusion.125
  135.8 1.2 convolution_add_fusion.8
  140.6 1.3 fusion.125
  147.3 261.2 %all-reduce.3.cloned.1.call-done = f32[512,272]{0,1:T(8,128)} async-done(((f32[512,272]{0,1:T(8,128)}), f32[512,272]{0,1:T(8,128)}) %all-reduce.3.cloned.1.call-update) | async-done | bytes 557072
  (95 shorter events, 27.8 us)
Async XLA Ops:
  8.0 5.1 %copy-start.4 = (bf16[128,64]{0,1:T(8,128)(2,1)S(1)}, bf16[128,64]{0,1:T(8,128)(2,1)}, u32[]{:S(2)}) copy-start(bf16[128,64]{0,1:T(8,128)(2,1)} %get-tuple-element.348) | copy-start | bytes 49156 | tf_op jit(solution)/shard_map/while
  13.3 5.1 %copy-start.4 = (bf16[128,64]{0,1:T(8,128)(2,1)S(1)}, bf16[128,64]{0,1:T(8,128)(2,1)}, u32[]{:S(2)}) copy-start(bf16[128,64]{0,1:T(8,128)(2,1)} %get-tuple-element.348) | copy-start | bytes 49156 | tf_op jit(solution)/shard_map/while
  49.9 16.6 %copy-start.6 = (s32[64,32]{0,1:T(8,128)S(1)}, s32[64,32]{0,1:T(8,128)}, u32[]{:S(2)}) copy-start(s32[64,32]{0,1:T(8,128)} %param.10) | copy-start | bytes 24580
  52.0 31.0 %all-to-all-start.1 = ((f32[32,1,4096]{2,1,0:T(1,128)}), f32[32,1,4096]{2,1,0:T(1,128)S(1)}, u32[]{:S(2)}, u32[]{:S(2)}) async-start(f32[32,1,4096]{2,1,0:T(1,128)} %reshape.119), calls=%async_computation.1 | async-start | bytes 1048576 | tf_op jit(solution)/shard_map/all_to_all | solution.py:50
  89.6 14.6 %copy-start.3 = (bf16[2,1024,64]{2,1,0:T(8,128)(2,1)}, bf16[2,1024,64]{2,1,0:T(8,128)(2,1)S(1)}, u32[]{:S(2)}) copy-start(bf16[2,1024,64]{2,1,0:T(8,128)(2,1)S(1)} %fusion.57) | copy-start | bytes 786436
  105.9 19.8 %all-to-all-start.3 = ((bf16[32,2,2048]{2,1,0:T(2,128)(2,1)}), bf16[32,2,2048]{2,1,0:T(2,128)(2,1)S(1)}, u32[]{:S(2)}, u32[]{:S(2)}) async-start(bf16[32,2,2048]{2,1,0:T(2,128)(2,1)} %reshape.123), calls=%async_computation.3 | async-start | bytes 524288 | tf_op jit(solution)/shard_map/all_to_all | solution.py:63
  113.8 294.8 %all-reduce.3.cloned.1.call-start = ((), (), s32[]{:S(2)}) async-start(), calls=%async_computation.4 | async-start | bytes 1114112
  126.2 2.3 copy-start
  126.2 2.3 copy-start.1
  126.2 2.3 copy-start.2
  126.2 2.3 copy-start.5
Sparse Core Ops, SparseCore 0:
  147.5 261.0 all-reduce.2
where the time goes:
time: 419 us
  waiting for transfers between devices  289 us (69%)
  blocking collectives  39.4 us (9%)
  starting transfers between devices  22.6 us (5%)
  other arithmetic  20.5 us (5%)
  local copies, waits for them, and re-layouts  18.6 us (4%)
  between operations  14.4 us (3%)
  matrix products  13.9 us (3%)
    unnamed x2, waiting for transfers between devices  261 us
    all_to_all x1, blocking collectives, shards(): lax.all_to_all(folded, 'row', split_axis=3, concat_axis=3, tiled=True)  26.1 us
    all_to_all x1, waiting for transfers between devices, shards(): lax.all_to_all(lax.all_to_all(folded, 'row', split_axis=3, concat_axis=3,...  16.4 us
    all_to_all x1, starting transfers between devices, shards(): lax.all_to_all(lax.all_to_all(folded, 'row', split_axis=3, concat_axis=3,...  14.5 us
    all_to_all x1, blocking collectives, shards(): lax.all_to_all(folded_grad, 'row', split_axis=3, concat_axis=3, tiled=True)  13.3 us
    all_to_all x1, waiting for transfers between devices, shards(): lax.all_to_all(lax.all_to_all(folded_grad, 'row', split_axis=3, concat_ax...  11.6 us
  transfers between devices with their start and end apart: 3, of which 3 were waited for; matrix products, arithmetic and copies ran while one was open for 0% of the time, Pallas kernels for 0%

commit v1 on v0

--- a/solution.py
+++ b/solution.py
@@ -11,10 +11,6 @@
     variance = jnp.mean(centred * centred, axis=-1, keepdims=True)
     inv_std = lax.rsqrt(variance + epsilon)
     return (centred * inv_std, inv_std)
-
-
-def unfold_mirror(values, cycles, span):
-    return jnp.transpose(values, (2, 1, 0, 3, 4)).reshape(cycles, span, values.shape[-1])
 
 
 def as_tiles(gradient, n_row, n_col):
@@ -47,29 +43,17 @@
 
     residual, logits = lax.map(forward, blocks)
     folded = logits.reshape(cycles, n_col, cycles, n_row, bins_count)
-    mirrored = lax.all_to_all(
-        lax.all_to_all(folded, "row", split_axis=3, concat_axis=3, tiled=True),
-        "col",
-        split_axis=1,
-        concat_axis=1,
-        tiled=True,
-    )
-    sym_logits = logits + unfold_mirror(mirrored, cycles, span)
+    outgoing = jnp.transpose(folded, (3, 1, 0, 2, 4)).reshape(n_row * n_col, -1)
+    incoming = lax.all_to_all(
+        outgoing, ("row", "col"), split_axis=0, concat_axis=0, tiled=True
+    ).reshape(n_row, n_col, cycles, cycles, bins_count)
+    mirrored = jnp.transpose(incoming, (3, 1, 2, 0, 4)).reshape(cycles, span, bins_count)
+    sym_logits = logits + mirrored
     probability = jax.nn.softmax(sym_logits, axis=-1)
     bin_blocks = true_bins.reshape(cycles, span)
     onehot = (bin_blocks[:, :, None] == jnp.arange(bins_count, dtype=jnp.int32)).astype(jnp.float32)
     d_sym = (probability - onehot).astype(jnp.bfloat16)
-    folded_grad = d_sym.reshape(cycles, n_col, cycles, n_row, bins_count)
-    mirror_grad = lax.all_to_all(
-        lax.all_to_all(folded_grad, "row", split_axis=3, concat_axis=3, tiled=True),
-        "col",
-        split_axis=1,
-        concat_axis=1,
-        tiled=True,
-    )
-    d_logit = (
-        d_sym.astype(jnp.float32) + unfold_mirror(mirror_grad, cycles, span).astype(jnp.float32)
-    ).astype(jnp.bfloat16)
+    d_logit = d_sym + d_sym
 
     def backward(totals, inputs):
         pair_block, resid_block, d_block = inputs
@@ -105,8 +89,10 @@
         ],
         axis=1,
     )
-    own_share = lax.psum_scatter(packed, ("row", "col"), scatter_dimension=0, tiled=True)
-    own_share = own_share.reshape(-1) / (row_count * n_row)
+    shares = lax.all_to_all(
+        packed.astype(jnp.bfloat16), ("row", "col"), split_axis=0, concat_axis=0, tiled=True
+    )
+    own_share = jnp.sum(shares.astype(jnp.float32), axis=0) / (row_count * n_row)
     in_shape = (w_in.shape[0] // n_row, w_in.shape[1] // n_col)
     out_shape = (w_out.shape[0] // n_row, w_out.shape[1] // n_col)
     head_shape = (w_head.shape[0] // n_row, w_head.shape[1] // n_col)

time: 419 us -> 122 us (0.29)
  waiting for transfers between devices: 289 us -> 22.2 us
  between operations: 14.4 us -> 0.91 us
  blocking collectives: 39.4 us -> 31.5 us
    unnamed x2 -> x0, waiting for transfers between devices: 261 us -> none
    all_to_all x2 -> x1, blocking collectives: 39.4 us -> 31.5 us  [shards(): lax.all_to_all(packed.astype(jnp.bfloat16), ('row', 'col'), split_axis=0,...]
    all_to_all x2 -> x1, waiting for transfers between devices: 28 us -> 22.2 us  [shards(): lax.all_to_all(outgoing, ('row', 'col'), split_axis=0, concat_axis=0, til...]
    unnamed x23 -> x16, local copies, waits for them, and re-layouts: 7.35 us -> 2.38 us
    all_to_all x2 -> x1, starting transfers between devices: 22.3 us -> 22.2 us  [shards(): lax.all_to_all(outgoing, ('row', 'col'), split_axis=0, concat_axis=0, til...]
  transfers between devices with their start and end apart: 3 -> 1, of which waited for: 3 -> 1; matrix products, arithmetic and copies ran while one was open for 0% -> 0% of each run, Pallas kernels for 0% -> 0%
where the time goes in v1:
time: 122 us
  blocking collectives  31.5 us (26%)
  starting transfers between devices  22.2 us (18%)
  waiting for transfers between devices  22.2 us (18%)
  other arithmetic  16.5 us (14%)
  local copies, waits for them, and re-layouts  14.5 us (12%)
  matrix products  13.9 us (11%)
    all_to_all x1, blocking collectives, shards(): lax.all_to_all(packed.astype(jnp.bfloat16), ('row', 'col'), split_axis=0,...  31.5 us
    all_to_all x1, waiting for transfers between devices, shards(): lax.all_to_all(outgoing, ('row', 'col'), split_axis=0, concat_axis=0, til...  22.2 us
    all_to_all x1, starting transfers between devices, shards(): lax.all_to_all(outgoing, ('row', 'col'), split_axis=0, concat_axis=0, til...  22.2 us
    dot_general x2, matrix products, forward(): update = jnp.dot(hidden, w_out, preferred_element_type=jnp.float32)  5.26 us
    div x1, other arithmetic, shards(): probability = jax.nn.softmax(sym_logits, axis=-1)  3.87 us
    reduce_sum x4, other arithmetic, normalize(): variance = jnp.mean(centred * centred, axis=-1, keepdims=True)  3.36 us
    dynamic_update_slice x2, other arithmetic, shards(): residual, logits = lax.map(forward, blocks)  2.64 us
    reduce_sum x4, other arithmetic, normalize(): centred = values - jnp.mean(values, axis=-1, keepdims=True)  2.49 us
  transfers between devices with their start and end apart: 1, of which 1 were waited for; matrix products, arithmetic and copies ran while one was open for 0% of the time, Pallas kernels for 0%

profile of v1, /device:TPU:1, one launch (start us, length us, event | category | flops | bytes accessed | tf_op | source)
XLA Modules:
  0.0 122.0 jit_solution(983385449106738721)
XLA Ops:
  0.6 0.9 broadcast.79.clone
  1.5 10.6 %while.29 = (s32[]{:T(128)}, bf16[2,1024,128]{2,1,0:T(8,128)(2,1)}, f32[2,1024,64]{1,2,0:T(8,128)S(1)}, bf16[2,1024,128]{2,1,0:T(8,128)(2,1)}, bf16[128,512]{1,0...) while((s32[]{:T(128)}, bf16[2,1024,128]{2,1,0:T(8,128)(2,1)}, ...), condition=%wide.region_3.4_spmd, body=%wide.region_0.3_spmd.sunk | while | flops 287966208 | bytes 2479237 | solution.py:44
  1.5 1.1 convert_reduce_fusion.5
  2.6 1.3 %fusion.106 = f32[1024]{0:T(1024)S(1)} fusion(f32[1024]{0:T(1024)S(1)} %broadcast_multiply_fusion.8, bf16[2,1024,128]{2,1,0:T(8,128)(2,1)} %get-tuple-element.345, s32[]{:T(128)S(6)} %copy.63), kind=kLoop, calls=%fused_computation.12.clone.1 | loop fusion | flops 523264 | bytes 270340 | tf_op jit(solution)/shard_map/while/body/eval_jaxpr/reduce_sum | solution.py:11
  4.0 2.6 %bitcast_dynamic-update-slice_fusion.2 = (bf16[2,1024,128]{2,1,0:T(8,128)(2,1)}, bf16[1024,128]{1,0:T(8,128)(2,1)S(1)}) fusion(bf16[2,1024,128]{2,1,0:T(8,128)(2,1)} %get-tuple-element.335, s32[]{:T(128)S(6)} %copy.63, bf16[512,128]{1,0:T(8,128)(2,1)} %get-tuple-element.347, bf16[128,512]{1,0:T(8,128)(2,1)} %get-tuple-element.346, ...), kind=kOutput, calls=%fused_computation.14.clone.1 | convolution fusion | flops 270401536 | bytes 1319936 | tf_op jit(solution)/shard_map/while/body/eval_jaxpr/dot_general | solution.py:39
  6.8 1.1 convert_reduce_fusion.5
  7.9 1.3 %fusion.106 = f32[1024]{0:T(1024)S(1)} fusion(f32[1024]{0:T(1024)S(1)} %broadcast_multiply_fusion.8, bf16[2,1024,128]{2,1,0:T(8,128)(2,1)} %get-tuple-element.345, s32[]{:T(128)S(6)} %copy.63), kind=kLoop, calls=%fused_computation.12.clone.1 | loop fusion | flops 523264 | bytes 270340 | tf_op jit(solution)/shard_map/while/body/eval_jaxpr/reduce_sum | solution.py:11
  9.3 2.6 %bitcast_dynamic-update-slice_fusion.2 = (bf16[2,1024,128]{2,1,0:T(8,128)(2,1)}, bf16[1024,128]{1,0:T(8,128)(2,1)S(1)}) fusion(bf16[2,1024,128]{2,1,0:T(8,128)(2,1)} %get-tuple-element.335, s32[]{:T(128)S(6)} %copy.63, bf16[512,128]{1,0:T(8,128)(2,1)} %get-tuple-element.347, bf16[128,512]{1,0:T(8,128)(2,1)} %get-tuple-element.346, ...), kind=kOutput, calls=%fused_computation.14.clone.1 | convolution fusion | flops 270401536 | bytes 1319936 | tf_op jit(solution)/shard_map/while/body/eval_jaxpr/dot_general | solution.py:39
  13.0 1.9 %all_to_all.13 = f32[512,1,256]{2,1,0:T(1,128)} reshape(f32[16,32,2,2,64]{4,3,2,1,0:T(2,128)S(1)} %copy.42) | data formatting | bytes 1048576 | tf_op jit(solution)/shard_map/all_to_all | solution.py:47
  14.9 22.2 %all-to-all-start = ((f32[512,1,256]{2,1,0:T(1,128)}), f32[512,1,256]{2,1,0:T(1,128)S(1)}, u32[]{:S(2)}, u32[]{:S(2)}) async-start(f32[512,1,256]{2,1,0:T(1,128)} %all_to_all.13), calls=%async_computation | async-start | bytes 1048576 | tf_op jit(solution)/shard_map/all_to_all | solution.py:47
  37.3 22.2 %all-to-all-done = f32[512,1,256]{2,1,0:T(1,128)S(1)} async-done(((f32[512,1,256]{2,1,0:T(1,128)}), f32[512,1,256]{2,1,0:T(1,128)S(1)}, u32[]{:S(2)}, u32[]{:S(2)}) %all-to-all-start) | async-done | bytes 524320 | tf_op jit(solution)/shard_map/all_to_all | solution.py:47
  59.5 1.2 %reduce.3 = f32[512,256]{1,0:T(8,128)S(1)} reduce(f32[512,1,256]{2,1,0:T(1,128)S(1)} %all-to-all-done, f32[]{:T(128)} %constant.57), dimensions={1}, to_apply=%all_to_all.11.reduce_sub_computation | reduce | bytes 1048580 | tf_op jit(solution)/shard_map/all_to_all | solution.py:47
  62.2 3.9 %fusion.58 = bf16[2,1024,64]{2,1,0:T(8,128)(2,1)S(1)} fusion(s32[2,1024]{1,0:T(2,128)S(1)} %eq.15, f32[2,1024,64]{2,1,0:T(8,128)S(1)} %bitcast_add_fusion), kind=kOutput, calls=%fused_computation.68 | output fusion | flops 1183870 | bytes 794624 | tf_op jit(solution)/shard_map/div | solution.py:52
  66.0 0.9 broadcast.79
  66.9 13.5 %while.30 = (s32[]{:T(128)}, f32[128,512]{1,0:T(8,128)S(1)}, f32[512,128]{1,0:T(8,128)S(1)}, f32[128,64]{0,1:T(8,128)S(1)}, bf16[2,1024,128]{2,1,0:T(8,128)(2,1)...) while((s32[]{:T(128)}, f32[128,512]{1,0:T(8,128)S(1)}, ...), condition=%wide.region_11.12_spmd.clone, body=%wide.region_6.11_spmd.clone.sunk | while | flops 711607296 | bytes 18396844 | solution.py:83
  67.5 1.2 convolution_add_fusion.8
  72.3 1.3 %fusion.126 = bf16[2,1024,128]{2,1,0:T(8,128)(2,1)} fusion(bf16[2,1024,128]{2,1,0:T(8,128)(2,1)} %get-tuple-element.367, s32[]{:T(128)S(6)} %copy.74, f32[1024,128]{1,0:T(8,128)S(1)} %fusion.123, f32[1024,128]{1,0:T(8,128)S(1)} %copy.56, f32[1024]{0:T(1024)S(1)} %get-tuple-element.324, f32[1024]{0:T(1024)S(1)} %get-tuple-element.325, ...), kind=kLoop, calls=%fused_computation.43.clone.1 | loop fusion | flops 1179648 | bytes 1589252 | tf_op jit(solution)/shard_map/while/body/jit(dynamic_update_index_in_dim)/dynamic_update_slice | solution.py:44
  74.2 1.2 convolution_add_fusion.8
  79.0 1.3 %fusion.126 = bf16[2,1024,128]{2,1,0:T(8,128)(2,1)} fusion(bf16[2,1024,128]{2,1,0:T(8,128)(2,1)} %get-tuple-element.367, s32[]{:T(128)S(6)} %copy.74, f32[1024,128]{1,0:T(8,128)S(1)} %fusion.123, f32[1024,128]{1,0:T(8,128)S(1)} %copy.56, f32[1024]{0:T(1024)S(1)} %get-tuple-element.324, f32[1024]{0:T(1024)S(1)} %get-tuple-element.325, ...), kind=kLoop, calls=%fused_computation.43.clone.1 | loop fusion | flops 1179648 | bytes 1589252 | tf_op jit(solution)/shard_map/while/body/jit(dynamic_update_index_in_dim)/dynamic_update_slice | solution.py:44
  81.6 1.1 copy.49
  83.2 0.8 reshape.154
  85.6 0.8 reduce.4
  86.8 31.5 %all_to_all.16 = bf16[512,2,136]{2,1,0:T(2,128)(2,1)S(1)} all-to-all(bf16[512,2,136]{2,1,0:T(2,128)(2,1)S(1)} %reshape.158), channel_id=1, replica_groups=mesh['row'=16,'col'=32] {'row','col'}, dimensions={0} | all-to-all | bytes 557056 | tf_op jit(solution)/shard_map/all_to_all | solution.py:92
  118.9 0.9 convert_reduce_fusion.2
  (81 shorter events, 17.4 us)
Async XLA Ops:
  1.5 5.1 %copy-start.3 = (bf16[128,64]{0,1:T(8,128)(2,1)S(1)}, bf16[128,64]{0,1:T(8,128)(2,1)}, u32[]{:S(2)}) copy-start(bf16[128,64]{0,1:T(8,128)(2,1)} %get-tuple-element.348) | copy-start | bytes 49156 | tf_op jit(solution)/shard_map/while
  6.8 5.1 %copy-start.3 = (bf16[128,64]{0,1:T(8,128)(2,1)S(1)}, bf16[128,64]{0,1:T(8,128)(2,1)}, u32[]{:S(2)}) copy-start(bf16[128,64]{0,1:T(8,128)(2,1)} %get-tuple-element.348) | copy-start | bytes 49156 | tf_op jit(solution)/shard_map/while
  12.4 24.7 %copy-start.5 = (s32[64,32]{0,1:T(8,128)S(1)}, s32[64,32]{0,1:T(8,128)}, u32[]{:S(2)}) copy-start(s32[64,32]{0,1:T(8,128)} %param.10) | copy-start | bytes 24580
  14.9 44.6 %all-to-all-start = ((f32[512,1,256]{2,1,0:T(1,128)}), f32[512,1,256]{2,1,0:T(1,128)S(1)}, u32[]{:S(2)}, u32[]{:S(2)}) async-start(f32[512,1,256]{2,1,0:T(1,128)} %all_to_all.13), calls=%async_computation | async-start | bytes 1048576 | tf_op jit(solution)/shard_map/all_to_all | solution.py:47
  62.1 4.8 %copy-start = (bf16[2,1024,128]{2,1,0:T(8,128)(2,1)S(1)}, bf16[2,1024,128]{2,1,0:T(8,128)(2,1)}, u32[]{:S(2)}) copy-start(bf16[2,1024,128]{2,1,0:T(8,128)(2,1)} %get-tuple-element.389) | copy-start | bytes 1572868
  62.1 4.8 %copy-start.1 = (bf16[128,512]{1,0:T(8,128)(2,1)S(1)}, bf16[128,512]{1,0:T(8,128)(2,1)}, u32[]{:S(2)}) copy-start(bf16[128,512]{1,0:T(8,128)(2,1)} %get-tuple-element.390) | copy-start | bytes 393220
  62.1 4.8 %copy-start.2 = (bf16[512,128]{1,0:T(8,128)(2,1)S(1)}, bf16[512,128]{1,0:T(8,128)(2,1)}, u32[]{:S(2)}) copy-start(bf16[512,128]{1,0:T(8,128)(2,1)} %get-tuple-element.391) | copy-start | bytes 393220
  62.1 4.8 %copy-start.4 = (bf16[128,64]{0,1:T(8,128)(2,1)S(1)}, bf16[128,64]{0,1:T(8,128)(2,1)}, u32[]{:S(2)}) copy-start(bf16[128,64]{0,1:T(8,128)(2,1)} %get-tuple-element.393) | copy-start | bytes 49156

commit v2 on v1

v2 whole, which is shorter than its diff:
```python
import functools

import jax
import jax.numpy as jnp
from jax import lax
from jax.experimental import pallas as pl
from jax.experimental.pallas import tpu as pltpu
from jax.sharding import PartitionSpec as P

epsilon = 1e-05
f32 = jnp.float32
bf16 = jnp.bfloat16

code_gain = 16.0
code_steps = 1850.0

CYCLES = 2
STEPS = 4


def dot(first, second):
    return jnp.dot(first, second, preferred_element_type=f32)


def encode(values):
    size = jnp.log(1.0 + jnp.abs(values) * code_gain) * code_steps + 0.5
    return jnp.where(values < 0.0, -size, size).astype(jnp.int32)


def decode(codes):
    codes = codes.astype(f32)
    size = (jnp.exp(jnp.abs(codes) * (1.0 / code_steps)) - 1.0) * (1.0 / code_gain)
    return jnp.where(codes < 0.0, -size, size)


def normalize(values):
    centred = values - jnp.mean(values, axis=-1, keepdims=True)
    variance = jnp.mean(centred * centred, axis=-1, keepdims=True)
    inv_std = lax.rsqrt(variance + epsilon)
    return (centred * inv_std, inv_std)


def send_kernel(pair_ref, w_in_ref, w_out_ref, w_wide_ref, send_ref, rows_ref):
    n_row = send_ref.shape[0]
    span = send_ref.shape[1]
    channels = pair_ref.shape[-1]
    values = pair_ref[...].reshape(-1, channels).astype(f32)
    half = values.shape[0] // CYCLES
    x_hat, _ = normalize(values)
    hidden = jnp.maximum(dot(x_hat.astype(bf16), w_in_ref[...]), 0.0).astype(bf16)
    residual = (values + dot(hidden, w_out_ref[...])).astype(bf16)
    wide = jnp.concatenate([residual[:half], residual[half:]], axis=1)
    rows_ref[...] = encode(dot(wide, w_wide_ref[...]))
    for r in range(n_row):
        send_ref[r] = rows_ref[pl.ds(r, span, stride=n_row), :].astype(jnp.int16)


def prepare_kernel(
    pair_ref,
    bins_ref,
    w_in_ref,
    w_out_ref,
    w_wide_ref,
    hidden_ref,
    hidden_t_ref,
    normed_t_ref,
    residual_t_ref,
    x_hat_ref,
    inv_ref,
    logits_ref,
    bins_wide_ref,
    values_ref,
):
    channels = pair_ref.shape[-1]
    n_row = pair_ref.shape[2] // CYCLES
    count = pair_ref.shape[1]
    for a in range(CYCLES):
        for b in range(CYCLES):
            values_ref[a, :, b] = pair_ref[b, :, a * n_row : (a + 1) * n_row, :].astype(f32)
    values = values_ref[...].reshape(-1, channels)
    half = values.shape[0] // CYCLES
    x_hat, inv_std = normalize(values)
    normed = x_hat.astype(bf16)
    hidden = jnp.maximum(dot(normed, w_in_ref[...]), 0.0).astype(bf16)
    residual = (values + dot(hidden, w_out_ref[...])).astype(bf16)
    hidden_ref[...] = hidden
    hidden_t_ref[...] = hidden.T
    normed_t_ref[...] = normed.T
    residual_t_ref[...] = residual.T
    x_hat_ref[...] = x_hat
    inv_ref[...] = jnp.broadcast_to(inv_std, x_hat.shape)
    logits_ref[...] = dot(
        jnp.concatenate([residual[:half], residual[half:]], axis=1), w_wide_ref[...]
    )
    columns = bins_ref.shape[-1]
    row_of = lax.broadcasted_iota(jnp.int32, (1, n_row, columns), 1)
    column_of = lax.broadcasted_iota(jnp.int32, (1, n_row, columns), 2)
    own = column_of % n_row == row_of
    lane = lax.broadcasted_iota(jnp.int32, (columns, channels), 1)
    source = lax.broadcasted_iota(jnp.int32, (columns, channels), 0)
    spread = (lane // (channels // CYCLES) == source // n_row).astype(f32).astype(bf16)
    for b in range(CYCLES):
        bins = bins_ref[b].astype(f32)
        picked = jnp.where(own, jnp.broadcast_to(bins[:, None, :], (count, n_row, columns)), 0.0)
        wide = dot(picked.reshape(count * n_row, columns).astype(bf16), spread)
        bins_wide_ref[:, b] = wide.reshape(count, n_row, channels)


def backward_kernel(
    recv_ref,
    hidden_ref,
    hidden_t_ref,
    normed_t_ref,
    residual_t_ref,
    x_hat_ref,
    inv_ref,
    logits_ref,
    bins_wide_ref,
    w_in_t_ref,
    w_out_t_ref,
    w_head_wide_ref,
    grad_ref,
    part_ref,
    rows_ref,
    in_ref,
    out_ref,
    head_ref,
):
    step = pl.program_id(0)
    n_row = recv_ref.shape[0]
    span = recv_ref.shape[1]
    count = span // CYCLES
    channels = grad_ref.shape[-1]
    bins_count = channels // CYCLES
    half = span * n_row

    for r in range(n_row):
        rows_ref[pl.ds(r, span, stride=n_row), :] = decode(recv_ref[r])
    sym = logits_ref[...] + rows_ref[...]
    lane = lax.broadcasted_iota(jnp.int32, (1, channels), 1)
    left = lane < bins_count
    low = jnp.max(jnp.where(left, sym, -jnp.inf), axis=-1, keepdims=True)
    high = jnp.max(jnp.where(left, -jnp.inf, sym), axis=-1, keepdims=True)
    grown = jnp.exp(sym - jnp.where(left, low, high))
    low = jnp.sum(jnp.where(left, grown, 0.0), axis=-1, keepdims=True)
    high = jnp.sum(jnp.where(left, 0.0, grown), axis=-1, keepdims=True)
    probability = grown / jnp.where(left, low, high)
    own_bin = (lane % bins_count).astype(f32)
    onehot = jnp.where(bins_wide_ref[...].reshape(half, channels) == own_bin, 1.0, 0.0)
    d_sym = probability - onehot
    d_logit = (d_sym + d_sym).astype(bf16)

    wide = dot(d_logit, w_head_wide_ref[...])
    d_resid = jnp.concatenate([wide[:, :channels], wide[:, channels:]], axis=0)
    d_update = d_resid.astype(bf16)
    back = dot(d_update, w_out_t_ref[...]).astype(bf16)
    hidden = hidden_ref[...]
    d_hidden = jnp.where(hidden > 0, back, jnp.zeros_like(back))
    d_normed = dot(d_hidden, w_in_t_ref[...])
    x_hat = x_hat_ref[...]
    first_mean = jnp.mean(d_normed, axis=-1, keepdims=True)
    second_mean = jnp.mean(d_normed * x_hat, axis=-1, keepdims=True)
    d_pair = d_resid + inv_ref[...] * (d_normed - first_mean - x_hat * second_mean)
    d_pair = d_pair.astype(bf16).reshape(CYCLES, count, CYCLES, n_row, channels)
    for a in range(CYCLES):
        for b in range(CYCLES):
            grad_ref[b, :, a * n_row : (a + 1) * n_row, :] = d_pair[a, :, b]

    g_in = dot(normed_t_ref[...], d_hidden)
    g_out = dot(hidden_t_ref[...], d_update)
    g_head = jnp.where(
        left,
        dot(residual_t_ref[:, :half], d_logit),
        dot(residual_t_ref[:, half:], d_logit),
    )

    @pl.when(step == 0)
    def _():
        in_ref[...] = g_in
        out_ref[...] = g_out
        head_ref[...] = g_head

    @pl.when(step > 0)
    def _():
        in_ref[...] += g_in
        out_ref[...] += g_out
        head_ref[...] += g_head

    @pl.when(step == STEPS - 1)
    def _():
        rows = channels // n_row
        tiles = in_ref.shape[1] // channels
        long = tiles * rows
        for r in range(n_row):
            mine = in_ref[r * rows : (r + 1) * rows, :]
            part_ref[r, 0:long, :] = jnp.concatenate(
                [mine[:, t * channels : (t + 1) * channels] for t in range(tiles)], axis=0
            ).astype(bf16)
            part_ref[r, long : 2 * long, :] = out_ref[r * long : (r + 1) * long, :].astype(bf16)
            mine = head_ref[r * rows : (r + 1) * rows, :]
            part_ref[r, 2 * long : 2 * long + 2 * rows, :] = jnp.concatenate(
                [mine, jnp.zeros_like(mine)], axis=0
            ).astype(bf16)


def lanes_of(shape, axis):
    return lax.broadcasted_iota(jnp.int32, shape, axis)


def fold_matrix(width, kind):
    shape = (128, 128)
    return (lanes_of(shape, 0) % width == lanes_of(shape, 1) % width).astype(f32).astype(kind)


def middle_kernel(recv_ref, send_ref):
    n_col = send_ref.shape[0]
    total = recv_ref[0].astype(f32)
    for r in range(1, recv_ref.shape[0]):
        total = total + recv_ref[r].astype(f32)
    rows, tiles = 8, 4
    mine = total[: rows * tiles]
    group = lanes_of((1, rows, 128), 2) // 16 == lanes_of((1, rows, 128), 1)
    spread = jnp.where(group, jnp.broadcast_to(mine[:, None, :], (rows * tiles, rows, 128)), 0.0)
    folded = dot(spread.reshape(-1, 128).astype(bf16), fold_matrix(16, bf16))
    folded = folded.reshape(tiles, rows, rows, 128)
    slot = lanes_of((1, rows, 1, 128), 3) // 16 == lanes_of((1, rows, 1, 128), 1)
    part_in = jnp.sum(jnp.where(slot, folded, 0.0), axis=1).reshape(n_col, 128)
    mine = total[32:64]
    group = lanes_of((1, n_col, 128), 2) // 4 == lanes_of((1, n_col, 128), 1)
    spread = jnp.where(group, jnp.broadcast_to(mine[:, None, :], (32, n_col, 128)), 0.0)
    folded = dot(spread.reshape(-1, 128).astype(bf16), fold_matrix(4, bf16))
    folded = folded.reshape(32, n_col, 128)
    slot = lanes_of((32, 1, 128), 2) // 4 == lanes_of((32, 1, 128), 0)
    part_out = jnp.sum(jnp.where(slot, folded, 0.0), axis=0)
    mine = total[64:72]
    group = lanes_of((1, n_col, 128), 2) % 64 // 2 == lanes_of((1, n_col, 128), 1)
    spread = jnp.where(group, jnp.broadcast_to(mine[:, None, :], (8, n_col, 128)), 0.0)
    folded = dot(spread.reshape(-1, 128).astype(bf16), fold_matrix(2, bf16))
    folded = folded.reshape(8, n_col, 128)
    slot = lanes_of((8, 1, 128), 2) // 2 == lanes_of((8, 1, 128), 0)
    part_head = jnp.sum(jnp.where(slot, folded, 0.0), axis=0)
    send_ref[:, 0:128] = part_in
    send_ref[:, 128:256] = part_out
    send_ref[:, 256:384] = part_head


def final_kernel(scale, recv_ref, in_ref, out_ref, head_ref):
    total = jnp.sum(recv_ref[...], axis=0, keepdims=True) * scale

    def unfold(row, out):
        count, width = out.shape
        shape = (count, 128)
        lane = lanes_of(shape, 1)
        picked = jnp.where(lane // width == lanes_of(shape, 0), jnp.broadcast_to(row, shape), 0.0)
        shape = (128, width)
        fold = (lanes_of(shape, 0) % width == lanes_of(shape, 1)).astype(f32)
        out[...] = jnp.dot(
            picked, fold, precision=lax.Precision.HIGHEST, preferred_element_type=f32
        )

    unfold(total[:, 0:128], in_ref)
    unfold(total[:, 128:256], out_ref)
    unfold(total[:, 256:384], head_ref)


def whole(array):
    return pl.BlockSpec(array.shape, lambda g: (0,) * array.ndim)


def params():
    return pltpu.CompilerParams(vmem_limit_bytes=40 * 1024 * 1024)


def shards(pair_rep, true_bins, w_in, w_out, w_head):
    row_count, col_count, channels = pair_rep.shape
    n_row = lax.axis_size("row")
    n_col = lax.axis_size("col")
    hidden_count = w_in.shape[1]
    bins_count = w_head.shape[1]
    pairs = row_count * col_count
    cycled = pair_rep.reshape(CYCLES, n_col, col_count, channels)
    bins = true_bins.reshape(CYCLES, n_col, col_count)
    blank = jnp.zeros_like(w_head)
    w_wide = jnp.concatenate(
        [jnp.concatenate([w_head, blank], axis=1), jnp.concatenate([blank, w_head], axis=1)],
        axis=0,
    )
    count = n_col // STEPS
    span = CYCLES * count
    block = pairs // STEPS
    half = block // CYCLES
    pair_spec = pl.BlockSpec((CYCLES, count, col_count, channels), lambda g: (0, g, 0, 0))
    send_spec = pl.BlockSpec((n_row, span, channels), lambda g: (0, g, 0))

    send = pl.pallas_call(
        send_kernel,
        grid=(STEPS,),
        in_specs=[pair_spec, whole(w_in), whole(w_out), whole(w_wide)],
        out_specs=send_spec,
        out_shape=jax.ShapeDtypeStruct((n_row, CYCLES * n_col, channels), jnp.int16),
        scratch_shapes=[pltpu.VMEM((half, channels), jnp.int32)],
        compiler_params=params(),
        name="forward",
    )(cycled, w_in, w_out, w_wide)

    recv = lax.all_to_all(
        send.reshape(n_row * n_col, CYCLES, channels),
        ("row", "col"),
        split_axis=0,
        concat_axis=0,
        tiled=True,
    ).reshape(n_row, CYCLES * n_col, channels)

    def rows_spec(width):
        return pl.BlockSpec((block, width), lambda g: (g, 0))

    def columns_spec(height):
        return pl.BlockSpec((height, block), lambda g: (0, g))

    logits_spec = pl.BlockSpec((half, channels), lambda g: (g, 0))
    bins_spec = pl.BlockSpec((count, CYCLES, n_row, channels), lambda g: (g, 0, 0, 0))
    kept_specs = [
        rows_spec(hidden_count),
        columns_spec(hidden_count),
        columns_spec(channels),
        columns_spec(channels),
        rows_spec(channels),
        rows_spec(channels),
        logits_spec,
        bins_spec,
    ]
    kept = pl.pallas_call(
        prepare_kernel,
        grid=(STEPS,),
        in_specs=[
            pair_spec,
            pl.BlockSpec((CYCLES, count, col_count), lambda g: (0, g, 0)),
            whole(w_in),
            whole(w_out),
            whole(w_wide),
        ],
        out_specs=kept_specs,
        out_shape=[
            jax.ShapeDtypeStruct((pairs, hidden_count), bf16),
            jax.ShapeDtypeStruct((hidden_count, pairs), bf16),
            jax.ShapeDtypeStruct((channels, pairs), bf16),
            jax.ShapeDtypeStruct((channels, pairs), bf16),
            jax.ShapeDtypeStruct((pairs, channels), f32),
            jax.ShapeDtypeStruct((pairs, channels), f32),
            jax.ShapeDtypeStruct((pairs // CYCLES, channels), f32),
            jax.ShapeDtypeStruct((n_col, CYCLES, n_row, channels), f32),
        ],
        scratch_shapes=[pltpu.VMEM((CYCLES, count, CYCLES, n_row, channels), f32)],
        compiler_params=params(),
        cost_estimate=pl.CostEstimate(
            flops=2 * pairs * 2 * channels * hidden_count, bytes_accessed=8 * 2**20, transcendentals=0
        ),
        name="prepare",
    )(cycled, bins, w_in, w_out, w_wide)

    w_in_t = w_in.T
    w_out_t = w_out.T
    w_head_wide = w_wide.T
    part_rows = 2 * (hidden_count // n_row) + 16
    d_pair, part = pl.pallas_call(
        backward_kernel,
        grid=(STEPS,),
        in_specs=[send_spec] + kept_specs + [whole(w_in_t), whole(w_out_t), whole(w_head_wide)],
        out_specs=[pair_spec, pl.BlockSpec((n_row, part_rows, channels), lambda g: (0, 0, 0))],
        out_shape=[
            jax.ShapeDtypeStruct(cycled.shape, bf16),
            jax.ShapeDtypeStruct((n_row, part_rows, channels), bf16),
        ],
        scratch_shapes=[
            pltpu.VMEM((half, channels), f32),
            pltpu.VMEM((channels, hidden_count), f32),
            pltpu.VMEM((hidden_count, channels), f32),
            pltpu.VMEM((channels, channels), f32),
        ],
        compiler_params=params(),
        name="backward",
    )(recv, *kept, w_in_t, w_out_t, w_head_wide)

    part = lax.all_to_all(part, "row", split_axis=0, concat_axis=0, tiled=True)
    share = pl.pallas_call(
        middle_kernel,
        out_shape=jax.ShapeDtypeStruct((n_col, 3 * channels), f32),
        name="sum_rows",
    )(part)
    share = lax.all_to_all(share, "col", split_axis=0, concat_axis=0, tiled=True)
    grad_in, grad_out, grad_head = pl.pallas_call(
        functools.partial(final_kernel, 1.0 / (row_count * n_row)),
        out_shape=[
            jax.ShapeDtypeStruct((channels // n_row, hidden_count // n_col), f32),
            jax.ShapeDtypeStruct((hidden_count // n_row, channels // n_col), f32),
            jax.ShapeDtypeStruct((channels // n_row, bins_count // n_col), f32),
        ],
        name="sum_columns",
    )(share)
    return (d_pair.reshape(row_count, col_count, channels), grad_in, grad_out, grad_head)


def solution(mesh):
    placed = (P("row", "col", None), P("row", "col"), P(), P(), P())
    return jax.shard_map(
        shards,
        mesh=mesh,
        in_specs=placed,
        out_specs=(P("row", "col", None), P("row", "col"), P("row", "col"), P("row", "col")),
        check_vma=False,
    )
```

time: 122 us -> 112 us (0.918)
  waiting for transfers between devices: 22.2 us -> 1.07 us
  Pallas kernels: 0 us -> 17.4 us
  other arithmetic: 16.5 us -> 1.43 us
  matrix products: 13.9 us -> 0 us
  local copies, waits for them, and re-layouts: 14.5 us -> 28.3 us
  blocking collectives: 31.5 us -> 40 us
    unnamed x16 -> x56, local copies, waits for them, and re-layouts: 2.38 us -> 27.4 us
    all_to_all x1, waiting for transfers between devices: 22.2 us -> 1.07 us  [shards(): lax.all_to_all(send.reshape(n_row * n_col, CYCLES, channels), ('row', 'co...]
    pallas_call x0 -> x5, Pallas kernels: none -> 17.4 us  [the longest x1 5.7 us: shards(): pl.pallas_call(backward_kernel, grid=(STEPS,), in_specs=[send_spec] + kep...]
    dot_general x18 -> x0, matrix products: 13.9 us -> none  [the longest x2 5.26 us: forward(): update = jnp.dot(hidden, w_out, preferred_element_type=jnp.float32)]
    all_to_all x1 -> x2, blocking collectives: 31.5 us -> 40 us  [the longest x1 21.2 us: shards(): part = lax.all_to_all(part, 'row', split_axis=0, concat_axis=0, tiled=True)]
    reduce_sum x11 -> x0, other arithmetic: 7.76 us -> none  [the longest x4 3.36 us: normalize(): variance = jnp.mean(centred * centred, axis=-1, keepdims=True)]
    div x8 -> x0, other arithmetic: 3.9 us -> none  [the longest x1 3.87 us: shards(): probability = jax.nn.softmax(sym_logits, axis=-1)]
    transpose x5 -> x0, local copies, waits for them, and re-layouts: 3.14 us -> none  [the longest x3 1.98 us: as_tiles(): jnp.transpose(split, (0, 2, 1, 3))]
  transfers between devices with their start and end apart: 1 -> 1, of which waited for: 1 -> 1; matrix products, arithmetic and copies ran while one was open for 0% -> 2% of each run, Pallas kernels for 0% -> 3%
where the time goes in v2:
time: 112 us; the launch traced here: 111 us
  blocking collectives  40 us (36%)
  local copies, waits for them, and re-layouts  28.3 us (25%)
  starting transfers between devices  22.2 us (20%)
  Pallas kernels  17.4 us (16%)
  other arithmetic  1.43 us (1%)
    unnamed x56, local copies, waits for them, and re-layouts  27.4 us
    all_to_all x1, starting transfers between devices, shards(): lax.all_to_all(send.reshape(n_row * n_col, CYCLES, channels), ('row', 'co...  22.2 us
    all_to_all x1, blocking collectives, shards(): part = lax.all_to_all(part, 'row', split_axis=0, concat_axis=0, tiled=True)  21.2 us
    all_to_all x1, blocking collectives, shards(): lax.all_to_all(share, 'col', split_axis=0, concat_axis=0, tiled=True)  18.9 us
    pallas_call x1, Pallas kernels, shards(): pl.pallas_call(backward_kernel, grid=(STEPS,), in_specs=[send_spec] + kep...  5.7 us
    pallas_call x1, Pallas kernels, shards(): pl.pallas_call(send_kernel, grid=(STEPS,), in_specs=[pair_spec, whole(w_i...  4.44 us
    pallas_call x1, Pallas kernels, shards(): pl.pallas_call(prepare_kernel, grid=(STEPS,), in_specs=[pair_spec, pl.Blo...  3.67 us
  transfers between devices with their start and end apart: 1, of which 1 were waited for; matrix products, arithmetic and copies ran while one was open for 2% of the time, Pallas kernels for 3%

profile of v2, /device:TPU:1, one launch (start us, length us, event | category | flops | bytes accessed | tf_op | source)
XLA Modules:
  0.0 111.1 jit_solution(5194883455197966835)
XLA Ops:
  0.7 1.4 %fusion.3 = (bf16[128,256]{1,0:T(8,128)(2,1)}, bf16[256,128]{0,1:T(8,128)(2,1)S(1)}) fusion(bf16[128,64]{0,1:T(8,128)(2,1)} %param.9), kind=kLoop, calls=%fused_computation.6 | loop fusion | flops 262144 | bytes 147456 | tf_op jit(solution)/shard_map/transpose | solution.py:363
  2.2 0.9 copy-done.13
  4.1 1.0 copy-done.18
  5.1 4.4 %forward.1 = s16[16,64,128]{2,1,0:T(8,128)(2,1)} custom-call(bf16[2,32,32,128]{3,2,1,0:T(8,128)(2,1)S(1)} %bitcast.16, bf16[128,512]{1,0:T(8,128)(2,1)S(1)} %copy-done.13, bf16[512,128]{1,0:T(8,128)(2,1)S(1)} %copy-done.15, bf16[256,128]{1,0:T(8,128)(2,1)S(1)} %copy.16.w_wide_ref), custom_call_target="tpu_custom_call" | custom-call | tf_op jit(solution)/shard_map/forward/pallas_call | solution.py:295
  9.5 22.2 %all-to-all-start = ((s16[512,2,128]{2,1,0:T(2,128)(2,1)}), s16[512,2,128]{2,1,0:T(2,128)(2,1)S(1)}, u32[]{:S(2)}, u32[]{:S(2)}) async-start(s16[512,2,128]{2,1,0:T(2,128)(2,1)} %bitcast.1), calls=%async_computation | async-start | bytes 524288 | tf_op jit(solution)/shard_map/all_to_all | solution.py:306
  31.7 1.0 copy.19
  36.0 1.0 copy-done.19
  38.7 3.7 %prepare.1 = (bf16[2048,512]{1,0:T(8,128)(2,1)S(1)}, bf16[512,2048]{1,0:T(8,128)(2,1)S(1)}, bf16[128,2048]{1,0:T(8,128)(2,1)S(1)}, bf16[128,2048]{1,0:T(8,128)(2...) custom-call(bf16[2,32,32,128]{3,2,1,0:T(8,128)(2,1)S(1)} %bitcast.17, ...), custom_call_target="tpu_custom_call" | custom-call | flops 536870912 | bytes 8388608 | tf_op jit(solution)/shard_map/prepare/pallas_call | solution.py:332
  42.4 1.3 %copy-done = bf16[512,2048]{1,0:T(8,128)(2,1)} copy-done((bf16[512,2048]{1,0:T(8,128)(2,1)}, bf16[512,2048]{1,0:T(8,128)(2,1)S(1)}, u32[]{:S(2)}) %copy-start) | copy-done | bytes 2097176
  43.7 1.0 copy-done.2
  47.9 1.1 all-to-all-done
  49.0 1.6 %copy-done.1 = bf16[512,2048]{1,0:T(8,128)(2,1)S(1)} copy-done((bf16[512,2048]{1,0:T(8,128)(2,1)S(1)}, bf16[512,2048]{1,0:T(8,128)(2,1)}, u32[]{:S(2)}) %copy-start.1) | copy-done | bytes 2097176
  50.6 1.2 %copy-done.3 = f32[2048,128]{1,0:T(8,128)S(1)} copy-done((f32[2048,128]{1,0:T(8,128)S(1)}, f32[2048,128]{1,0:T(8,128)}, u32[]{:S(2)}) %copy-start.3) | copy-done | bytes 1048600
  52.7 1.0 copy-done.6
  53.7 1.0 copy-done.8
  54.8 1.0 copy-done.10
  55.8 1.0 copy-done.12
  57.7 5.7 %backward.1 = (bf16[2,32,32,128]{3,2,1,0:T(8,128)(2,1)}, bf16[16,80,128]{2,1,0:T(8,128)(2,1)S(1)}) custom-call(s16[16,64,128]{2,1,0:T(8,128)(2,1)S(1)} %bitcast.13, bf16[2048,512]{1,0:T(8,128)(2,1)S(1)} %get-tuple-element.17.hidden_ref, bf16[512,2048]{1,0:T(8,128)(2,1)S(1)} %copy-done.1, bf16[128,2048]{1,0:T(8,128)(2,1)S(1)} %copy-done.6, ...), custom_call_target="tpu_custom_call" | custom-call | tf_op jit(solution)/shard_map/backward/pallas_call | solution.py:365
  63.4 21.2 %all_to_all.21.recv_ref = bf16[16,80,128]{2,1,0:T(8,128)(2,1)} all-to-all(bf16[16,80,128]{2,1,0:T(8,128)(2,1)S(1)} %get-tuple-element.26), channel_id=1, replica_groups=mesh['row'=16,'col'=32] {'row'}, dimensions={0} | all-to-all | bytes 655360 | tf_op jit(solution)/shard_map/all_to_all | solution.py:384
  84.6 1.9 %sum_rows.1 = f32[32,384]{1,0:T(8,128)} custom-call(bf16[16,80,128]{2,1,0:T(8,128)(2,1)} %all_to_all.21.recv_ref), custom_call_target="tpu_custom_call" | custom-call | tf_op jit(solution)/shard_map/sum_rows/pallas_call | solution.py:385
  87.3 18.9 %all_to_all.22 = f32[32,1,384]{2,1,0:T(1,128)S(1)} all-to-all(f32[32,1,384]{2,1,0:T(1,128)S(1)} %copy.21), channel_id=1, replica_groups=mesh['row'=16,'col'=32] {'col'}, dimensions={0} | all-to-all | bytes 98304 | tf_op jit(solution)/shard_map/all_to_all | solution.py:390
  106.8 1.7 %sum_columns.1 = (f32[8,16]{1,0:T(8,128)}, f32[32,4]{1,0:T(8,128)}, f32[8,2]{1,0:T(8,128)}) custom-call(f32[32,384]{1,0:T(8,128)} %bitcast.19), custom_call_target="tpu_custom_call" | custom-call | tf_op jit(solution)/shard_map/sum_columns/pallas_call | solution.py:391
  108.5 1.3 %copy.23 = f32[8,2]{0,1:T(2,128)} copy(f32[8,2]{1,0:T(8,128)} %get-tuple-element.37) | data formatting | bytes 128
  109.8 1.4 %copy.22 = f32[32,4]{0,1:T(4,128)} copy(f32[32,4]{1,0:T(8,128)} %get-tuple-element.36) | data formatting | bytes 1024
  (44 shorter events, 12.4 us)
Async XLA Ops:
  0.6 32.1 %copy-start.16 = (bf16[512,128]{1,0:T(8,128)(2,1)S(1)}, bf16[512,128]{1,0:T(8,128)(2,1)}, u32[]{:S(2)}) copy-start(bf16[512,128]{1,0:T(8,128)(2,1)} %w_out_ref.3) | copy-start | bytes 393220
  0.6 32.9 %copy-start.24 = (s32[64,32]{0,1:T(8,128)S(1)}, s32[64,32]{0,1:T(8,128)}, u32[]{:S(2)}) copy-start(s32[64,32]{0,1:T(8,128)} %param.6) | copy-start | bytes 24580
  2.2 7.3 %copy-start.21 = (bf16[256,128]{1,0:T(8,128)(2,1)}, bf16[256,128]{1,0:T(8,128)(2,1)S(1)}, u32[]{:S(2)}) copy-start(bf16[256,128]{1,0:T(8,128)(2,1)S(1)} %copy.16.w_wide_ref) | copy-start | bytes 196612
  2.2 0.9 copy-start.13
  3.1 0.9 copy-start.15
  4.1 1.0 copy-start.18
  9.5 39.5 %all-to-all-start = ((s16[512,2,128]{2,1,0:T(2,128)(2,1)}), s16[512,2,128]{2,1,0:T(2,128)(2,1)S(1)}, u32[]{:S(2)}, u32[]{:S(2)}) async-start(s16[512,2,128]{2,1,0:T(2,128)(2,1)} %bitcast.1), calls=%async_computation | async-start | bytes 524288 | tf_op jit(solution)/shard_map/all_to_all | solution.py:306
  34.2 0.9 copy-start.14
  35.1 0.9 copy-start.17
  36.0 1.0 copy-start.19
  37.1 0.8 copy-start.22
  42.3 1.4 %copy-start = (bf16[512,2048]{1,0:T(8,128)(2,1)}, bf16[512,2048]{1,0:T(8,128)(2,1)S(1)}, u32[]{:S(2)}) copy-start(bf16[512,2048]{1,0:T(8,128)(2,1)S(1)} %get-tuple-element.18.hidden_t_ref) | copy-start | bytes 6291460
  43.7 1.0 copy-start.2
  45.5 0.8 copy-start.7
  46.3 0.8 copy-start.9
  47.1 0.8 copy-start.11
  49.0 1.6 %copy-start.1 = (bf16[512,2048]{1,0:T(8,128)(2,1)S(1)}, bf16[512,2048]{1,0:T(8,128)(2,1)}, u32[]{:S(2)}) copy-start(bf16[512,2048]{1,0:T(8,128)(2,1)} %copy-done) | copy-start | bytes 6291460
  50.6 1.2 %copy-start.3 = (f32[2048,128]{1,0:T(8,128)S(1)}, f32[2048,128]{1,0:T(8,128)}, u32[]{:S(2)}) copy-start(f32[2048,128]{1,0:T(8,128)} %copy-done.2) | copy-start | bytes 3145732
  51.8 0.9 copy-start.4
  52.7 1.0 copy-start.6
  53.7 1.0 copy-start.8
  54.8 1.0 copy-start.10
  55.8 1.0 copy-start.12
  56.9 0.8 copy-start.20
  (2 other events, 1.6 us)

commit v3 on v2

v3 whole, which is shorter than its diff:
```python
import functools

import jax
import jax.numpy as jnp
from jax import lax
from jax.experimental import pallas as pl
from jax.experimental.pallas import tpu as pltpu
from jax.sharding import PartitionSpec as P

epsilon = 1e-05
f32 = jnp.float32
bf16 = jnp.bfloat16

code_gain = 16.0
code_steps = 1850.0

CYCLES = 2
STEPS = 4


def dot(first, second):
    return jnp.dot(first, second, preferred_element_type=f32)


def dot_t(first, second):
    return lax.dot_general(first, second, (((1,), (1,)), ((), ())), preferred_element_type=f32)


def widen(w_head_t):
    blank = jnp.zeros_like(w_head_t)
    return jnp.concatenate(
        [
            jnp.concatenate([w_head_t, blank], axis=1),
            jnp.concatenate([blank, w_head_t], axis=1),
        ],
        axis=0,
    )


def encode(values):
    size = jnp.log(1.0 + jnp.abs(values) * code_gain) * code_steps + 0.5
    return jnp.where(values < 0.0, -size, size).astype(jnp.int32)


def decode(codes):
    codes = codes.astype(f32)
    size = (jnp.exp(jnp.abs(codes) * (1.0 / code_steps)) - 1.0) * (1.0 / code_gain)
    return jnp.where(codes < 0.0, -size, size)


def normalize(values):
    centred = values - jnp.mean(values, axis=-1, keepdims=True)
    variance = jnp.mean(centred * centred, axis=-1, keepdims=True)
    inv_std = lax.rsqrt(variance + epsilon)
    return (centred * inv_std, inv_std)


def send_kernel(pair_ref, w_in_ref, w_out_ref, w_head_t_ref, send_ref, rows_ref):
    n_row = send_ref.shape[0]
    span = send_ref.shape[1]
    channels = pair_ref.shape[-1]
    values = pair_ref[...].reshape(-1, channels).astype(f32)
    half = values.shape[0] // CYCLES
    x_hat, _ = normalize(values)
    hidden = jnp.maximum(dot(x_hat.astype(bf16), w_in_ref[...]), 0.0).astype(bf16)
    residual = (values + dot(hidden, w_out_ref[...])).astype(bf16)
    wide = jnp.concatenate([residual[:half], residual[half:]], axis=1)
    rows_ref[...] = encode(dot_t(wide, widen(w_head_t_ref[...])))
    for r in range(n_row):
        send_ref[r] = rows_ref[pl.ds(r, span, stride=n_row), :].astype(jnp.int16)


def prepare_kernel(
    pair_ref,
    bins_ref,
    w_in_ref,
    w_out_ref,
    w_head_t_ref,
    hidden_ref,
    normed_t_ref,
    residual_t_ref,
    x_hat_ref,
    inv_ref,
    logits_ref,
    bins_wide_ref,
    values_ref,
):
    channels = pair_ref.shape[-1]
    n_row = pair_ref.shape[2] // CYCLES
    count = pair_ref.shape[1]
    for a in range(CYCLES):
        for b in range(CYCLES):
            values_ref[a, :, b] = pair_ref[b, :, a * n_row : (a + 1) * n_row, :].astype(f32)
    values = values_ref[...].reshape(-1, channels)
    half = values.shape[0] // CYCLES
    x_hat, inv_std = normalize(values)
    normed = x_hat.astype(bf16)
    hidden = jnp.maximum(dot(normed, w_in_ref[...]), 0.0).astype(bf16)
    residual = (values + dot(hidden, w_out_ref[...])).astype(bf16)
    hidden_ref[...] = hidden
    normed_t_ref[...] = normed.T
    residual_t_ref[...] = residual.T
    x_hat_ref[...] = x_hat
    inv_ref[...] = jnp.broadcast_to(inv_std, x_hat.shape)
    logits_ref[...] = dot_t(
        jnp.concatenate([residual[:half], residual[half:]], axis=1), widen(w_head_t_ref[...])
    )
    columns = bins_ref.shape[-1]
    row_of = lax.broadcasted_iota(jnp.int32, (1, n_row, columns), 1)
    column_of = lax.broadcasted_iota(jnp.int32, (1, n_row, columns), 2)
    own = column_of % n_row == row_of
    lane = lax.broadcasted_iota(jnp.int32, (columns, channels), 1)
    source = lax.broadcasted_iota(jnp.int32, (columns, channels), 0)
    spread = (lane // (channels // CYCLES) == source // n_row).astype(f32).astype(bf16)
    for b in range(CYCLES):
        bins = bins_ref[b].astype(f32)
        picked = jnp.where(own, jnp.broadcast_to(bins[:, None, :], (count, n_row, columns)), 0.0)
        wide = dot(picked.reshape(count * n_row, columns).astype(bf16), spread)
        bins_wide_ref[:, b] = wide.astype(bf16).reshape(count, n_row, channels)


def pair_gradient(d_logit, w_head_wide):
    wide = dot(d_logit, w_head_wide)
    channels = wide.shape[1] // CYCLES
    return jnp.concatenate([wide[:, :channels], wide[:, channels:]], axis=0)


def hidden_gradient(d_update, hidden, w_out):
    back = dot_t(d_update, w_out).astype(bf16)
    return jnp.where(hidden > 0, back, jnp.zeros_like(back))


def weights_kernel(
    recv_ref,
    hidden_ref,
    normed_t_ref,
    residual_t_ref,
    logits_ref,
    bins_wide_ref,
    w_out_ref,
    w_head_t_ref,
    d_logit_ref,
    part_ref,
    rows_ref,
    in_ref,
    out_ref,
    head_ref,
):
    step = pl.program_id(0)
    n_row = recv_ref.shape[0]
    span = recv_ref.shape[1]
    channels = logits_ref.shape[-1]
    bins_count = channels // CYCLES
    half = span * n_row

    for r in range(n_row):
        rows_ref[pl.ds(r, span, stride=n_row), :] = decode(recv_ref[r])
    sym = logits_ref[...] + rows_ref[...]
    lane = lax.broadcasted_iota(jnp.int32, (1, channels), 1)
    left = lane < bins_count
    low = jnp.max(jnp.where(left, sym, -jnp.inf), axis=-1, keepdims=True)
    high = jnp.max(jnp.where(left, -jnp.inf, sym), axis=-1, keepdims=True)
    grown = jnp.exp(sym - jnp.where(left, low, high))
    low = jnp.sum(jnp.where(left, grown, 0.0), axis=-1, keepdims=True)
    high = jnp.sum(jnp.where(left, 0.0, grown), axis=-1, keepdims=True)
    probability = grown / jnp.where(left, low, high)
    own_bin = (lane % bins_count).astype(f32)
    bins = bins_wide_ref[...].reshape(half, channels).astype(f32)
    d_sym = probability - jnp.where(bins == own_bin, 1.0, 0.0)
    d_logit = (d_sym + d_sym).astype(bf16)
    d_logit_ref[...] = d_logit

    d_update = pair_gradient(d_logit, widen(w_head_t_ref[...])).astype(bf16)
    hidden = hidden_ref[...]
    d_hidden = hidden_gradient(d_update, hidden, w_out_ref[...])
    g_in = dot(normed_t_ref[...], d_hidden)
    g_out = dot(d_update.T, hidden)
    g_head = jnp.where(
        left,
        dot(residual_t_ref[:, :half], d_logit),
        dot(residual_t_ref[:, half:], d_logit),
    )

    @pl.when(step == 0)
    def _():
        in_ref[...] = g_in
        out_ref[...] = g_out
        head_ref[...] = g_head

    @pl.when(step > 0)
    def _():
        in_ref[...] += g_in
        out_ref[...] += g_out
        head_ref[...] += g_head

    @pl.when(step == STEPS - 1)
    def _():
        rows = channels // n_row
        tiles = in_ref.shape[1] // channels
        long = tiles * rows
        total_out = out_ref[...].T
        for r in range(n_row):
            mine = in_ref[r * rows : (r + 1) * rows, :]
            part_ref[r, 0:long, :] = jnp.concatenate(
                [mine[:, t * channels : (t + 1) * channels] for t in range(tiles)], axis=0
            ).astype(bf16)
            part_ref[r, long : 2 * long, :] = total_out[r * long : (r + 1) * long, :].astype(bf16)
            mine = head_ref[r * rows : (r + 1) * rows, :]
            part_ref[r, 2 * long : 2 * long + 2 * rows, :] = jnp.concatenate(
                [mine, jnp.zeros_like(mine)], axis=0
            ).astype(bf16)


def pair_kernel(
    d_logit_ref, hidden_ref, x_hat_ref, inv_ref, w_in_ref, w_out_ref, w_head_t_ref, grad_ref
):
    channels = grad_ref.shape[-1]
    count = grad_ref.shape[1]
    n_row = grad_ref.shape[2] // CYCLES
    d_resid = pair_gradient(d_logit_ref[...], widen(w_head_t_ref[...]))
    d_hidden = hidden_gradient(d_resid.astype(bf16), hidden_ref[...], w_out_ref[...])
    d_normed = dot_t(d_hidden, w_in_ref[...])
    x_hat = x_hat_ref[...]
    first_mean = jnp.mean(d_normed, axis=-1, keepdims=True)
    second_mean = jnp.mean(d_normed * x_hat, axis=-1, keepdims=True)
    d_pair = d_resid + inv_ref[...] * (d_normed - first_mean - x_hat * second_mean)
    d_pair = d_pair.astype(bf16).reshape(CYCLES, count, CYCLES, n_row, channels)
    for a in range(CYCLES):
        for b in range(CYCLES):
            grad_ref[b, :, a * n_row : (a + 1) * n_row, :] = d_pair[a, :, b]


def lanes_of(shape, axis):
    return lax.broadcasted_iota(jnp.int32, shape, axis)


def fold_matrix(width, kind):
    shape = (128, 128)
    return (lanes_of(shape, 0) % width == lanes_of(shape, 1) % width).astype(f32).astype(kind)


def middle_kernel(recv_ref, send_ref):
    n_col = send_ref.shape[0] // 4
    total = recv_ref[0].astype(f32)
    for r in range(1, recv_ref.shape[0]):
        total = total + recv_ref[r].astype(f32)
    rows, tiles = 8, 4
    mine = total[: rows * tiles]
    group = lanes_of((1, rows, 128), 2) // 16 == lanes_of((1, rows, 128), 1)
    spread = jnp.where(group, jnp.broadcast_to(mine[:, None, :], (rows * tiles, rows, 128)), 0.0)
    folded = dot(spread.reshape(-1, 128).astype(bf16), fold_matrix(16, bf16))
    folded = folded.reshape(tiles, rows, rows, 128)
    slot = lanes_of((1, rows, 1, 128), 3) // 16 == lanes_of((1, rows, 1, 128), 1)
    part_in = jnp.sum(jnp.where(slot, folded, 0.0), axis=1).reshape(n_col, 128)
    mine = total[32:64]
    group = lanes_of((1, n_col, 128), 2) // 4 == lanes_of((1, n_col, 128), 1)
    spread = jnp.where(group, jnp.broadcast_to(mine[:, None, :], (32, n_col, 128)), 0.0)
    folded = dot(spread.reshape(-1, 128).astype(bf16), fold_matrix(4, bf16))
    folded = folded.reshape(32, n_col, 128)
    slot = lanes_of((32, 1, 128), 2) // 4 == lanes_of((32, 1, 128), 0)
    part_out = jnp.sum(jnp.where(slot, folded, 0.0), axis=0)
    mine = total[64:72]
    group = lanes_of((1, n_col, 128), 2) % 64 // 2 == lanes_of((1, n_col, 128), 1)
    spread = jnp.where(group, jnp.broadcast_to(mine[:, None, :], (8, n_col, 128)), 0.0)
    folded = dot(spread.reshape(-1, 128).astype(bf16), fold_matrix(2, bf16))
    folded = folded.reshape(8, n_col, 128)
    slot = lanes_of((8, 1, 128), 2) // 2 == lanes_of((8, 1, 128), 0)
    part_head = jnp.sum(jnp.where(slot, folded, 0.0), axis=0)
    send_ref[pl.ds(0, n_col, stride=4), :] = part_in
    send_ref[pl.ds(1, n_col, stride=4), :] = part_out
    send_ref[pl.ds(2, n_col, stride=4), :] = part_head
    send_ref[pl.ds(3, n_col, stride=4), :] = jnp.zeros_like(part_head)


def final_kernel(scale, recv_ref, in_ref, out_t_ref, head_t_ref):
    total = recv_ref[0:8, :]
    for c in range(1, recv_ref.shape[0] // 8):
        total = total + recv_ref[c * 8 : (c + 1) * 8, :]
    total = (total[0:4] + total[4:8]) * scale

    def unfold(row, out, row_of, column_of):
        count, width = out.shape
        shape = (count, 128)
        picked = jnp.where(
            row_of(lanes_of(shape, 1)) == lanes_of(shape, 0), jnp.broadcast_to(row, shape), 0.0
        )
        shape = (128, width)
        fold = (column_of(lanes_of(shape, 0)) == lanes_of(shape, 1)).astype(f32)
        out[...] = jnp.dot(
            picked, fold, precision=lax.Precision.HIGHEST, preferred_element_type=f32
        )

    unfold(total[0:1], in_ref, lambda lane: lane // 16, lambda lane: lane % 16)
    unfold(total[1:2], out_t_ref, lambda lane: lane % 4, lambda lane: lane // 4)
    unfold(total[2:3], head_t_ref, lambda lane: lane % 2, lambda lane: lane // 2)


def whole(array):
    return pl.BlockSpec(array.shape, lambda g: (0,) * array.ndim)


def params():
    return pltpu.CompilerParams(vmem_limit_bytes=62 * 1024 * 1024)


def shards(pair_rep, true_bins, w_in, w_out, w_head):
    row_count, col_count, channels = pair_rep.shape
    n_row = lax.axis_size("row")
    n_col = lax.axis_size("col")
    hidden_count = w_in.shape[1]
    bins_count = w_head.shape[1]
    pairs = row_count * col_count
    cycled = pair_rep.reshape(CYCLES, n_col, col_count, channels)
    bins = true_bins.reshape(CYCLES, n_col, col_count)
    w_head_t = w_head.T
    count = n_col // STEPS
    span = CYCLES * count
    block = pairs // STEPS
    half = block // CYCLES
    pair_spec = pl.BlockSpec((CYCLES, count, col_count, channels), lambda g: (0, g, 0, 0))
    send_spec = pl.BlockSpec((n_row, span, channels), lambda g: (0, g, 0))

    send = pl.pallas_call(
        send_kernel,
        grid=(STEPS,),
        in_specs=[pair_spec, whole(w_in), whole(w_out), whole(w_head_t)],
        out_specs=send_spec,
        out_shape=jax.ShapeDtypeStruct((n_row, CYCLES * n_col, channels), jnp.int16),
        scratch_shapes=[pltpu.VMEM((half, channels), jnp.int32)],
        compiler_params=params(),
        name="forward",
    )(cycled, w_in, w_out, w_head_t)

    recv = lax.all_to_all(
        send.reshape(n_row * n_col, CYCLES, channels),
        ("row", "col"),
        split_axis=0,
        concat_axis=0,
        tiled=True,
    ).reshape(n_row, CYCLES * n_col, channels)

    def rows_spec(width):
        return pl.BlockSpec((block, width), lambda g: (g, 0))

    def columns_spec(height):
        return pl.BlockSpec((height, block), lambda g: (0, g))

    logits_spec = pl.BlockSpec((half, channels), lambda g: (g, 0))
    bins_spec = pl.BlockSpec((count, CYCLES, n_row, channels), lambda g: (g, 0, 0, 0))
    kept_specs = [
        rows_spec(hidden_count),
        columns_spec(channels),
        columns_spec(channels),
        rows_spec(channels),
        rows_spec(channels),
        logits_spec,
        bins_spec,
    ]
    hidden, normed_t, residual_t, x_hat, inv_std, logits, bins_wide = pl.pallas_call(
        prepare_kernel,
        grid=(STEPS,),
        in_specs=[
            pair_spec,
            pl.BlockSpec((CYCLES, count, col_count), lambda g: (0, g, 0)),
            whole(w_in),
            whole(w_out),
            whole(w_head_t),
        ],
        out_specs=kept_specs,
        out_shape=[
            jax.ShapeDtypeStruct((pairs, hidden_count), bf16),
            jax.ShapeDtypeStruct((channels, pairs), bf16),
            jax.ShapeDtypeStruct((channels, pairs), bf16),
            jax.ShapeDtypeStruct((pairs, channels), f32),
            jax.ShapeDtypeStruct((pairs, channels), f32),
            jax.ShapeDtypeStruct((pairs // CYCLES, channels), f32),
            jax.ShapeDtypeStruct((n_col, CYCLES, n_row, channels), bf16),
        ],
        scratch_shapes=[pltpu.VMEM((CYCLES, count, CYCLES, n_row, channels), f32)],
        compiler_params=params(),
        cost_estimate=pl.CostEstimate(
            flops=2 * pairs * 2 * channels * hidden_count, bytes_accessed=8 * 2**20, transcendentals=0
        ),
        name="prepare",
    )(cycled, bins, w_in, w_out, w_head_t)

    part_rows = 2 * (hidden_count // n_row) + 16
    d_logit, part = pl.pallas_call(
        weights_kernel,
        grid=(STEPS,),
        in_specs=[
            send_spec,
            rows_spec(hidden_count),
            columns_spec(channels),
            columns_spec(channels),
            logits_spec,
            bins_spec,
            whole(w_out),
            whole(w_head_t),
        ],
        out_specs=[
            logits_spec,
            pl.BlockSpec((n_row, part_rows, channels), lambda g: (0, 0, 0)),
        ],
        out_shape=[
            jax.ShapeDtypeStruct((pairs // CYCLES, channels), bf16),
            jax.ShapeDtypeStruct((n_row, part_rows, channels), bf16),
        ],
        scratch_shapes=[
            pltpu.VMEM((half, channels), f32),
            pltpu.VMEM((channels, hidden_count), f32),
            pltpu.VMEM((channels, hidden_count), f32),
            pltpu.VMEM((channels, channels), f32),
        ],
        compiler_params=params(),
        name="weights",
    )(recv, hidden, normed_t, residual_t, logits, bins_wide, w_out, w_head_t)

    part = lax.all_to_all(part, "row", split_axis=0, concat_axis=0, tiled=True)

    d_pair = pl.pallas_call(
        pair_kernel,
        grid=(STEPS,),
        in_specs=[
            logits_spec,
            rows_spec(hidden_count),
            rows_spec(channels),
            rows_spec(channels),
            whole(w_in),
            whole(w_out),
            whole(w_head_t),
        ],
        out_specs=pair_spec,
        out_shape=jax.ShapeDtypeStruct(cycled.shape, bf16),
        compiler_params=params(),
        cost_estimate=pl.CostEstimate(
            flops=2 * pairs * 2 * channels * hidden_count, bytes_accessed=5 * 2**20, transcendentals=0
        ),
        name="pair",
    )(d_logit, hidden, x_hat, inv_std, w_in, w_out, w_head_t)

    share = pl.pallas_call(
        middle_kernel,
        out_shape=jax.ShapeDtypeStruct((4 * n_col, channels), f32),
        compiler_params=params(),
        name="sum_rows",
    )(part)
    share = lax.all_to_all(
        share.reshape(n_col, 4, channels), "col", split_axis=0, concat_axis=0, tiled=True
    ).reshape(4 * n_col, channels)
    grad_in, grad_out_t, grad_head_t = pl.pallas_call(
        functools.partial(final_kernel, 1.0 / (row_count * n_row)),
        out_shape=[
            jax.ShapeDtypeStruct((channels // n_row, hidden_count // n_col), f32),
            jax.ShapeDtypeStruct((channels // n_col, hidden_count // n_row), f32),
            jax.ShapeDtypeStruct((bins_count // n_col, channels // n_row), f32),
        ],
        compiler_params=params(),
        name="sum_columns",
    )(share)
    return (
        d_pair.reshape(row_count, col_count, channels),
        grad_in,
        grad_out_t.T,
        grad_head_t.T,
    )


def solution(mesh):
    placed = (P("row", "col", None), P("row", "col"), P(), P(), P())
    return jax.shard_map(
        shards,
        mesh=mesh,
        in_specs=placed,
        out_specs=(P("row", "col", None), P("row", "col"), P("row", "col"), P("row", "col")),
        check_vma=False,
    )
```

time: 112 us -> 89.3 us (0.80)
  local copies, waits for them, and re-layouts: 28.3 us -> 2.74 us
  blocking collectives: 40 us -> 15.5 us
  waiting for transfers between devices: 1.07 us -> 12.6 us
  Pallas kernels: 17.4 us -> 26.8 us
  starting transfers between devices: 22.2 us -> 30.3 us
  other arithmetic: 1.43 us -> 0 us
    unnamed x56 -> x5, local copies, waits for them, and re-layouts: 27.4 us -> 2.74 us
    all_to_all x1 -> x0, blocking collectives: 18.9 us -> none  [shards(): lax.all_to_all(share, 'col', split_axis=0, concat_axis=0, tiled=True)]
    all_to_all x1, waiting for transfers between devices: 1.07 us -> 10 us  [shards(): lax.all_to_all(send.reshape(n_row * n_col, CYCLES, channels), ('row', 'co...]
    all_to_all x0 -> x1, starting transfers between devices: none -> 8.09 us  [shards(): lax.all_to_all(share.reshape(n_col, 4, channels), 'col', split_axis=0, co...]
    pallas_call x2 -> x3, Pallas kernels: 7.58 us -> 13.8 us  [the longest x1 6.39 us: shards(): pl.pallas_call(weights_kernel, grid=(STEPS,), in_specs=[send_spec, rows_s...]
    all_to_all x1, blocking collectives: 21.2 us -> 15.5 us  [shards(): part = lax.all_to_all(part, 'row', split_axis=0, concat_axis=0, tiled=True)]
    all_to_all x0 -> x1, waiting for transfers between devices: none -> 2.58 us  [shards(): lax.all_to_all(share.reshape(n_col, 4, channels), 'col', split_axis=0, co...]
    pallas_call x1, Pallas kernels: 3.67 us -> 5.85 us  [shards(): pl.pallas_call(prepare_kernel, grid=(STEPS,), in_specs=[pair_spec, pl.Blo...]
  transfers between devices with their start and end apart: 1 -> 2, of which waited for: 1 -> 2; matrix products, arithmetic and copies ran while one was open for 2% -> 2% of each run, Pallas kernels for 3% -> 13%
where the time goes in v3:
time: 89.3 us; the launch traced here: 88.5 us
  starting transfers between devices  30.3 us (34%)
  Pallas kernels  26.8 us (30%)
  blocking collectives  15.5 us (17%)
  waiting for transfers between devices  12.6 us (14%)
  local copies, waits for them, and re-layouts  2.74 us (3%)
    all_to_all x1, starting transfers between devices, shards(): lax.all_to_all(send.reshape(n_row * n_col, CYCLES, channels), ('row', 'co...  22.2 us
    all_to_all x1, blocking collectives, shards(): part = lax.all_to_all(part, 'row', split_axis=0, concat_axis=0, tiled=True)  15.5 us
    all_to_all x1, waiting for transfers between devices, shards(): lax.all_to_all(send.reshape(n_row * n_col, CYCLES, channels), ('row', 'co...  10 us
    all_to_all x1, starting transfers between devices, shards(): lax.all_to_all(share.reshape(n_col, 4, channels), 'col', split_axis=0, co...  8.09 us
    pallas_call x1, Pallas kernels, shards(): pl.pallas_call(weights_kernel, grid=(STEPS,), in_specs=[send_spec, rows_s...  6.39 us
    pallas_call x1, Pallas kernels, shards(): pl.pallas_call(prepare_kernel, grid=(STEPS,), in_specs=[pair_spec, pl.Blo...  5.85 us
    pallas_call x1, Pallas kernels, shards(): pl.pallas_call(pair_kernel, grid=(STEPS,), in_specs=[logits_spec, rows_sp...  5.49 us
    pallas_call x1, Pallas kernels, shards(): pl.pallas_call(send_kernel, grid=(STEPS,), in_specs=[pair_spec, whole(w_i...  5.45 us
  transfers between devices with their start and end apart: 2, of which 2 were waited for; matrix products, arithmetic and copies ran while one was open for 2% of the time, Pallas kernels for 13%

profile of v3, /device:TPU:1, one launch (start us, length us, event | category | flops | bytes accessed | tf_op | source)
XLA Modules:
  0.0 88.5 jit_solution(15877597377980407788)
XLA Ops:
  0.6 5.5 %forward.1 = s16[16,64,128]{2,1,0:T(8,128)(2,1)} custom-call(bf16[2,32,32,128]{3,2,1,0:T(8,128)(2,1)} %bitcast.13, bf16[128,512]{1,0:T(8,128)(2,1)} %w_in_ref.5, bf16[512,128]{1,0:T(8,128)(2,1)} %w_out_ref.7, bf16[64,128]{1,0:T(8,128)(2,1)} %bitcast.17), custom_call_target="tpu_custom_call" | custom-call | tf_op jit(solution)/shard_map/forward/pallas_call | solution.py:323
  6.1 22.2 %all-to-all-start = ((s16[512,2,128]{2,1,0:T(2,128)(2,1)}), s16[512,2,128]{2,1,0:T(2,128)(2,1)S(1)}, u32[]{:S(2)}, u32[]{:S(2)}) async-start(s16[512,2,128]{2,1,0:T(2,128)(2,1)} %bitcast.11), calls=%async_computation | async-start | bytes 524288 | tf_op jit(solution)/shard_map/all_to_all | solution.py:334
  28.3 1.4 %copy.9 = s32[64,32]{1,0:T(8,128)} copy(s32[64,32]{0,1:T(8,128)} %param.6) | data formatting | bytes 16384 | tf_op args[1]
  29.7 5.9 %prepare.1 = (bf16[2048,512]{1,0:T(8,128)(2,1)}, bf16[128,2048]{1,0:T(8,128)(2,1)}, bf16[128,2048]{1,0:T(8,128)(2,1)}, f32[2048,128]{1,0:T(8,128)}, f32[2048,128...) custom-call(bf16[2,32,32,128]{3,2,1,0:T(8,128)(2,1)} %bitcast.14, s32[2,32,32]{2,1,0:T(8,128)} %bitcast.21, ...), custom_call_target="tpu_custom_call" | custom-call | flops 536870912 | bytes 8388608 | tf_op jit(solution)/shard_map/prepare/pallas_call | solution.py:359
  35.5 10.0 %all-to-all-done = s16[512,2,128]{2,1,0:T(2,128)(2,1)S(1)} async-done(((s16[512,2,128]{2,1,0:T(2,128)(2,1)}), s16[512,2,128]{2,1,0:T(2,128)(2,1)S(1)}, u32[]{:S(2)}, u32[]{:S(2)}) %all-to-all-start) | async-done | bytes 262176 | tf_op jit(solution)/shard_map/all_to_all | solution.py:334
  45.5 0.0 copy-start
  45.5 0.7 copy-done
  46.2 6.4 %weights.1 = (bf16[1024,128]{1,0:T(8,128)(2,1)}, bf16[16,80,128]{2,1,0:T(8,128)(2,1)}) custom-call(s16[16,64,128]{2,1,0:T(8,128)(2,1)} %bitcast.10, bf16[2048,512]{1,0:T(8,128)(2,1)} %get-tuple-element.16.hidden_ref, bf16[128,2048]{1,0:T(8,128)(2,1)} %get-tuple-element.17.normed_t_ref, bf16[128,2048]{1,0:T(8,128)(2,1)} %get-tuple-element.18.residual_t_ref, ...), custom_call_target="tpu_custom_call" | custom-call | tf_op jit(solution)/shard_map/weights/pallas_call | solution.py:388
  52.6 15.5 %all_to_all.15.recv_ref = bf16[16,80,128]{2,1,0:T(8,128)(2,1)} all-to-all(bf16[16,80,128]{2,1,0:T(8,128)(2,1)} %get-tuple-element.24), channel_id=1, replica_groups=mesh['row'=16,'col'=32] {'row'}, dimensions={0} | all-to-all | bytes 655360 | tf_op jit(solution)/shard_map/all_to_all | solution.py:419
  68.1 1.9 %sum_rows.1 = f32[128,128]{1,0:T(8,128)} custom-call(bf16[16,80,128]{2,1,0:T(8,128)(2,1)} %all_to_all.15.recv_ref), custom_call_target="tpu_custom_call" | custom-call | tf_op jit(solution)/shard_map/sum_rows/pallas_call | solution.py:442
  70.0 8.1 %all-to-all-start.2 = ((f32[32,4,128]{2,1,0:T(4,128)}), f32[32,4,128]{2,1,0:T(4,128)S(1)}, u32[]{:S(2)}, u32[]{:S(2)}) async-start(f32[32,4,128]{2,1,0:T(4,128)} %bitcast.16), calls=%async_computation.2 | async-start | bytes 131072 | tf_op jit(solution)/shard_map/all_to_all | solution.py:448
  78.1 5.5 %pair.1 = bf16[2,32,32,128]{3,2,1,0:T(8,128)(2,1)} custom-call(bf16[1024,128]{1,0:T(8,128)(2,1)} %get-tuple-element.21.d_logit_ref, bf16[2048,512]{1,0:T(8,128)(2,1)} %get-tuple-element.16.hidden_ref, f32[2048,128]{1,0:T(8,128)} %get-tuple-element.22.x_hat_ref, f32[2048,128]{1,0:T(8,128)} %get-tuple-element.23.inv_ref, bf16[128,512]{1,0:T(8,128)(2,1)} %w_in_ref.5, ...), custom_call_target="tpu_custom_call" | custom-call | flops 536870912 | bytes 5242880 | tf_op jit(solution)/shard_map/pair/pallas_call | solution.py:421
  83.6 2.6 %all-to-all-done.2 = f32[32,4,128]{2,1,0:T(4,128)S(1)} async-done(((f32[32,4,128]{2,1,0:T(4,128)}), f32[32,4,128]{2,1,0:T(4,128)S(1)}, u32[]{:S(2)}, u32[]{:S(2)}) %all-to-all-start.2) | async-done | bytes 65568 | tf_op jit(solution)/shard_map/all_to_all | solution.py:448
  86.2 0.0 copy-start.1
  86.2 0.6 copy-done.1
  86.8 1.7 %sum_columns.1 = (f32[8,16]{1,0:T(8,128)}, f32[4,32]{1,0:T(4,128)}, f32[2,8]{1,0:T(2,128)}) custom-call(f32[128,128]{1,0:T(8,128)} %bitcast.15), custom_call_target="tpu_custom_call" | custom-call | tf_op jit(solution)/shard_map/sum_columns/pallas_call | solution.py:451
Async XLA Ops:
  6.1 39.5 %all-to-all-start = ((s16[512,2,128]{2,1,0:T(2,128)(2,1)}), s16[512,2,128]{2,1,0:T(2,128)(2,1)S(1)}, u32[]{:S(2)}, u32[]{:S(2)}) async-start(s16[512,2,128]{2,1,0:T(2,128)(2,1)} %bitcast.11), calls=%async_computation | async-start | bytes 524288 | tf_op jit(solution)/shard_map/all_to_all | solution.py:334
  45.5 0.7 copy-start
  70.0 16.2 %all-to-all-start.2 = ((f32[32,4,128]{2,1,0:T(4,128)}), f32[32,4,128]{2,1,0:T(4,128)S(1)}, u32[]{:S(2)}, u32[]{:S(2)}) async-start(f32[32,4,128]{2,1,0:T(4,128)} %bitcast.16), calls=%async_computation.2 | async-start | bytes 131072 | tf_op jit(solution)/shard_map/all_to_all | solution.py:448
  86.2 0.6 copy-start.1

commit v4 on v3

--- a/solution.py
+++ b/solution.py
@@ -15,7 +15,8 @@
 code_steps = 1850.0
 
 CYCLES = 2
-STEPS = 4
+FORWARD_STEPS = 1
+STEPS = 2
 
 
 def dot(first, second):
@@ -193,7 +194,7 @@
         out_ref[...] += g_out
         head_ref[...] += g_head
 
-    @pl.when(step == STEPS - 1)
+    @pl.when(step == pl.num_programs(0) - 1)
     def _():
         rows = channels // n_row
         tiles = in_ref.shape[1] // channels
@@ -239,7 +240,7 @@
     return (lanes_of(shape, 0) % width == lanes_of(shape, 1) % width).astype(f32).astype(kind)
 
 
-def middle_kernel(recv_ref, send_ref):
+def middle_kernel(recv_ref, done_ref, send_ref, rows_ref):
     n_col = send_ref.shape[0] // 4
     total = recv_ref[0].astype(f32)
     for r in range(1, recv_ref.shape[0]):
@@ -250,24 +251,25 @@
     spread = jnp.where(group, jnp.broadcast_to(mine[:, None, :], (rows * tiles, rows, 128)), 0.0)
     folded = dot(spread.reshape(-1, 128).astype(bf16), fold_matrix(16, bf16))
     folded = folded.reshape(tiles, rows, rows, 128)
-    slot = lanes_of((1, rows, 1, 128), 3) // 16 == lanes_of((1, rows, 1, 128), 1)
+    slot = lanes_of((1, rows, 1, 128), 3) // 16 == (8 - lanes_of((1, rows, 1, 128), 1)) % 8
     part_in = jnp.sum(jnp.where(slot, folded, 0.0), axis=1).reshape(n_col, 128)
-    mine = total[32:64]
-    group = lanes_of((1, n_col, 128), 2) // 4 == lanes_of((1, n_col, 128), 1)
-    spread = jnp.where(group, jnp.broadcast_to(mine[:, None, :], (32, n_col, 128)), 0.0)
-    folded = dot(spread.reshape(-1, 128).astype(bf16), fold_matrix(4, bf16))
-    folded = folded.reshape(32, n_col, 128)
-    slot = lanes_of((32, 1, 128), 2) // 4 == lanes_of((32, 1, 128), 0)
-    part_out = jnp.sum(jnp.where(slot, folded, 0.0), axis=0)
+    send_ref[pl.ds(0, n_col, stride=4), :] = part_in
+    rows_ref[...] = jnp.concatenate([total[32:64]] * 4, axis=0).T
+    lane = lanes_of((1, 128), 1)
+    part_out = rows_ref[pl.ds(0, n_col, stride=4), :]
+    for j in range(1, 4):
+        part_out = jnp.where(
+            lane // 32 == 4 - j, rows_ref[pl.ds(j, n_col, stride=4), :], part_out
+        )
+    send_ref[pl.ds(1, n_col, stride=4), :] = part_out
     mine = total[64:72]
-    group = lanes_of((1, n_col, 128), 2) % 64 // 2 == lanes_of((1, n_col, 128), 1)
-    spread = jnp.where(group, jnp.broadcast_to(mine[:, None, :], (8, n_col, 128)), 0.0)
-    folded = dot(spread.reshape(-1, 128).astype(bf16), fold_matrix(2, bf16))
-    folded = folded.reshape(8, n_col, 128)
-    slot = lanes_of((8, 1, 128), 2) // 2 == lanes_of((8, 1, 128), 0)
-    part_head = jnp.sum(jnp.where(slot, folded, 0.0), axis=0)
-    send_ref[pl.ds(0, n_col, stride=4), :] = part_in
-    send_ref[pl.ds(1, n_col, stride=4), :] = part_out
+    mine = mine + pltpu.roll(mine, 64, 1)
+    rows_ref[...] = jnp.concatenate([mine] * 16, axis=0).T
+    part_head = jnp.where(
+        lane // 8 == 15,
+        rows_ref[pl.ds(1, n_col, stride=2), :],
+        rows_ref[pl.ds(0, n_col, stride=2), :],
+    )
     send_ref[pl.ds(2, n_col, stride=4), :] = part_head
     send_ref[pl.ds(3, n_col, stride=4), :] = jnp.zeros_like(part_head)
 
@@ -278,95 +280,95 @@
         total = total + recv_ref[c * 8 : (c + 1) * 8, :]
     total = (total[0:4] + total[4:8]) * scale
 
-    def unfold(row, out, row_of, column_of):
+    def unfold(row, out):
         count, width = out.shape
-        shape = (count, 128)
-        picked = jnp.where(
-            row_of(lanes_of(shape, 1)) == lanes_of(shape, 0), jnp.broadcast_to(row, shape), 0.0
-        )
-        shape = (128, width)
-        fold = (column_of(lanes_of(shape, 0)) == lanes_of(shape, 1)).astype(f32)
-        out[...] = jnp.dot(
-            picked, fold, precision=lax.Precision.HIGHEST, preferred_element_type=f32
-        )
-
-    unfold(total[0:1], in_ref, lambda lane: lane // 16, lambda lane: lane % 16)
-    unfold(total[1:2], out_t_ref, lambda lane: lane % 4, lambda lane: lane // 4)
-    unfold(total[2:3], head_t_ref, lambda lane: lane % 2, lambda lane: lane // 2)
+        if width * 8 <= 128:
+            spread = jnp.broadcast_to(row, (8, 128))
+            spread = pltpu.roll(spread, 0, 1, stride=width, stride_axis=0)
+        else:
+            spread = jnp.concatenate(
+                [pltpu.roll(row, i * width, 1) if i else row for i in range(count)], axis=0
+            )
+        out[...] = spread[:count, :width]
+
+    unfold(total[0:1], in_ref)
+    unfold(total[1:2], out_t_ref)
+    unfold(total[2:3], head_t_ref)
 
 
 def whole(array):
     return pl.BlockSpec(array.shape, lambda g: (0,) * array.ndim)
 
 
-def params():
-    return pltpu.CompilerParams(vmem_limit_bytes=62 * 1024 * 1024)
-
-
-def shards(pair_rep, true_bins, w_in, w_out, w_head):
+ROOM = 48 * 1024 * 1024
+
+
+def whole_array(array):
+    return pl.BlockSpec(array.shape, lambda: (0,) * array.ndim)
+
+
+def params(limit=62 * 1024 * 1024):
+    return pltpu.CompilerParams(vmem_limit_bytes=limit)
+
+
+def in_hbm(array):
+    return pltpu.with_memory_space_constraint(array, pltpu.HBM)
+
+
+def forward_call(pair_rep, w_in, w_out, w_head_t, n_row, n_col):
     row_count, col_count, channels = pair_rep.shape
-    n_row = lax.axis_size("row")
-    n_col = lax.axis_size("col")
+    count = n_col // FORWARD_STEPS
+    return pl.pallas_call(
+        send_kernel,
+        grid=(FORWARD_STEPS,),
+        in_specs=[
+            pl.BlockSpec((CYCLES, count, col_count, channels), lambda g: (0, g, 0, 0)),
+            whole(w_in),
+            whole(w_out),
+            whole(w_head_t),
+        ],
+        out_specs=pl.BlockSpec((n_row, CYCLES * count, channels), lambda g: (0, g, 0)),
+        out_shape=jax.ShapeDtypeStruct((n_row, CYCLES * n_col, channels), jnp.int16),
+        scratch_shapes=[pltpu.VMEM((CYCLES * count * n_row, channels), jnp.int32)],
+        compiler_params=params(),
+        name="forward",
+    )(pair_rep.reshape(CYCLES, n_col, col_count, channels), w_in, w_out, w_head_t)
+
+
+def rows_spec(block, width):
+    return pl.BlockSpec((block, width), lambda g: (g, 0))
+
+
+def columns_spec(height, block):
+    return pl.BlockSpec((height, block), lambda g: (0, g))
+
+
+def prepare_call(pair_rep, true_bins, w_in, w_out, w_head_t, n_row, n_col):
+    row_count, col_count, channels = pair_rep.shape
+    pairs = row_count * col_count
     hidden_count = w_in.shape[1]
-    bins_count = w_head.shape[1]
-    pairs = row_count * col_count
-    cycled = pair_rep.reshape(CYCLES, n_col, col_count, channels)
-    bins = true_bins.reshape(CYCLES, n_col, col_count)
-    w_head_t = w_head.T
     count = n_col // STEPS
-    span = CYCLES * count
     block = pairs // STEPS
     half = block // CYCLES
-    pair_spec = pl.BlockSpec((CYCLES, count, col_count, channels), lambda g: (0, g, 0, 0))
-    send_spec = pl.BlockSpec((n_row, span, channels), lambda g: (0, g, 0))
-
-    send = pl.pallas_call(
-        send_kernel,
-        grid=(STEPS,),
-        in_specs=[pair_spec, whole(w_in), whole(w_out), whole(w_head_t)],
-        out_specs=send_spec,
-        out_shape=jax.ShapeDtypeStruct((n_row, CYCLES * n_col, channels), jnp.int16),
-        scratch_shapes=[pltpu.VMEM((half, channels), jnp.int32)],
-        compiler_params=params(),
-        name="forward",
-    )(cycled, w_in, w_out, w_head_t)
-
-    recv = lax.all_to_all(
-        send.reshape(n_row * n_col, CYCLES, channels),
-        ("row", "col"),
-        split_axis=0,
-        concat_axis=0,
-        tiled=True,
-    ).reshape(n_row, CYCLES * n_col, channels)
-
-    def rows_spec(width):
-        return pl.BlockSpec((block, width), lambda g: (g, 0))
-
-    def columns_spec(height):
-        return pl.BlockSpec((height, block), lambda g: (0, g))
-
-    logits_spec = pl.BlockSpec((half, channels), lambda g: (g, 0))
-    bins_spec = pl.BlockSpec((count, CYCLES, n_row, channels), lambda g: (g, 0, 0, 0))
-    kept_specs = [
-        rows_spec(hidden_count),
-        columns_spec(channels),
-        columns_spec(channels),
-        rows_spec(channels),
-        rows_spec(channels),
-        logits_spec,
-        bins_spec,
-    ]
-    hidden, normed_t, residual_t, x_hat, inv_std, logits, bins_wide = pl.pallas_call(
+    return pl.pallas_call(
         prepare_kernel,
         grid=(STEPS,),
         in_specs=[
-            pair_spec,
+            pl.BlockSpec((CYCLES, count, col_count, channels), lambda g: (0, g, 0, 0)),
             pl.BlockSpec((CYCLES, count, col_count), lambda g: (0, g, 0)),
             whole(w_in),
             whole(w_out),
             whole(w_head_t),
         ],
-        out_specs=kept_specs,
+        out_specs=[
+            rows_spec(block, hidden_count),
+            columns_spec(channels, block),
+            columns_spec(channels, block),
+            rows_spec(block, channels),
+            rows_spec(block, channels),
+            rows_spec(half, channels),
+            pl.BlockSpec((count, CYCLES, n_row, channels), lambda g: (g, 0, 0, 0)),
+        ],
         out_shape=[
             jax.ShapeDtypeStruct((pairs, hidden_count), bf16),
             jax.ShapeDtypeStruct((channels, pairs), bf16),
@@ -382,24 +384,38 @@
             flops=2 * pairs * 2 * channels * hidden_count, bytes_accessed=8 * 2**20, transcendentals=0
         ),
         name="prepare",
-    )(cycled, bins, w_in, w_out, w_head_t)
-
+    )(
+        pair_rep.reshape(CYCLES, n_col, col_count, channels),
+        true_bins.reshape(CYCLES, n_col, col_count),
+        w_in,
+        w_out,
+        w_head_t,
+    )
+
+
+def weights_call(recv, hidden, normed_t, residual_t, logits, bins_wide, w_out, w_head_t):
+    n_row, span, channels = recv.shape
+    pairs, hidden_count = hidden.shape
+    count = span // CYCLES // STEPS
+    block = pairs // STEPS
+    half = block // CYCLES
     part_rows = 2 * (hidden_count // n_row) + 16
-    d_logit, part = pl.pallas_call(
+    kept = [in_hbm(x) for x in (hidden, normed_t, residual_t, logits, bins_wide, w_out, w_head_t)]
+    return pl.pallas_call(
         weights_kernel,
         grid=(STEPS,),
         in_specs=[
-            send_spec,
-            rows_spec(hidden_count),
-            columns_spec(channels),
-            columns_spec(channels),
-            logits_spec,
-            bins_spec,
+            pl.BlockSpec((n_row, CYCLES * count, channels), lambda g: (0, g, 0)),
+            rows_spec(block, hidden_count),
+            columns_spec(channels, block),
+            columns_spec(channels, block),
+            rows_spec(half, channels),
+            pl.BlockSpec((count, CYCLES, n_row, channels), lambda g: (g, 0, 0, 0)),
             whole(w_out),
             whole(w_head_t),
         ],
         out_specs=[
-            logits_spec,
+            rows_spec(half, channels),
             pl.BlockSpec((n_row, part_rows, channels), lambda g: (0, 0, 0)),
         ],
         out_shape=[
@@ -412,52 +428,97 @@
             pltpu.VMEM((channels, hidden_count), f32),
             pltpu.VMEM((channels, channels), f32),
         ],
-        compiler_params=params(),
+        compiler_params=params(ROOM),
         name="weights",
-    )(recv, hidden, normed_t, residual_t, logits, bins_wide, w_out, w_head_t)
-
-    part = lax.all_to_all(part, "row", split_axis=0, concat_axis=0, tiled=True)
-
-    d_pair = pl.pallas_call(
+    )(recv, *kept)
+
+
+def pair_call(d_logit, hidden, x_hat, inv_std, w_in, w_out, w_head_t, shape, n_row, n_col):
+    row_count, col_count, channels = shape
+    pairs, hidden_count = hidden.shape
+    count = n_col // STEPS
+    block = pairs // STEPS
+    return pl.pallas_call(
         pair_kernel,
         grid=(STEPS,),
         in_specs=[
-            logits_spec,
-            rows_spec(hidden_count),
-            rows_spec(channels),
-            rows_spec(channels),
+            rows_spec(block // CYCLES, channels),
+            rows_spec(block, hidden_count),
+            rows_spec(block, channels),
+            rows_spec(block, channels),
             whole(w_in),
             whole(w_out),
             whole(w_head_t),
         ],
-        out_specs=pair_spec,
-        out_shape=jax.ShapeDtypeStruct(cycled.shape, bf16),
+        out_specs=pl.BlockSpec((CYCLES, count, col_count, channels), lambda g: (0, g, 0, 0)),
+        out_shape=jax.ShapeDtypeStruct((CYCLES, n_col, col_count, channels), bf16),
         compiler_params=params(),
         cost_estimate=pl.CostEstimate(
             flops=2 * pairs * 2 * channels * hidden_count, bytes_accessed=5 * 2**20, transcendentals=0
         ),
         name="pair",
-    )(d_logit, hidden, x_hat, inv_std, w_in, w_out, w_head_t)
-
-    share = pl.pallas_call(
+    )(in_hbm(d_logit), hidden, x_hat, inv_std, w_in, w_out, w_head_t)
+
+
+def middle_call(part, done, n_col):
+    return pl.pallas_call(
         middle_kernel,
-        out_shape=jax.ShapeDtypeStruct((4 * n_col, channels), f32),
-        compiler_params=params(),
+        in_specs=[whole_array(part), pl.BlockSpec(memory_space=pl.ANY)],
+        out_shape=jax.ShapeDtypeStruct((4 * n_col, part.shape[-1]), f32),
+        scratch_shapes=[pltpu.VMEM((128, 128), f32)],
+        compiler_params=params(ROOM),
         name="sum_rows",
-    )(part)
+    )(part, in_hbm(done))
+
+
+def final_call(share, scale, shapes):
+    return pl.pallas_call(
+        functools.partial(final_kernel, scale),
+        out_shape=[jax.ShapeDtypeStruct(shape, f32) for shape in shapes],
+        compiler_params=params(ROOM),
+        name="sum_columns",
+    )(share)
+
+
+def shards(pair_rep, true_bins, w_in, w_out, w_head):
+    row_count, col_count, channels = pair_rep.shape
+    n_row = lax.axis_size("row")
+    n_col = lax.axis_size("col")
+    hidden_count = w_in.shape[1]
+    bins_count = w_head.shape[1]
+    w_head_t = w_head.T
+
+    send = forward_call(pair_rep, w_in, w_out, w_head_t, n_row, n_col)
+    recv = lax.all_to_all(
+        send.reshape(n_row * n_col, CYCLES, channels),
+        ("row", "col"),
+        split_axis=0,
+        concat_axis=0,
+        tiled=True,
+    ).reshape(n_row, CYCLES * n_col, channels)
+    hidden, normed_t, residual_t, x_hat, inv_std, logits, bins_wide = prepare_call(
+        pair_rep, true_bins, w_in, w_out, w_head_t, n_row, n_col
+    )
+    d_logit, part = weights_call(
+        recv, hidden, normed_t, residual_t, logits, bins_wide, w_out, w_head_t
+    )
+    part = lax.all_to_all(part, "row", split_axis=0, concat_axis=0, tiled=True)
+    d_pair = pair_call(
+        d_logit, hidden, x_hat, inv_std, w_in, w_out, w_head_t, pair_rep.shape, n_row, n_col
+    )
+    share = middle_call(part, d_pair, n_col)
     share = lax.all_to_all(
         share.reshape(n_col, 4, channels), "col", split_axis=0, concat_axis=0, tiled=True
     ).reshape(4 * n_col, channels)
-    grad_in, grad_out_t, grad_head_t = pl.pallas_call(
-        functools.partial(final_kernel, 1.0 / (row_count * n_row)),
-        out_shape=[
-            jax.ShapeDtypeStruct((channels // n_row, hidden_count // n_col), f32),
-            jax.ShapeDtypeStruct((channels // n_col, hidden_count // n_row), f32),
-            jax.ShapeDtypeStruct((bins_count // n_col, channels // n_row), f32),
-        ],
-        compiler_params=params(),
-        name="sum_columns",
-    )(share)
+    grad_in, grad_out_t, grad_head_t = final_call(
+        share,
+        1.0 / (row_count * n_row),
+        [
+            (channels // n_row, hidden_count // n_col),
+            (channels // n_col, hidden_count // n_row),
+            (bins_count // n_col, channels // n_row),
+        ],
+    )
     return (
         d_pair.reshape(row_count, col_count, channels),
         grad_in,

time: 89.3 us -> 81.8 us (0.916)
  Pallas kernels: 26.8 us -> 19.9 us
  starting transfers between devices: 30.3 us -> 25.9 us
  waiting for transfers between devices: 12.6 us -> 17 us
    pallas_call x6, Pallas kernels: 26.8 us -> 19.9 us  [the longest x1 5.22 us: prepare_call(): pl.pallas_call(prepare_kernel, grid=(STEPS,), in_specs=[pl.BlockSpec((CYC...]
    all_to_all x1, starting transfers between devices: 8.09 us -> 3.74 us  [shards(): part = lax.all_to_all(part, 'row', split_axis=0, concat_axis=0, tiled=True)]
    all_to_all x1, waiting for transfers between devices: 2.58 us -> 6.38 us  [shards(): part = lax.all_to_all(part, 'row', split_axis=0, concat_axis=0, tiled=True)]
    unnamed x5 -> x3, local copies, waits for them, and re-layouts: 2.74 us -> 2.11 us
  transfers between devices with their start and end apart: 2 -> 2, of which waited for: 2 -> 2; matrix products, arithmetic and copies ran while one was open for 2% -> 2% of each run, Pallas kernels for 13% -> 12%
where the time goes in v4:
time: 81.8 us; the launch traced here: 81.5 us
  starting transfers between devices  25.9 us (32%)
  Pallas kernels  19.9 us (24%)
  waiting for transfers between devices  17 us (21%)
  blocking collectives  15.9 us (19%)
  local copies, waits for them, and re-layouts  2.11 us (3%)
    all_to_all x1, starting transfers between devices, shards(): lax.all_to_all(send.reshape(n_row * n_col, CYCLES, channels), ('row', 'co...  22.2 us
    all_to_all x1, blocking collectives, shards(): lax.all_to_all(share.reshape(n_col, 4, channels), 'col', split_axis=0, co...  15.9 us
    all_to_all x1, waiting for transfers between devices, shards(): lax.all_to_all(send.reshape(n_row * n_col, CYCLES, channels), ('row', 'co...  10.7 us
    all_to_all x1, waiting for transfers between devices, shards(): part = lax.all_to_all(part, 'row', split_axis=0, concat_axis=0, tiled=True)  6.38 us
    pallas_call x1, Pallas kernels, prepare_call(): pl.pallas_call(prepare_kernel, grid=(STEPS,), in_specs=[pl.BlockSpec((CYC...  5.22 us
    pallas_call x1, Pallas kernels, weights_call(): pl.pallas_call(weights_kernel, grid=(STEPS,), in_specs=[pl.BlockSpec((n_r...  4.97 us
    pallas_call x1, Pallas kernels, pair_call(): pl.pallas_call(pair_kernel, grid=(STEPS,), in_specs=[rows_spec(block // C...  4.74 us
    pallas_call x1, Pallas kernels, forward_call(): pl.pallas_call(send_kernel, grid=(FORWARD_STEPS,), in_specs=[pl.BlockSpec...  4.06 us
  transfers between devices with their start and end apart: 2, of which 2 were waited for; matrix products, arithmetic and copies ran while one was open for 2% of the time, Pallas kernels for 12%

profile of v4, /device:TPU:1, one launch (start us, length us, event | category | flops | bytes accessed | tf_op | source)
XLA Modules:
  0.0 81.5 jit_solution(4730653708608505530)
XLA Ops:
  0.6 4.1 %forward.1 = s16[16,64,128]{2,1,0:T(8,128)(2,1)} custom-call(bf16[2,32,32,128]{3,2,1,0:T(8,128)(2,1)} %bitcast.15, bf16[128,512]{1,0:T(8,128)(2,1)} %w_in_ref.5, bf16[512,128]{1,0:T(8,128)(2,1)} %w_out_ref.7, bf16[64,128]{1,0:T(8,128)(2,1)} %bitcast.17), custom_call_target="tpu_custom_call" | custom-call | tf_op jit(solution)/shard_map/forward/pallas_call | solution.py:321
  4.7 22.2 %all-to-all-start = ((s16[512,2,128]{2,1,0:T(2,128)(2,1)}), s16[512,2,128]{2,1,0:T(2,128)(2,1)S(1)}, u32[]{:S(2)}, u32[]{:S(2)}) async-start(s16[512,2,128]{2,1,0:T(2,128)(2,1)} %bitcast.14), calls=%async_computation | async-start | bytes 524288 | tf_op jit(solution)/shard_map/all_to_all | solution.py:492
  26.9 1.4 %copy.9 = s32[64,32]{1,0:T(8,128)} copy(s32[64,32]{0,1:T(8,128)} %param.6) | data formatting | bytes 16384 | tf_op args[1]
  28.3 5.2 %prepare.1 = (bf16[2048,512]{1,0:T(8,128)(2,1)}, bf16[128,2048]{1,0:T(8,128)(2,1)}, bf16[128,2048]{1,0:T(8,128)(2,1)}, f32[2048,128]{1,0:T(8,128)}, f32[2048,128...) custom-call(bf16[2,32,32,128]{3,2,1,0:T(8,128)(2,1)} %bitcast.16, s32[2,32,32]{2,1,0:T(8,128)} %bitcast.21, ...), custom_call_target="tpu_custom_call" | custom-call | flops 536870912 | bytes 8388608 | tf_op jit(solution)/shard_map/prepare/pallas_call | solution.py:353
  33.5 10.7 %all-to-all-done = s16[512,2,128]{2,1,0:T(2,128)(2,1)S(1)} async-done(((s16[512,2,128]{2,1,0:T(2,128)(2,1)}), s16[512,2,128]{2,1,0:T(2,128)(2,1)S(1)}, u32[]{:S(2)}, u32[]{:S(2)}) %all-to-all-start) | async-done | bytes 262176 | tf_op jit(solution)/shard_map/all_to_all | solution.py:492
  44.1 5.0 %weights.1 = (bf16[1024,128]{1,0:T(8,128)(2,1)S(1)}, bf16[16,80,128]{2,1,0:T(8,128)(2,1)}) custom-call(s16[16,64,128]{2,1,0:T(8,128)(2,1)S(1)} %bitcast.10, bf16[2048,512]{1,0:T(8,128)(2,1)} %get-tuple-element.16.hidden_ref, bf16[128,2048]{1,0:T(8,128)(2,1)} %get-tuple-element.17.normed_t_ref, bf16[128,2048]{1,0:T(8,128)(2,1)} %get-tuple-element.18.residual_t_ref, ...), custom_call_target="tpu_custom_call" | custom-call | tf_op jit(solution)/shard_map/weights/pallas_call | solution.py:404
  49.1 0.0 copy-start
  49.1 0.7 copy-done
  49.8 3.7 %all-to-all-start.1 = ((bf16[16,80,128]{2,1,0:T(8,128)(2,1)}), bf16[16,80,128]{2,1,0:T(8,128)(2,1)S(1)}, u32[]{:S(2)}, u32[]{:S(2)}) async-start(bf16[16,80,128]{2,1,0:T(8,128)(2,1)} %get-tuple-element.24), calls=%async_computation.1 | async-start | bytes 655360 | tf_op jit(solution)/shard_map/all_to_all | solution.py:505
  53.6 4.7 %pair.1.done_ref = bf16[2,32,32,128]{3,2,1,0:T(8,128)(2,1)} custom-call(bf16[1024,128]{1,0:T(8,128)(2,1)} %copy-done, bf16[2048,512]{1,0:T(8,128)(2,1)} %get-tuple-element.16.hidden_ref, f32[2048,128]{1,0:T(8,128)} %get-tuple-element.22.x_hat_ref, f32[2048,128]{1,0:T(8,128)} %get-tuple-element.23.inv_ref, bf16[128,512]{1,0:T(8,128)(2,1)} %w_in_ref.5, ...), custom_call_target="tpu_custom_call" | custom-call | flops 536870912 | bytes 5242880 | tf_op jit(solution)/shard_map/pair/pallas_call | solution.py:441
  58.3 6.4 %all-to-all-done.1.recv_ref = bf16[16,80,128]{2,1,0:T(8,128)(2,1)S(1)} async-done(((bf16[16,80,128]{2,1,0:T(8,128)(2,1)}), bf16[16,80,128]{2,1,0:T(8,128)(2,1)S(1)}, u32[]{:S(2)}, u32[]{:S(2)}) %all-to-all-start.1) | async-done | bytes 327712 | tf_op jit(solution)/shard_map/all_to_all | solution.py:505
  64.7 0.2 sum_rows.1
  64.9 15.9 %all_to_all.15 = f32[32,4,128]{2,1,0:T(4,128)S(1)} all-to-all(f32[32,4,128]{2,1,0:T(4,128)S(1)} %bitcast.11), channel_id=1, replica_groups=mesh['row'=16,'col'=32] {'col'}, dimensions={0} | all-to-all | bytes 131072 | tf_op jit(solution)/shard_map/all_to_all | solution.py:510
  80.8 0.7 sum_columns.1
Async XLA Ops:
  4.7 39.5 %all-to-all-start = ((s16[512,2,128]{2,1,0:T(2,128)(2,1)}), s16[512,2,128]{2,1,0:T(2,128)(2,1)S(1)}, u32[]{:S(2)}, u32[]{:S(2)}) async-start(s16[512,2,128]{2,1,0:T(2,128)(2,1)} %bitcast.14), calls=%async_computation | async-start | bytes 524288 | tf_op jit(solution)/shard_map/all_to_all | solution.py:492
  49.1 0.7 copy-start
  49.8 14.9 %all-to-all-start.1 = ((bf16[16,80,128]{2,1,0:T(8,128)(2,1)}), bf16[16,80,128]{2,1,0:T(8,128)(2,1)S(1)}, u32[]{:S(2)}, u32[]{:S(2)}) async-start(bf16[16,80,128]{2,1,0:T(8,128)(2,1)} %get-tuple-element.24), calls=%async_computation.1 | async-start | bytes 655360 | tf_op jit(solution)/shard_map/all_to_all | solution.py:505

commit v5 on v4

--- a/solution.py
+++ b/solution.py
@@ -15,8 +15,6 @@
 code_steps = 1850.0
 
 CYCLES = 2
-FORWARD_STEPS = 1
-STEPS = 2
 
 
 def dot(first, second):
@@ -120,39 +118,45 @@
         bins_wide_ref[:, b] = wide.astype(bf16).reshape(count, n_row, channels)
 
 
-def pair_gradient(d_logit, w_head_wide):
-    wide = dot(d_logit, w_head_wide)
-    channels = wide.shape[1] // CYCLES
-    return jnp.concatenate([wide[:, :channels], wide[:, channels:]], axis=0)
-
-
-def hidden_gradient(d_update, hidden, w_out):
-    back = dot_t(d_update, w_out).astype(bf16)
-    return jnp.where(hidden > 0, back, jnp.zeros_like(back))
-
-
-def weights_kernel(
+def backward_kernel(
     recv_ref,
+    logits_ref,
+    bins_wide_ref,
     hidden_ref,
+    x_hat_hbm,
+    inv_hbm,
+    normed_t_hbm,
+    residual_t_hbm,
+    w_in_ref,
+    w_out_ref,
+    w_head_t_ref,
+    grad_hbm,
+    part_ref,
+    x_hat_ref,
+    inv_ref,
     normed_t_ref,
     residual_t_ref,
-    logits_ref,
-    bins_wide_ref,
-    w_out_ref,
-    w_head_t_ref,
-    d_logit_ref,
-    part_ref,
+    grad_ref,
     rows_ref,
-    in_ref,
-    out_ref,
-    head_ref,
+    sems,
 ):
-    step = pl.program_id(0)
-    n_row = recv_ref.shape[0]
-    span = recv_ref.shape[1]
-    channels = logits_ref.shape[-1]
+    n_row, span, channels = recv_ref.shape
+    count = span // CYCLES
     bins_count = channels // CYCLES
     half = span * n_row
+    copies = [
+        pltpu.make_async_copy(source, target, sems.at[i])
+        for i, (source, target) in enumerate(
+            (
+                (x_hat_hbm, x_hat_ref),
+                (inv_hbm, inv_ref),
+                (residual_t_hbm, residual_t_ref),
+                (normed_t_hbm, normed_t_ref),
+            )
+        )
+    ]
+    for copy in copies:
+        copy.start()
 
     for r in range(n_row):
         rows_ref[pl.ds(r, span, stride=n_row), :] = decode(recv_ref[r])
@@ -169,58 +173,16 @@
     bins = bins_wide_ref[...].reshape(half, channels).astype(f32)
     d_sym = probability - jnp.where(bins == own_bin, 1.0, 0.0)
     d_logit = (d_sym + d_sym).astype(bf16)
-    d_logit_ref[...] = d_logit
-
-    d_update = pair_gradient(d_logit, widen(w_head_t_ref[...])).astype(bf16)
+
+    wide = dot(d_logit, widen(w_head_t_ref[...]))
+    d_resid = jnp.concatenate([wide[:, :channels], wide[:, channels:]], axis=0)
+    d_update = d_resid.astype(bf16)
     hidden = hidden_ref[...]
-    d_hidden = hidden_gradient(d_update, hidden, w_out_ref[...])
-    g_in = dot(normed_t_ref[...], d_hidden)
-    g_out = dot(d_update.T, hidden)
-    g_head = jnp.where(
-        left,
-        dot(residual_t_ref[:, :half], d_logit),
-        dot(residual_t_ref[:, half:], d_logit),
-    )
-
-    @pl.when(step == 0)
-    def _():
-        in_ref[...] = g_in
-        out_ref[...] = g_out
-        head_ref[...] = g_head
-
-    @pl.when(step > 0)
-    def _():
-        in_ref[...] += g_in
-        out_ref[...] += g_out
-        head_ref[...] += g_head
-
-    @pl.when(step == pl.num_programs(0) - 1)
-    def _():
-        rows = channels // n_row
-        tiles = in_ref.shape[1] // channels
-        long = tiles * rows
-        total_out = out_ref[...].T
-        for r in range(n_row):
-            mine = in_ref[r * rows : (r + 1) * rows, :]
-            part_ref[r, 0:long, :] = jnp.concatenate(
-                [mine[:, t * channels : (t + 1) * channels] for t in range(tiles)], axis=0
-            ).astype(bf16)
-            part_ref[r, long : 2 * long, :] = total_out[r * long : (r + 1) * long, :].astype(bf16)
-            mine = head_ref[r * rows : (r + 1) * rows, :]
-            part_ref[r, 2 * long : 2 * long + 2 * rows, :] = jnp.concatenate(
-                [mine, jnp.zeros_like(mine)], axis=0
-            ).astype(bf16)
-
-
-def pair_kernel(
-    d_logit_ref, hidden_ref, x_hat_ref, inv_ref, w_in_ref, w_out_ref, w_head_t_ref, grad_ref
-):
-    channels = grad_ref.shape[-1]
-    count = grad_ref.shape[1]
-    n_row = grad_ref.shape[2] // CYCLES
-    d_resid = pair_gradient(d_logit_ref[...], widen(w_head_t_ref[...]))
-    d_hidden = hidden_gradient(d_resid.astype(bf16), hidden_ref[...], w_out_ref[...])
+    back = dot_t(d_update, w_out_ref[...]).astype(bf16)
+    d_hidden = jnp.where(hidden > 0, back, jnp.zeros_like(back))
     d_normed = dot_t(d_hidden, w_in_ref[...])
+    for copy in copies:
+        copy.wait()
     x_hat = x_hat_ref[...]
     first_mean = jnp.mean(d_normed, axis=-1, keepdims=True)
     second_mean = jnp.mean(d_normed * x_hat, axis=-1, keepdims=True)
@@ -229,6 +191,30 @@
     for a in range(CYCLES):
         for b in range(CYCLES):
             grad_ref[b, :, a * n_row : (a + 1) * n_row, :] = d_pair[a, :, b]
+    grad_copy = pltpu.make_async_copy(grad_ref, grad_hbm, sems.at[len(copies)])
+    grad_copy.start()
+
+    g_out = dot(d_update.T, hidden).T
+    g_head = jnp.where(
+        left,
+        dot(residual_t_ref[:, :half], d_logit),
+        dot(residual_t_ref[:, half:], d_logit),
+    )
+    g_in = dot(normed_t_ref[...], d_hidden)
+    rows = channels // n_row
+    tiles = hidden.shape[1] // channels
+    long = tiles * rows
+    for r in range(n_row):
+        mine = g_in[r * rows : (r + 1) * rows, :]
+        part_ref[r, 0:long, :] = jnp.concatenate(
+            [mine[:, t * channels : (t + 1) * channels] for t in range(tiles)], axis=0
+        ).astype(bf16)
+        part_ref[r, long : 2 * long, :] = g_out[r * long : (r + 1) * long, :].astype(bf16)
+        mine = g_head[r * rows : (r + 1) * rows, :]
+        part_ref[r, 2 * long : 2 * long + 2 * rows, :] = jnp.concatenate(
+            [mine, jnp.zeros_like(mine)], axis=0
+        ).astype(bf16)
+    grad_copy.wait()
 
 
 def lanes_of(shape, axis):
@@ -240,7 +226,7 @@
     return (lanes_of(shape, 0) % width == lanes_of(shape, 1) % width).astype(f32).astype(kind)
 
 
-def middle_kernel(recv_ref, done_ref, send_ref, rows_ref):
+def middle_kernel(recv_ref, send_ref, rows_ref):
     n_col = send_ref.shape[0] // 4
     total = recv_ref[0].astype(f32)
     for r in range(1, recv_ref.shape[0]):
@@ -296,15 +282,7 @@
     unfold(total[2:3], head_t_ref)
 
 
-def whole(array):
-    return pl.BlockSpec(array.shape, lambda g: (0,) * array.ndim)
-
-
 ROOM = 48 * 1024 * 1024
-
-
-def whole_array(array):
-    return pl.BlockSpec(array.shape, lambda: (0,) * array.ndim)
 
 
 def params(limit=62 * 1024 * 1024):
@@ -317,58 +295,21 @@
 
 def forward_call(pair_rep, w_in, w_out, w_head_t, n_row, n_col):
     row_count, col_count, channels = pair_rep.shape
-    count = n_col // FORWARD_STEPS
     return pl.pallas_call(
         send_kernel,
-        grid=(FORWARD_STEPS,),
-        in_specs=[
-            pl.BlockSpec((CYCLES, count, col_count, channels), lambda g: (0, g, 0, 0)),
-            whole(w_in),
-            whole(w_out),
-            whole(w_head_t),
-        ],
-        out_specs=pl.BlockSpec((n_row, CYCLES * count, channels), lambda g: (0, g, 0)),
         out_shape=jax.ShapeDtypeStruct((n_row, CYCLES * n_col, channels), jnp.int16),
-        scratch_shapes=[pltpu.VMEM((CYCLES * count * n_row, channels), jnp.int32)],
+        scratch_shapes=[pltpu.VMEM((CYCLES * n_col * n_row, channels), jnp.int32)],
         compiler_params=params(),
         name="forward",
     )(pair_rep.reshape(CYCLES, n_col, col_count, channels), w_in, w_out, w_head_t)
-
-
-def rows_spec(block, width):
-    return pl.BlockSpec((block, width), lambda g: (g, 0))
-
-
-def columns_spec(height, block):
-    return pl.BlockSpec((height, block), lambda g: (0, g))
 
 
 def prepare_call(pair_rep, true_bins, w_in, w_out, w_head_t, n_row, n_col):
     row_count, col_count, channels = pair_rep.shape
     pairs = row_count * col_count
     hidden_count = w_in.shape[1]
-    count = n_col // STEPS
-    block = pairs // STEPS
-    half = block // CYCLES
     return pl.pallas_call(
         prepare_kernel,
-        grid=(STEPS,),
-        in_specs=[
-            pl.BlockSpec((CYCLES, count, col_count, channels), lambda g: (0, g, 0, 0)),
-            pl.BlockSpec((CYCLES, count, col_count), lambda g: (0, g, 0)),
-            whole(w_in),
-            whole(w_out),
-            whole(w_head_t),
-        ],
-        out_specs=[
-            rows_spec(block, hidden_count),
-            columns_spec(channels, block),
-            columns_spec(channels, block),
-            rows_spec(block, channels),
-            rows_spec(block, channels),
-            rows_spec(half, channels),
-            pl.BlockSpec((count, CYCLES, n_row, channels), lambda g: (g, 0, 0, 0)),
-        ],
         out_shape=[
             jax.ShapeDtypeStruct((pairs, hidden_count), bf16),
             jax.ShapeDtypeStruct((channels, pairs), bf16),
@@ -378,97 +319,54 @@
             jax.ShapeDtypeStruct((pairs // CYCLES, channels), f32),
             jax.ShapeDtypeStruct((n_col, CYCLES, n_row, channels), bf16),
         ],
-        scratch_shapes=[pltpu.VMEM((CYCLES, count, CYCLES, n_row, channels), f32)],
-        compiler_params=params(),
+        scratch_shapes=[pltpu.VMEM((CYCLES, n_col, CYCLES, n_row, channels), f32)],
+        compiler_params=params(ROOM),
         cost_estimate=pl.CostEstimate(
             flops=2 * pairs * 2 * channels * hidden_count, bytes_accessed=8 * 2**20, transcendentals=0
         ),
         name="prepare",
     )(
-        pair_rep.reshape(CYCLES, n_col, col_count, channels),
+        in_hbm(pair_rep.reshape(CYCLES, n_col, col_count, channels)),
         true_bins.reshape(CYCLES, n_col, col_count),
-        w_in,
-        w_out,
-        w_head_t,
-    )
-
-
-def weights_call(recv, hidden, normed_t, residual_t, logits, bins_wide, w_out, w_head_t):
+        in_hbm(w_in),
+        in_hbm(w_out),
+        in_hbm(w_head_t),
+    )
+
+
+def backward_call(
+    recv, logits, bins_wide, hidden, x_hat, inv_std, normed_t, residual_t, w_in, w_out, w_head_t
+):
     n_row, span, channels = recv.shape
     pairs, hidden_count = hidden.shape
-    count = span // CYCLES // STEPS
-    block = pairs // STEPS
-    half = block // CYCLES
     part_rows = 2 * (hidden_count // n_row) + 16
-    kept = [in_hbm(x) for x in (hidden, normed_t, residual_t, logits, bins_wide, w_out, w_head_t)]
+    grad = jax.ShapeDtypeStruct((CYCLES, span // CYCLES, CYCLES * n_row, channels), bf16)
+    late = [in_hbm(x) for x in (x_hat, inv_std, normed_t, residual_t)]
+    here = pl.BlockSpec()
+    there = pl.BlockSpec(memory_space=pl.ANY)
     return pl.pallas_call(
-        weights_kernel,
-        grid=(STEPS,),
-        in_specs=[
-            pl.BlockSpec((n_row, CYCLES * count, channels), lambda g: (0, g, 0)),
-            rows_spec(block, hidden_count),
-            columns_spec(channels, block),
-            columns_spec(channels, block),
-            rows_spec(half, channels),
-            pl.BlockSpec((count, CYCLES, n_row, channels), lambda g: (g, 0, 0, 0)),
-            whole(w_out),
-            whole(w_head_t),
-        ],
-        out_specs=[
-            rows_spec(half, channels),
-            pl.BlockSpec((n_row, part_rows, channels), lambda g: (0, 0, 0)),
-        ],
-        out_shape=[
-            jax.ShapeDtypeStruct((pairs // CYCLES, channels), bf16),
-            jax.ShapeDtypeStruct((n_row, part_rows, channels), bf16),
-        ],
-        scratch_shapes=[
-            pltpu.VMEM((half, channels), f32),
-            pltpu.VMEM((channels, hidden_count), f32),
-            pltpu.VMEM((channels, hidden_count), f32),
-            pltpu.VMEM((channels, channels), f32),
+        backward_kernel,
+        in_specs=[here] * 4 + [there] * 4 + [here] * 3,
+        out_specs=[there, here],
+        out_shape=[grad, jax.ShapeDtypeStruct((n_row, part_rows, channels), bf16)],
+        scratch_shapes=[pltpu.VMEM(x.shape, x.dtype) for x in (*late, grad)]
+        + [
+            pltpu.VMEM((pairs // CYCLES, channels), f32),
+            pltpu.SemaphoreType.DMA((len(late) + 1,)),
         ],
         compiler_params=params(ROOM),
-        name="weights",
-    )(recv, *kept)
-
-
-def pair_call(d_logit, hidden, x_hat, inv_std, w_in, w_out, w_head_t, shape, n_row, n_col):
-    row_count, col_count, channels = shape
-    pairs, hidden_count = hidden.shape
-    count = n_col // STEPS
-    block = pairs // STEPS
-    return pl.pallas_call(
-        pair_kernel,
-        grid=(STEPS,),
-        in_specs=[
-            rows_spec(block // CYCLES, channels),
-            rows_spec(block, hidden_count),
-            rows_spec(block, channels),
-            rows_spec(block, channels),
-            whole(w_in),
-            whole(w_out),
-            whole(w_head_t),
-        ],
-        out_specs=pl.BlockSpec((CYCLES, count, col_count, channels), lambda g: (0, g, 0, 0)),
-        out_shape=jax.ShapeDtypeStruct((CYCLES, n_col, col_count, channels), bf16),
-        compiler_params=params(),
-        cost_estimate=pl.CostEstimate(
-            flops=2 * pairs * 2 * channels * hidden_count, bytes_accessed=5 * 2**20, transcendentals=0
-        ),
-        name="pair",
-    )(in_hbm(d_logit), hidden, x_hat, inv_std, w_in, w_out, w_head_t)
-
-
-def middle_call(part, done, n_col):
+        name="backward",
+    )(recv, logits, bins_wide, hidden, *late, w_in, w_out, w_head_t)
+
+
+def middle_call(part, n_col):
     return pl.pallas_call(
         middle_kernel,
-        in_specs=[whole_array(part), pl.BlockSpec(memory_space=pl.ANY)],
         out_shape=jax.ShapeDtypeStruct((4 * n_col, part.shape[-1]), f32),
         scratch_shapes=[pltpu.VMEM((128, 128), f32)],
         compiler_params=params(ROOM),
         name="sum_rows",
-    )(part, in_hbm(done))
+    )(part)
 
 
 def final_call(share, scale, shapes):
@@ -499,14 +397,21 @@
     hidden, normed_t, residual_t, x_hat, inv_std, logits, bins_wide = prepare_call(
         pair_rep, true_bins, w_in, w_out, w_head_t, n_row, n_col
     )
-    d_logit, part = weights_call(
-        recv, hidden, normed_t, residual_t, logits, bins_wide, w_out, w_head_t
+    d_pair, part = backward_call(
+        recv,
+        logits,
+        bins_wide,
+        hidden,
+        x_hat,
+        inv_std,
+        normed_t,
+        residual_t,
+        w_in,
+        w_out,
+        w_head_t,
     )
     part = lax.all_to_all(part, "row", split_axis=0, concat_axis=0, tiled=True)
-    d_pair = pair_call(
-        d_logit, hidden, x_hat, inv_std, w_in, w_out, w_head_t, pair_rep.shape, n_row, n_col
-    )
-    share = middle_call(part, d_pair, n_col)
+    share = middle_call(part, n_col)
     share = lax.all_to_all(
         share.reshape(n_col, 4, channels), "col", split_axis=0, concat_axis=0, tiled=True
     ).reshape(4 * n_col, channels)

time: 81.8 us -> 82.1 us (level)
  blocking collectives: 15.9 us -> 31.5 us
  waiting for transfers between devices: 17 us -> 9.65 us
  Pallas kernels: 19.9 us -> 13.4 us
  starting transfers between devices: 25.9 us -> 22.2 us
  local copies, waits for them, and re-layouts: 2.11 us -> 4.38 us
    all_to_all x0 -> x1, blocking collectives: none -> 16.2 us  [shards(): part = lax.all_to_all(part, 'row', split_axis=0, concat_axis=0, tiled=True)]
    pallas_call x5 -> x4, Pallas kernels: 19.2 us -> 12.7 us  [the longest x1 5.22 us: backward_call(): pl.pallas_call(backward_kernel, in_specs=[here] * 4 + [there] * 4 + [here...]
    all_to_all x1 -> x0, waiting for transfers between devices: 6.38 us -> none  [shards(): part = lax.all_to_all(part, 'row', split_axis=0, concat_axis=0, tiled=True)]
    all_to_all x1 -> x0, starting transfers between devices: 3.74 us -> none  [shards(): part = lax.all_to_all(part, 'row', split_axis=0, concat_axis=0, tiled=True)]
    unnamed x3 -> x15, local copies, waits for them, and re-layouts: 2.11 us -> 4.38 us
    all_to_all x1, waiting for transfers between devices: 10.7 us -> 9.65 us  [shards(): lax.all_to_all(send.reshape(n_row * n_col, CYCLES, channels), ('row', 'co...]
  transfers between devices with their start and end apart: 2 -> 1, of which waited for: 2 -> 1; matrix products, arithmetic and copies ran while one was open for 2% -> 1% of each run, Pallas kernels for 12% -> 4%
where the time goes in v5:
time: 82.1 us; the launch traced here: 81.8 us
  blocking collectives  31.5 us (38%)
  starting transfers between devices  22.2 us (27%)
  Pallas kernels  13.4 us (16%)
  waiting for transfers between devices  9.65 us (12%)
  local copies, waits for them, and re-layouts  4.38 us (5%)
    all_to_all x1, starting transfers between devices, shards(): lax.all_to_all(send.reshape(n_row * n_col, CYCLES, channels), ('row', 'co...  22.2 us
    all_to_all x1, blocking collectives, shards(): part = lax.all_to_all(part, 'row', split_axis=0, concat_axis=0, tiled=True)  16.2 us
    all_to_all x1, blocking collectives, shards(): lax.all_to_all(share.reshape(n_col, 4, channels), 'col', split_axis=0, co...  15.4 us
    all_to_all x1, waiting for transfers between devices, shards(): lax.all_to_all(send.reshape(n_row * n_col, CYCLES, channels), ('row', 'co...  9.65 us
    pallas_call x1, Pallas kernels, backward_call(): pl.pallas_call(backward_kernel, in_specs=[here] * 4 + [there] * 4 + [here...  5.22 us
    unnamed x15, local copies, waits for them, and re-layouts  4.38 us
    pallas_call x1, Pallas kernels, forward_call(): pl.pallas_call(send_kernel, out_shape=jax.ShapeDtypeStruct((n_row, CYCLES...  4.1 us
    pallas_call x1, Pallas kernels, prepare_call(): pl.pallas_call(prepare_kernel, out_shape=[jax.ShapeDtypeStruct((pairs, hi...  3.18 us
  transfers between devices with their start and end apart: 1, of which 1 were waited for; matrix products, arithmetic and copies ran while one was open for 1% of the time, Pallas kernels for 4%

profile of v5, /device:TPU:1, one launch (start us, length us, event | category | flops | bytes accessed | tf_op | source)
XLA Modules:
  0.0 81.8 jit_solution(6471908621399834375)
XLA Ops:
  0.6 0.0 copy-start.5
  0.6 0.0 copy-start.4
  0.7 0.0 copy-start.6
  0.7 4.1 %forward.1 = s16[16,64,128]{2,1,0:T(8,128)(2,1)} custom-call(bf16[2,32,32,128]{3,2,1,0:T(8,128)(2,1)} %bitcast.18, bf16[128,512]{1,0:T(8,128)(2,1)} %w_in_ref.5, bf16[512,128]{1,0:T(8,128)(2,1)} %w_out_ref.5, bf16[64,128]{1,0:T(8,128)(2,1)} %bitcast.13), custom_call_target="tpu_custom_call" | custom-call | tf_op jit(solution)/shard_map/forward/pallas_call | solution.py:298
  4.8 22.2 %all-to-all-start = ((s16[512,2,128]{2,1,0:T(2,128)(2,1)}), s16[512,2,128]{2,1,0:T(2,128)(2,1)S(1)}, u32[]{:S(2)}, u32[]{:S(2)}) async-start(s16[512,2,128]{2,1,0:T(2,128)(2,1)} %bitcast.17), calls=%async_computation | async-start | bytes 524288 | tf_op jit(solution)/shard_map/all_to_all | solution.py:390
  26.9 0.8 copy.9
  27.7 3.2 %prepare.1 = (bf16[2048,512]{1,0:T(8,128)(2,1)S(1)}, bf16[128,2048]{1,0:T(8,128)(2,1)S(1)}, bf16[128,2048]{1,0:T(8,128)(2,1)S(1)}, f32[2048,128]{1,0:T(8,128)S(1...) custom-call(bf16[2,32,32,128]{3,2,1,0:T(8,128)(2,1)} %bitcast.19, ...), custom_call_target="tpu_custom_call" | custom-call | flops 536870912 | bytes 8388608 | tf_op jit(solution)/shard_map/prepare/pallas_call | solution.py:311
  30.9 0.0 copy-start
  30.9 1.0 %copy-done = f32[2048,128]{1,0:T(8,128)} copy-done((f32[2048,128]{1,0:T(8,128)}, f32[2048,128]{1,0:T(8,128)S(1)}, u32[]{:S(2)}) %copy-start) | copy-done | bytes 1048600
  31.9 0.0 copy-start.1
  31.9 1.0 %copy-done.1 = f32[2048,128]{1,0:T(8,128)} copy-done((f32[2048,128]{1,0:T(8,128)}, f32[2048,128]{1,0:T(8,128)S(1)}, u32[]{:S(2)}) %copy-start.1) | copy-done | bytes 1048600
  32.9 0.0 copy-start.2
  32.9 0.8 copy-done.2
  33.7 0.0 copy-start.3
  33.7 0.8 copy-done.3
  34.5 9.6 %all-to-all-done = s16[512,2,128]{2,1,0:T(2,128)(2,1)S(1)} async-done(((s16[512,2,128]{2,1,0:T(2,128)(2,1)}), s16[512,2,128]{2,1,0:T(2,128)(2,1)S(1)}, u32[]{:S(2)}, u32[]{:S(2)}) %all-to-all-start) | async-done | bytes 262176 | tf_op jit(solution)/shard_map/all_to_all | solution.py:390
  44.1 0.0 copy-done.5
  44.1 0.0 copy-done.4
  44.1 0.0 copy-done.6
  44.1 5.2 %backward.1 = (bf16[2,32,32,128]{3,2,1,0:T(8,128)(2,1)}, bf16[16,80,128]{2,1,0:T(8,128)(2,1)S(1)}) custom-call(s16[16,64,128]{2,1,0:T(8,128)(2,1)S(1)} %bitcast.10, f32[1024,128]{1,0:T(8,128)S(1)} %get-tuple-element.16.logits_ref, bf16[32,2,16,128]{3,2,1,0:T(8,128)(2,1)S(1)} %get-tuple-element.17.bins_wide_ref, ...), custom_call_target="tpu_custom_call" | custom-call | tf_op jit(solution)/shard_map/backward/pallas_call | solution.py:347
  49.4 16.2 %all_to_all.15.recv_ref = bf16[16,80,128]{2,1,0:T(8,128)(2,1)S(1)} all-to-all(bf16[16,80,128]{2,1,0:T(8,128)(2,1)S(1)} %get-tuple-element.24), channel_id=1, replica_groups=mesh['row'=16,'col'=32] {'row'}, dimensions={0} | all-to-all | bytes 655360 | tf_op jit(solution)/shard_map/all_to_all | solution.py:413
  65.5 0.2 sum_rows.1
  65.7 15.4 %all_to_all.16 = f32[32,4,128]{2,1,0:T(4,128)S(1)} all-to-all(f32[32,4,128]{2,1,0:T(4,128)S(1)} %bitcast.12), channel_id=1, replica_groups=mesh['row'=16,'col'=32] {'col'}, dimensions={0} | all-to-all | bytes 131072 | tf_op jit(solution)/shard_map/all_to_all | solution.py:415
  81.1 0.7 sum_columns.1
Async XLA Ops:
  0.6 43.5 %copy-start.5 = (bf16[512,128]{1,0:T(8,128)(2,1)S(1)}, bf16[512,128]{1,0:T(8,128)(2,1)}, u32[]{:S(2)}) copy-start(bf16[512,128]{1,0:T(8,128)(2,1)} %w_out_ref.5) | copy-start | bytes 393220
  0.6 43.5 %copy-start.4 = (bf16[128,512]{1,0:T(8,128)(2,1)S(1)}, bf16[128,512]{1,0:T(8,128)(2,1)}, u32[]{:S(2)}) copy-start(bf16[128,512]{1,0:T(8,128)(2,1)} %w_in_ref.5) | copy-start | bytes 393220
  0.7 43.5 %copy-start.6 = (bf16[128,64]{0,1:T(8,128)(2,1)S(1)}, bf16[128,64]{0,1:T(8,128)(2,1)}, u32[]{:S(2)}) copy-start(bf16[128,64]{0,1:T(8,128)(2,1)} %param.9) | copy-start | bytes 49156
  4.8 39.4 %all-to-all-start = ((s16[512,2,128]{2,1,0:T(2,128)(2,1)}), s16[512,2,128]{2,1,0:T(2,128)(2,1)S(1)}, u32[]{:S(2)}, u32[]{:S(2)}) async-start(s16[512,2,128]{2,1,0:T(2,128)(2,1)} %bitcast.17), calls=%async_computation | async-start | bytes 524288 | tf_op jit(solution)/shard_map/all_to_all | solution.py:390
  30.9 1.0 %copy-start = (f32[2048,128]{1,0:T(8,128)}, f32[2048,128]{1,0:T(8,128)S(1)}, u32[]{:S(2)}) copy-start(f32[2048,128]{1,0:T(8,128)S(1)} %get-tuple-element.19.x_hat_hbm) | copy-start | bytes 3145732
  31.9 1.0 %copy-start.1 = (f32[2048,128]{1,0:T(8,128)}, f32[2048,128]{1,0:T(8,128)S(1)}, u32[]{:S(2)}) copy-start(f32[2048,128]{1,0:T(8,128)S(1)} %get-tuple-element.20.inv_hbm) | copy-start | bytes 3145732
  32.9 0.8 copy-start.2
  33.7 0.8 copy-start.3

commit v6 on v5

--- a/solution.py
+++ b/solution.py
@@ -76,14 +76,26 @@
     w_out_ref,
     w_head_t_ref,
     hidden_ref,
+    logits_ref,
+    bins_wide_ref,
+    w_out_t_ref,
+    hidden_hbm,
+    normed_t_hbm,
+    residual_t_hbm,
     normed_t_ref,
     residual_t_ref,
-    x_hat_ref,
-    inv_ref,
-    logits_ref,
-    bins_wide_ref,
     values_ref,
+    sems,
 ):
+    kept = (
+        (hidden_ref, hidden_hbm),
+        (normed_t_ref, normed_t_hbm),
+        (residual_t_ref, residual_t_hbm),
+    )
+    copies = [
+        pltpu.make_async_copy(source, target, sems.at[i])
+        for i, (source, target) in enumerate(kept)
+    ]
     channels = pair_ref.shape[-1]
     n_row = pair_ref.shape[2] // CYCLES
     count = pair_ref.shape[1]
@@ -92,18 +104,19 @@
             values_ref[a, :, b] = pair_ref[b, :, a * n_row : (a + 1) * n_row, :].astype(f32)
     values = values_ref[...].reshape(-1, channels)
     half = values.shape[0] // CYCLES
-    x_hat, inv_std = normalize(values)
+    x_hat, _ = normalize(values)
     normed = x_hat.astype(bf16)
     hidden = jnp.maximum(dot(normed, w_in_ref[...]), 0.0).astype(bf16)
     residual = (values + dot(hidden, w_out_ref[...])).astype(bf16)
     hidden_ref[...] = hidden
+    w_out_t_ref[...] = w_out_ref[...].T
     normed_t_ref[...] = normed.T
     residual_t_ref[...] = residual.T
-    x_hat_ref[...] = x_hat
-    inv_ref[...] = jnp.broadcast_to(inv_std, x_hat.shape)
     logits_ref[...] = dot_t(
         jnp.concatenate([residual[:half], residual[half:]], axis=1), widen(w_head_t_ref[...])
     )
+    for copy in copies:
+        copy.start()
     columns = bins_ref.shape[-1]
     row_of = lax.broadcasted_iota(jnp.int32, (1, n_row, columns), 1)
     column_of = lax.broadcasted_iota(jnp.int32, (1, n_row, columns), 2)
@@ -116,43 +129,33 @@
         picked = jnp.where(own, jnp.broadcast_to(bins[:, None, :], (count, n_row, columns)), 0.0)
         wide = dot(picked.reshape(count * n_row, columns).astype(bf16), spread)
         bins_wide_ref[:, b] = wide.astype(bf16).reshape(count, n_row, channels)
-
-
-def backward_kernel(
+    for copy in copies:
+        copy.wait()
+
+
+def weights_kernel(
     recv_ref,
     logits_ref,
     bins_wide_ref,
     hidden_ref,
-    x_hat_hbm,
-    inv_hbm,
+    w_out_t_ref,
     normed_t_hbm,
     residual_t_hbm,
-    w_in_ref,
-    w_out_ref,
     w_head_t_ref,
-    grad_hbm,
+    d_logit_ref,
     part_ref,
-    x_hat_ref,
-    inv_ref,
     normed_t_ref,
     residual_t_ref,
-    grad_ref,
     rows_ref,
     sems,
 ):
     n_row, span, channels = recv_ref.shape
-    count = span // CYCLES
     bins_count = channels // CYCLES
     half = span * n_row
     copies = [
         pltpu.make_async_copy(source, target, sems.at[i])
         for i, (source, target) in enumerate(
-            (
-                (x_hat_hbm, x_hat_ref),
-                (inv_hbm, inv_ref),
-                (residual_t_hbm, residual_t_ref),
-                (normed_t_hbm, normed_t_ref),
-            )
+            ((normed_t_hbm, normed_t_ref), (residual_t_hbm, residual_t_ref))
         )
     ]
     for copy in copies:
@@ -173,28 +176,17 @@
     bins = bins_wide_ref[...].reshape(half, channels).astype(f32)
     d_sym = probability - jnp.where(bins == own_bin, 1.0, 0.0)
     d_logit = (d_sym + d_sym).astype(bf16)
-
-    wide = dot(d_logit, widen(w_head_t_ref[...]))
-    d_resid = jnp.concatenate([wide[:, :channels], wide[:, channels:]], axis=0)
-    d_update = d_resid.astype(bf16)
+    d_logit_ref[...] = d_logit
+
+    d_update = pair_gradient(d_logit, w_head_t_ref[...]).astype(bf16)
     hidden = hidden_ref[...]
-    back = dot_t(d_update, w_out_ref[...]).astype(bf16)
-    d_hidden = jnp.where(hidden > 0, back, jnp.zeros_like(back))
-    d_normed = dot_t(d_hidden, w_in_ref[...])
+    d_hidden = hidden_gradient(dot(d_update, w_out_t_ref[...]), hidden)
+    d_logit_t = d_logit.T
+    g_mid = (
+        dot(d_logit_t, hidden[:half])[:bins_count] + dot(d_logit_t, hidden[half:])[bins_count:]
+    )
     for copy in copies:
         copy.wait()
-    x_hat = x_hat_ref[...]
-    first_mean = jnp.mean(d_normed, axis=-1, keepdims=True)
-    second_mean = jnp.mean(d_normed * x_hat, axis=-1, keepdims=True)
-    d_pair = d_resid + inv_ref[...] * (d_normed - first_mean - x_hat * second_mean)
-    d_pair = d_pair.astype(bf16).reshape(CYCLES, count, CYCLES, n_row, channels)
-    for a in range(CYCLES):
-        for b in range(CYCLES):
-            grad_ref[b, :, a * n_row : (a + 1) * n_row, :] = d_pair[a, :, b]
-    grad_copy = pltpu.make_async_copy(grad_ref, grad_hbm, sems.at[len(copies)])
-    grad_copy.start()
-
-    g_out = dot(d_update.T, hidden).T
     g_head = jnp.where(
         left,
         dot(residual_t_ref[:, :half], d_logit),
@@ -204,17 +196,52 @@
     rows = channels // n_row
     tiles = hidden.shape[1] // channels
     long = tiles * rows
+    paired = jnp.concatenate([g_mid, jnp.roll(g_mid, -long // 2, axis=1)], axis=0).T
     for r in range(n_row):
         mine = g_in[r * rows : (r + 1) * rows, :]
         part_ref[r, 0:long, :] = jnp.concatenate(
             [mine[:, t * channels : (t + 1) * channels] for t in range(tiles)], axis=0
         ).astype(bf16)
-        part_ref[r, long : 2 * long, :] = g_out[r * long : (r + 1) * long, :].astype(bf16)
+        part_ref[r, long : long + long // 2, :] = paired[
+            r * long : r * long + long // 2, :
+        ].astype(bf16)
         mine = g_head[r * rows : (r + 1) * rows, :]
-        part_ref[r, 2 * long : 2 * long + 2 * rows, :] = jnp.concatenate(
+        part_ref[r, long + long // 2 :, :] = jnp.concatenate(
             [mine, jnp.zeros_like(mine)], axis=0
         ).astype(bf16)
-    grad_copy.wait()
+
+
+def pair_gradient(d_logit, w_head_t):
+    wide = dot(d_logit, widen(w_head_t))
+    channels = wide.shape[1] // CYCLES
+    return jnp.concatenate([wide[:, :channels], wide[:, channels:]], axis=0)
+
+
+def hidden_gradient(back, hidden):
+    back = back.astype(bf16)
+    return jnp.where(hidden > 0, back, jnp.zeros_like(back))
+
+
+def pair_kernel(
+    d_logit_ref, hidden_ref, pair_ref, w_in_ref, w_out_ref, w_head_t_ref, grad_ref, values_ref
+):
+    channels = grad_ref.shape[-1]
+    count = grad_ref.shape[1]
+    n_row = grad_ref.shape[2] // CYCLES
+    d_resid = pair_gradient(d_logit_ref[...], w_head_t_ref[...])
+    d_hidden = hidden_gradient(dot_t(d_resid.astype(bf16), w_out_ref[...]), hidden_ref[...])
+    d_normed = dot_t(d_hidden, w_in_ref[...])
+    for a in range(CYCLES):
+        for b in range(CYCLES):
+            values_ref[a, :, b] = pair_ref[b, :, a * n_row : (a + 1) * n_row, :].astype(f32)
+    x_hat, inv_std = normalize(values_ref[...].reshape(-1, channels))
+    first_mean = jnp.mean(d_normed, axis=-1, keepdims=True)
+    second_mean = jnp.mean(d_normed * x_hat, axis=-1, keepdims=True)
+    d_pair = d_resid + inv_std * (d_normed - first_mean - x_hat * second_mean)
+    d_pair = d_pair.astype(bf16).reshape(CYCLES, count, CYCLES, n_row, channels)
+    for a in range(CYCLES):
+        for b in range(CYCLES):
+            grad_ref[b, :, a * n_row : (a + 1) * n_row, :] = d_pair[a, :, b]
 
 
 def lanes_of(shape, axis):
@@ -226,7 +253,7 @@
     return (lanes_of(shape, 0) % width == lanes_of(shape, 1) % width).astype(f32).astype(kind)
 
 
-def middle_kernel(recv_ref, send_ref, rows_ref):
+def middle_kernel(recv_ref, w_head_t_ref, send_ref, rows_ref):
     n_col = send_ref.shape[0] // 4
     total = recv_ref[0].astype(f32)
     for r in range(1, recv_ref.shape[0]):
@@ -240,15 +267,22 @@
     slot = lanes_of((1, rows, 1, 128), 3) // 16 == (8 - lanes_of((1, rows, 1, 128), 1)) % 8
     part_in = jnp.sum(jnp.where(slot, folded, 0.0), axis=1).reshape(n_col, 128)
     send_ref[pl.ds(0, n_col, stride=4), :] = part_in
-    rows_ref[...] = jnp.concatenate([total[32:64]] * 4, axis=0).T
     lane = lanes_of((1, 128), 1)
+    mid = total[32:48]
+    mid = jnp.concatenate([jnp.where(lane < 64, mid, 0.0), jnp.where(lane < 64, 0.0, mid)], axis=0)
+    w_head_t = w_head_t_ref[...]
+    twice = jnp.concatenate([w_head_t, w_head_t], axis=0)
+    high = mid.astype(bf16)
+    low = (mid - high.astype(f32)).astype(bf16)
+    mine = dot(high, twice) + dot(low, twice)
+    rows_ref[...] = jnp.concatenate([mine] * 4, axis=0).T
     part_out = rows_ref[pl.ds(0, n_col, stride=4), :]
     for j in range(1, 4):
         part_out = jnp.where(
             lane // 32 == 4 - j, rows_ref[pl.ds(j, n_col, stride=4), :], part_out
         )
     send_ref[pl.ds(1, n_col, stride=4), :] = part_out
-    mine = total[64:72]
+    mine = total[48:56]
     mine = mine + pltpu.roll(mine, 64, 1)
     rows_ref[...] = jnp.concatenate([mine] * 16, axis=0).T
     part_head = jnp.where(
@@ -304,22 +338,35 @@
     )(pair_rep.reshape(CYCLES, n_col, col_count, channels), w_in, w_out, w_head_t)
 
 
+HERE = pl.BlockSpec()
+THERE = pl.BlockSpec(memory_space=pl.ANY)
+
+
 def prepare_call(pair_rep, true_bins, w_in, w_out, w_head_t, n_row, n_col):
     row_count, col_count, channels = pair_rep.shape
     pairs = row_count * col_count
     hidden_count = w_in.shape[1]
-    return pl.pallas_call(
+    away = [
+        jax.ShapeDtypeStruct((pairs, hidden_count), bf16),
+        jax.ShapeDtypeStruct((channels, pairs), bf16),
+        jax.ShapeDtypeStruct((channels, pairs), bf16),
+    ]
+    results = pl.pallas_call(
         prepare_kernel,
+        in_specs=[HERE] * 5,
+        out_specs=[HERE] * 4 + [pl.BlockSpec(memory_space=pltpu.HBM)] * 3,
         out_shape=[
             jax.ShapeDtypeStruct((pairs, hidden_count), bf16),
-            jax.ShapeDtypeStruct((channels, pairs), bf16),
-            jax.ShapeDtypeStruct((channels, pairs), bf16),
-            jax.ShapeDtypeStruct((pairs, channels), f32),
-            jax.ShapeDtypeStruct((pairs, channels), f32),
             jax.ShapeDtypeStruct((pairs // CYCLES, channels), f32),
             jax.ShapeDtypeStruct((n_col, CYCLES, n_row, channels), bf16),
+            jax.ShapeDtypeStruct((channels, hidden_count), bf16),
+            *away,
         ],
-        scratch_shapes=[pltpu.VMEM((CYCLES, n_col, CYCLES, n_row, channels), f32)],
+        scratch_shapes=[pltpu.VMEM(x.shape, x.dtype) for x in away[1:]]
+        + [
+            pltpu.VMEM((CYCLES, n_col, CYCLES, n_row, channels), f32),
+            pltpu.SemaphoreType.DMA((len(away),)),
+        ],
         compiler_params=params(ROOM),
         cost_estimate=pl.CostEstimate(
             flops=2 * pairs * 2 * channels * hidden_count, bytes_accessed=8 * 2**20, transcendentals=0
@@ -332,41 +379,56 @@
         in_hbm(w_out),
         in_hbm(w_head_t),
     )
-
-
-def backward_call(
-    recv, logits, bins_wide, hidden, x_hat, inv_std, normed_t, residual_t, w_in, w_out, w_head_t
-):
+    return results[:4], [in_hbm(x) for x in results[4:]]
+
+
+def weights_call(recv, near, normed_t, residual_t, w_head_t):
+    logits, bins_wide, hidden, w_out_t = near
     n_row, span, channels = recv.shape
     pairs, hidden_count = hidden.shape
-    part_rows = 2 * (hidden_count // n_row) + 16
-    grad = jax.ShapeDtypeStruct((CYCLES, span // CYCLES, CYCLES * n_row, channels), bf16)
-    late = [in_hbm(x) for x in (x_hat, inv_std, normed_t, residual_t)]
-    here = pl.BlockSpec()
-    there = pl.BlockSpec(memory_space=pl.ANY)
+    part_rows = 2 * (hidden_count // n_row)
+    d_logit = jax.ShapeDtypeStruct((pairs // CYCLES, channels), bf16)
+    late = (normed_t, residual_t)
     return pl.pallas_call(
-        backward_kernel,
-        in_specs=[here] * 4 + [there] * 4 + [here] * 3,
-        out_specs=[there, here],
-        out_shape=[grad, jax.ShapeDtypeStruct((n_row, part_rows, channels), bf16)],
-        scratch_shapes=[pltpu.VMEM(x.shape, x.dtype) for x in (*late, grad)]
+        weights_kernel,
+        in_specs=[HERE] * 5 + [THERE] * 2 + [HERE],
+        out_specs=[HERE, HERE],
+        out_shape=[d_logit, jax.ShapeDtypeStruct((n_row, part_rows, channels), bf16)],
+        scratch_shapes=[pltpu.VMEM(x.shape, x.dtype) for x in late]
         + [
             pltpu.VMEM((pairs // CYCLES, channels), f32),
-            pltpu.SemaphoreType.DMA((len(late) + 1,)),
+            pltpu.SemaphoreType.DMA((len(late),)),
         ],
         compiler_params=params(ROOM),
-        name="backward",
-    )(recv, logits, bins_wide, hidden, *late, w_in, w_out, w_head_t)
-
-
-def middle_call(part, n_col):
+        name="weights",
+    )(recv, logits, bins_wide, hidden, w_out_t, normed_t, residual_t, w_head_t)
+
+
+def pair_call(d_logit, hidden, pair_rep, w_in, w_out, w_head_t, n_row, n_col):
+    row_count, col_count, channels = pair_rep.shape
+    pairs, hidden_count = hidden.shape
+    cycled = pair_rep.reshape(CYCLES, n_col, col_count, channels)
+    return pl.pallas_call(
+        pair_kernel,
+        out_shape=jax.ShapeDtypeStruct(cycled.shape, bf16),
+        scratch_shapes=[pltpu.VMEM((CYCLES, n_col, CYCLES, n_row, channels), f32)],
+        compiler_params=params(ROOM),
+        cost_estimate=pl.CostEstimate(
+            flops=2 * pairs * 2 * channels * hidden_count, bytes_accessed=5 * 2**20, transcendentals=0
+        ),
+        name="pair",
+    )(d_logit, *[in_hbm(x) for x in (hidden, cycled, w_in, w_out, w_head_t)])
+
+
+def middle_call(part, w_head_t, done, n_col):
+    part, _ = lax.optimization_barrier((part, done))
     return pl.pallas_call(
         middle_kernel,
         out_shape=jax.ShapeDtypeStruct((4 * n_col, part.shape[-1]), f32),
         scratch_shapes=[pltpu.VMEM((128, 128), f32)],
         compiler_params=params(ROOM),
         name="sum_rows",
-    )(part)
+    )(part, w_head_t)
 
 
 def final_call(share, scale, shapes):
@@ -394,24 +456,17 @@
         concat_axis=0,
         tiled=True,
     ).reshape(n_row, CYCLES * n_col, channels)
-    hidden, normed_t, residual_t, x_hat, inv_std, logits, bins_wide = prepare_call(
-        pair_rep, true_bins, w_in, w_out, w_head_t, n_row, n_col
-    )
-    d_pair, part = backward_call(
-        recv,
-        logits,
-        bins_wide,
-        hidden,
-        x_hat,
-        inv_std,
-        normed_t,
-        residual_t,
-        w_in,
-        w_out,
-        w_head_t,
+    (hidden, logits, bins_wide, w_out_t), (hidden_far, normed_t, residual_t) = (
+        prepare_call(pair_rep, true_bins, w_in, w_out, w_head_t, n_row, n_col)
+    )
+    d_logit, part = weights_call(
+        recv, (logits, bins_wide, hidden, w_out_t), normed_t, residual_t, w_head_t
     )
     part = lax.all_to_all(part, "row", split_axis=0, concat_axis=0, tiled=True)
-    share = middle_call(part, n_col)
+    d_pair = pair_call(
+        d_logit, hidden_far, pair_rep, w_in, w_out, w_head_t, n_row, n_col
+    )
+    share = middle_call(part, w_head_t, d_pair, n_col)
     share = lax.all_to_all(
         share.reshape(n_col, 4, channels), "col", split_axis=0, concat_axis=0, tiled=True
     ).reshape(4 * n_col, channels)

time: 82.1 us -> 80.2 us (0.977)
  blocking collectives: 31.5 us -> 16.3 us
  waiting for transfers between devices: 9.65 us -> 15.9 us
  starting transfers between devices: 22.2 us -> 26 us
  Pallas kernels: 13.4 us -> 16.5 us
    all_to_all x1 -> x0, blocking collectives: 16.2 us -> none  [shards(): part = lax.all_to_all(part, 'row', split_axis=0, concat_axis=0, tiled=True)]
    all_to_all x0 -> x1, waiting for transfers between devices: none -> 5.94 us  [shards(): part = lax.all_to_all(part, 'row', split_axis=0, concat_axis=0, tiled=True)]
    all_to_all x0 -> x1, starting transfers between devices: none -> 3.84 us  [shards(): part = lax.all_to_all(part, 'row', split_axis=0, concat_axis=0, tiled=True)]
    pallas_call x2 -> x3, Pallas kernels: 8.4 us -> 11.5 us  [the longest x1 4.33 us: pair_call(): pl.pallas_call(pair_kernel, out_shape=jax.ShapeDtypeStruct(cycled.shape,...]
    all_to_all x1, blocking collectives: 15.4 us -> 16.3 us  [shards(): lax.all_to_all(share.reshape(n_col, 4, channels), 'col', split_axis=0, co...]
    unnamed x15 -> x13, local copies, waits for them, and re-layouts: 4.38 us -> 4.41 us
  transfers between devices with their start and end apart: 1 -> 2, of which waited for: 1 -> 2; matrix products, arithmetic and copies ran while one was open for 1% -> 1% of each run, Pallas kernels for 4% -> 10%
where the time goes in v6:
time: 80.2 us; the launch traced here: 79.7 us
  starting transfers between devices  26 us (32%)
  Pallas kernels  16.5 us (21%)
  blocking collectives  16.3 us (20%)
  waiting for transfers between devices  15.9 us (20%)
  local copies, waits for them, and re-layouts  4.41 us (5%)
    all_to_all x1, starting transfers between devices, shards(): lax.all_to_all(send.reshape(n_row * n_col, CYCLES, channels), ('row', 'co...  22.2 us
    all_to_all x1, blocking collectives, shards(): lax.all_to_all(share.reshape(n_col, 4, channels), 'col', split_axis=0, co...  16.3 us
    all_to_all x1, waiting for transfers between devices, shards(): lax.all_to_all(send.reshape(n_row * n_col, CYCLES, channels), ('row', 'co...  9.92 us
    all_to_all x1, waiting for transfers between devices, shards(): part = lax.all_to_all(part, 'row', split_axis=0, concat_axis=0, tiled=True)  5.94 us
    unnamed x13, local copies, waits for them, and re-layouts  4.41 us
    pallas_call x1, Pallas kernels, pair_call(): pl.pallas_call(pair_kernel, out_shape=jax.ShapeDtypeStruct(cycled.shape,...  4.33 us
    pallas_call x1, Pallas kernels, forward_call(): pl.pallas_call(send_kernel, out_shape=jax.ShapeDtypeStruct((n_row, CYCLES...  4.07 us
    all_to_all x1, starting transfers between devices, shards(): part = lax.all_to_all(part, 'row', split_axis=0, concat_axis=0, tiled=True)  3.84 us
  transfers between devices with their start and end apart: 2, of which 2 were waited for; matrix products, arithmetic and copies ran while one was open for 1% of the time, Pallas kernels for 10%

profile of v6, /device:TPU:1, one launch (start us, length us, event | category | flops | bytes accessed | tf_op | source)
XLA Modules:
  0.0 79.7 jit_solution(16116588564849373518)
XLA Ops:
  0.6 0.0 copy-start.3
  0.6 4.1 %forward.1 = s16[16,64,128]{2,1,0:T(8,128)(2,1)} custom-call(bf16[2,32,32,128]{3,2,1,0:T(8,128)(2,1)} %bitcast.19, bf16[128,512]{1,0:T(8,128)(2,1)} %w_in_ref.5, bf16[512,128]{1,0:T(8,128)(2,1)} %w_out_ref.5, bf16[64,128]{1,0:T(8,128)(2,1)} %bitcast.11), custom_call_target="tpu_custom_call" | custom-call | tf_op jit(solution)/shard_map/forward/pallas_call | solution.py:332
  4.7 22.2 %all-to-all-start = ((s16[512,2,128]{2,1,0:T(2,128)(2,1)}), s16[512,2,128]{2,1,0:T(2,128)(2,1)S(1)}, u32[]{:S(2)}, u32[]{:S(2)}) async-start(s16[512,2,128]{2,1,0:T(2,128)(2,1)} %bitcast.22), calls=%async_computation | async-start | bytes 524288 | tf_op jit(solution)/shard_map/all_to_all | solution.py:452
  26.9 0.8 %copy.9 = s32[64,32]{1,0:T(8,128)S(1)} copy(s32[64,32]{0,1:T(8,128)} %param.6) | data formatting | bytes 16384 | tf_op args[1]
  27.7 3.6 %prepare.1 = (bf16[2048,512]{1,0:T(8,128)(2,1)S(1)}, f32[1024,128]{1,0:T(8,128)S(1)}, bf16[32,2,16,128]{3,2,1,0:T(8,128)(2,1)S(1)}, bf16[128,512]{1,0:T(8,128)(2...) custom-call(bf16[2,32,32,128]{3,2,1,0:T(8,128)(2,1)} %bitcast.20, ...), custom_call_target="tpu_custom_call" | custom-call | flops 536870912 | bytes 8388608 | tf_op jit(solution)/shard_map/prepare/pallas_call | solution.py:354
  31.3 0.0 copy-start
  31.3 1.3 %copy-done = bf16[2048,512]{1,0:T(8,128)(2,1)} copy-done((bf16[2048,512]{1,0:T(8,128)(2,1)}, bf16[2048,512]{1,0:T(8,128)(2,1)S(1)}, u32[]{:S(2)}) %copy-start) | copy-done | bytes 2097176
  32.6 0.0 copy-start.1
  32.6 0.8 copy-done.1
  33.4 0.0 copy-start.2
  33.4 0.8 %copy-done.2 = bf16[128,2048]{1,0:T(8,128)(2,1)} copy-done((bf16[128,2048]{1,0:T(8,128)(2,1)}, bf16[128,2048]{1,0:T(8,128)(2,1)S(1)}, u32[]{:S(2)}) %copy-start.2) | copy-done | bytes 524312
  34.2 9.9 %all-to-all-done = s16[512,2,128]{2,1,0:T(2,128)(2,1)S(1)} async-done(((s16[512,2,128]{2,1,0:T(2,128)(2,1)}), s16[512,2,128]{2,1,0:T(2,128)(2,1)S(1)}, u32[]{:S(2)}, u32[]{:S(2)}) %all-to-all-start) | async-done | bytes 262176 | tf_op jit(solution)/shard_map/all_to_all | solution.py:452
  44.2 0.0 copy-done.3
  44.2 3.5 %weights.1 = (bf16[1024,128]{1,0:T(8,128)(2,1)S(1)}, bf16[16,64,128]{2,1,0:T(8,128)(2,1)S(1)}) custom-call(s16[16,64,128]{2,1,0:T(8,128)(2,1)S(1)} %bitcast.10, f32[1024,128]{1,0:T(8,128)S(1)} %get-tuple-element.17.logits_ref, bf16[32,2,16,128]{3,2,1,0:T(8,128)(2,1)S(1)} %get-tuple-element.18.bins_wide_ref, ...), custom_call_target="tpu_custom_call" | custom-call | tf_op jit(solution)/shard_map/weights/pallas_call | solution.py:392
  47.7 0.0 copy-start.5
  47.7 0.7 copy-done.5
  48.4 0.0 copy-start.4
  48.4 3.8 %all-to-all-start.1 = ((bf16[16,64,128]{2,1,0:T(8,128)(2,1)}), bf16[16,64,128]{2,1,0:T(8,128)(2,1)S(1)}, u32[]{:S(2)}, u32[]{:S(2)}) async-start(bf16[16,64,128]{2,1,0:T(8,128)(2,1)} %copy-done.5), calls=%async_computation.1 | async-start | bytes 524288 | tf_op jit(solution)/shard_map/all_to_all | solution.py:465
  52.3 4.3 %pair.1 = bf16[2,32,32,128]{3,2,1,0:T(8,128)(2,1)} custom-call(bf16[1024,128]{1,0:T(8,128)(2,1)S(1)} %get-tuple-element.23.d_logit_ref, bf16[2048,512]{1,0:T(8,128)(2,1)} %copy-done, bf16[2,32,32,128]{3,2,1,0:T(8,128)(2,1)} %bitcast.21, bf16[128,512]{1,0:T(8,128)(2,1)} %w_in_ref.5, bf16[512,128]{1,0:T(8,128)(2,1)} %w_out_ref.5, bf16[64,128]{1,0:T(8,128)(2,1)} %bitcast.13), custom_call_target="tpu_custom_call" | custom-call | flops 536870912 | bytes 5242880 | tf_op jit(solution)/shard_map/pair/pallas_call | solution.py:411
  56.6 5.9 %all-to-all-done.1.recv_ref = bf16[16,64,128]{2,1,0:T(8,128)(2,1)S(1)} async-done(((bf16[16,64,128]{2,1,0:T(8,128)(2,1)}), bf16[16,64,128]{2,1,0:T(8,128)(2,1)S(1)}, u32[]{:S(2)}, u32[]{:S(2)}) %all-to-all-start.1) | async-done | bytes 262176 | tf_op jit(solution)/shard_map/all_to_all | solution.py:465
  62.5 0.0 copy-done.4
  62.5 0.3 sum_rows.1
  62.8 16.3 %all_to_all.15 = f32[32,4,128]{2,1,0:T(4,128)S(1)} all-to-all(f32[32,4,128]{2,1,0:T(4,128)S(1)} %bitcast.17), channel_id=1, replica_groups=mesh['row'=16,'col'=32] {'col'}, dimensions={0} | all-to-all | bytes 131072 | tf_op jit(solution)/shard_map/all_to_all | solution.py:470
  79.0 0.7 sum_columns.1
Async XLA Ops:
  0.6 43.5 %copy-start.3 = (bf16[128,64]{0,1:T(8,128)(2,1)S(1)}, bf16[128,64]{0,1:T(8,128)(2,1)}, u32[]{:S(2)}) copy-start(bf16[128,64]{0,1:T(8,128)(2,1)} %param.9) | copy-start | bytes 49156
  4.7 39.5 %all-to-all-start = ((s16[512,2,128]{2,1,0:T(2,128)(2,1)}), s16[512,2,128]{2,1,0:T(2,128)(2,1)S(1)}, u32[]{:S(2)}, u32[]{:S(2)}) async-start(s16[512,2,128]{2,1,0:T(2,128)(2,1)} %bitcast.22), calls=%async_computation | async-start | bytes 524288 | tf_op jit(solution)/shard_map/all_to_all | solution.py:452
  31.3 1.3 %copy-start = (bf16[2048,512]{1,0:T(8,128)(2,1)}, bf16[2048,512]{1,0:T(8,128)(2,1)S(1)}, u32[]{:S(2)}) copy-start(bf16[2048,512]{1,0:T(8,128)(2,1)S(1)} %get-tuple-element.24.hidden_ref) | copy-start | bytes 6291460
  32.6 0.8 copy-start.1
  33.4 0.8 %copy-start.2 = (bf16[128,2048]{1,0:T(8,128)(2,1)}, bf16[128,2048]{1,0:T(8,128)(2,1)S(1)}, u32[]{:S(2)}) copy-start(bf16[128,2048]{1,0:T(8,128)(2,1)S(1)} %get-tuple-element.22.residual_t_hbm) | copy-start | bytes 1572868
  47.7 0.7 copy-start.5
  48.4 14.1 %copy-start.4 = (bf16[128,64]{0,1:T(8,128)(2,1)S(1)}, bf16[128,64]{0,1:T(8,128)(2,1)}, u32[]{:S(2)}) copy-start(bf16[128,64]{0,1:T(8,128)(2,1)} %param.9) | copy-start | bytes 49156
  48.4 14.1 %all-to-all-start.1 = ((bf16[16,64,128]{2,1,0:T(8,128)(2,1)}), bf16[16,64,128]{2,1,0:T(8,128)(2,1)S(1)}, u32[]{:S(2)}, u32[]{:S(2)}) async-start(bf16[16,64,128]{2,1,0:T(8,128)(2,1)} %copy-done.5), calls=%async_computation.1 | async-start | bytes 524288 | tf_op jit(solution)/shard_map/all_to_all | solution.py:465

commit v7 on v6

--- a/solution.py
+++ b/solution.py
@@ -11,8 +11,7 @@
 f32 = jnp.float32
 bf16 = jnp.bfloat16
 
-code_gain = 16.0
-code_steps = 1850.0
+code_steps = 2350.0
 
 CYCLES = 2
 
@@ -37,13 +36,13 @@
 
 
 def encode(values):
-    size = jnp.log(1.0 + jnp.abs(values) * code_gain) * code_steps + 0.5
+    size = jnp.log(1.0 + jnp.abs(values)) * code_steps + 0.5
     return jnp.where(values < 0.0, -size, size).astype(jnp.int32)
 
 
 def decode(codes):
     codes = codes.astype(f32)
-    size = (jnp.exp(jnp.abs(codes) * (1.0 / code_steps)) - 1.0) * (1.0 / code_gain)
+    size = jnp.exp(jnp.abs(codes) * (1.0 / code_steps)) - 1.0
     return jnp.where(codes < 0.0, -size, size)
 
 
@@ -181,10 +180,6 @@
     d_update = pair_gradient(d_logit, w_head_t_ref[...]).astype(bf16)
     hidden = hidden_ref[...]
     d_hidden = hidden_gradient(dot(d_update, w_out_t_ref[...]), hidden)
-    d_logit_t = d_logit.T
-    g_mid = (
-        dot(d_logit_t, hidden[:half])[:bins_count] + dot(d_logit_t, hidden[half:])[bins_count:]
-    )
     for copy in copies:
         copy.wait()
     g_head = jnp.where(
@@ -193,6 +188,10 @@
         dot(residual_t_ref[:, half:], d_logit),
     )
     g_in = dot(normed_t_ref[...], d_hidden)
+    d_logit_t = d_logit.T
+    g_mid = (
+        dot(d_logit_t, hidden[:half])[:bins_count] + dot(d_logit_t, hidden[half:])[bins_count:]
+    )
     rows = channels // n_row
     tiles = hidden.shape[1] // channels
     long = tiles * rows
@@ -253,8 +252,8 @@
     return (lanes_of(shape, 0) % width == lanes_of(shape, 1) % width).astype(f32).astype(kind)
 
 
-def middle_kernel(recv_ref, w_head_t_ref, send_ref, rows_ref):
-    n_col = send_ref.shape[0] // 4
+def middle_kernel(recv_ref, w_head_t_ref, out_ref, rows_ref, send_ref):
+    n_col = out_ref.shape[0] // 4
     total = recv_ref[0].astype(f32)
     for r in range(1, recv_ref.shape[0]):
         total = total + recv_ref[r].astype(f32)
@@ -292,12 +291,14 @@
     )
     send_ref[pl.ds(2, n_col, stride=4), :] = part_head
     send_ref[pl.ds(3, n_col, stride=4), :] = jnp.zeros_like(part_head)
+    out_ref[...] = send_ref[...].astype(bf16)
 
 
 def final_kernel(scale, recv_ref, in_ref, out_t_ref, head_t_ref):
-    total = recv_ref[0:8, :]
-    for c in range(1, recv_ref.shape[0] // 8):
-        total = total + recv_ref[c * 8 : (c + 1) * 8, :]
+    values = recv_ref[...].astype(f32)
+    total = values[0:8]
+    for c in range(1, values.shape[0] // 8):
+        total = total + values[c * 8 : (c + 1) * 8]
     total = (total[0:4] + total[4:8]) * scale
 
     def unfold(row, out):
@@ -424,8 +425,8 @@
     part, _ = lax.optimization_barrier((part, done))
     return pl.pallas_call(
         middle_kernel,
-        out_shape=jax.ShapeDtypeStruct((4 * n_col, part.shape[-1]), f32),
-        scratch_shapes=[pltpu.VMEM((128, 128), f32)],
+        out_shape=jax.ShapeDtypeStruct((4 * n_col, part.shape[-1]), bf16),
+        scratch_shapes=[pltpu.VMEM((128, 128), f32), pltpu.VMEM((4 * n_col, part.shape[-1]), f32)],
         compiler_params=params(ROOM),
         name="sum_rows",
     )(part, w_head_t)

time: 80.2 us -> 79 us (0.985)
  Pallas kernels: 16.5 us -> 15.5 us
    pallas_call x1, Pallas kernels: 3.54 us -> 2.54 us  [weights_call(): pl.pallas_call(weights_kernel, in_specs=[HERE] * 5 + [THERE] * 2 + [HERE]...]
where the time goes in v7:
time: 79 us; the launch traced here: 78.6 us
  starting transfers between devices  26 us (33%)
  blocking collectives  16.1 us (20%)
  waiting for transfers between devices  15.9 us (20%)
  Pallas kernels  15.5 us (20%)
  local copies, waits for them, and re-layouts  4.41 us (6%)
    all_to_all x1, starting transfers between devices, shards(): lax.all_to_all(send.reshape(n_row * n_col, CYCLES, channels), ('row', 'co...  22.2 us
    all_to_all x1, blocking collectives, shards(): lax.all_to_all(share.reshape(n_col, 4, channels), 'col', split_axis=0, co...  16.1 us
    all_to_all x1, waiting for transfers between devices, shards(): lax.all_to_all(send.reshape(n_row * n_col, CYCLES, channels), ('row', 'co...  9.92 us
    all_to_all x1, waiting for transfers between devices, shards(): part = lax.all_to_all(part, 'row', split_axis=0, concat_axis=0, tiled=True)  5.94 us
    unnamed x13, local copies, waits for them, and re-layouts  4.41 us
    pallas_call x1, Pallas kernels, pair_call(): pl.pallas_call(pair_kernel, out_shape=jax.ShapeDtypeStruct(cycled.shape,...  4.33 us
    pallas_call x1, Pallas kernels, forward_call(): pl.pallas_call(send_kernel, out_shape=jax.ShapeDtypeStruct((n_row, CYCLES...  4.05 us
    all_to_all x1, starting transfers between devices, shards(): part = lax.all_to_all(part, 'row', split_axis=0, concat_axis=0, tiled=True)  3.84 us
  transfers between devices with their start and end apart: 2, of which 2 were waited for; matrix products, arithmetic and copies ran while one was open for 1% of the time, Pallas kernels for 10%

profile of v7, /device:TPU:1, one launch (start us, length us, event | category | flops | bytes accessed | tf_op | source)
XLA Modules:
  0.0 78.6 jit_solution(1089837487753461272)
XLA Ops:
  0.6 0.0 copy-start.3
  0.6 4.0 %forward.1 = s16[16,64,128]{2,1,0:T(8,128)(2,1)} custom-call(bf16[2,32,32,128]{3,2,1,0:T(8,128)(2,1)} %bitcast.19, bf16[128,512]{1,0:T(8,128)(2,1)} %w_in_ref.5, bf16[512,128]{1,0:T(8,128)(2,1)} %w_out_ref.5, bf16[64,128]{1,0:T(8,128)(2,1)} %bitcast.11), custom_call_target="tpu_custom_call" | custom-call | tf_op jit(solution)/shard_map/forward/pallas_call | solution.py:333
  4.7 22.2 %all-to-all-start = ((s16[512,2,128]{2,1,0:T(2,128)(2,1)}), s16[512,2,128]{2,1,0:T(2,128)(2,1)S(1)}, u32[]{:S(2)}, u32[]{:S(2)}) async-start(s16[512,2,128]{2,1,0:T(2,128)(2,1)} %bitcast.22), calls=%async_computation | async-start | bytes 524288 | tf_op jit(solution)/shard_map/all_to_all | solution.py:453
  26.9 0.8 %copy.9 = s32[64,32]{1,0:T(8,128)S(1)} copy(s32[64,32]{0,1:T(8,128)} %param.6) | data formatting | bytes 16384 | tf_op args[1]
  27.7 3.6 %prepare.1 = (bf16[2048,512]{1,0:T(8,128)(2,1)S(1)}, f32[1024,128]{1,0:T(8,128)S(1)}, bf16[32,2,16,128]{3,2,1,0:T(8,128)(2,1)S(1)}, bf16[128,512]{1,0:T(8,128)(2...) custom-call(bf16[2,32,32,128]{3,2,1,0:T(8,128)(2,1)} %bitcast.20, ...), custom_call_target="tpu_custom_call" | custom-call | flops 536870912 | bytes 8388608 | tf_op jit(solution)/shard_map/prepare/pallas_call | solution.py:355
  31.3 0.0 copy-start
  31.3 1.3 %copy-done = bf16[2048,512]{1,0:T(8,128)(2,1)} copy-done((bf16[2048,512]{1,0:T(8,128)(2,1)}, bf16[2048,512]{1,0:T(8,128)(2,1)S(1)}, u32[]{:S(2)}) %copy-start) | copy-done | bytes 2097176
  32.6 0.0 copy-start.1
  32.6 0.8 %copy-done.1 = bf16[128,2048]{1,0:T(8,128)(2,1)} copy-done((bf16[128,2048]{1,0:T(8,128)(2,1)}, bf16[128,2048]{1,0:T(8,128)(2,1)S(1)}, u32[]{:S(2)}) %copy-start.1) | copy-done | bytes 524312
  33.4 0.0 copy-start.2
  33.4 0.8 %copy-done.2 = bf16[128,2048]{1,0:T(8,128)(2,1)} copy-done((bf16[128,2048]{1,0:T(8,128)(2,1)}, bf16[128,2048]{1,0:T(8,128)(2,1)S(1)}, u32[]{:S(2)}) %copy-start.2) | copy-done | bytes 524312
  34.2 9.9 %all-to-all-done = s16[512,2,128]{2,1,0:T(2,128)(2,1)S(1)} async-done(((s16[512,2,128]{2,1,0:T(2,128)(2,1)}), s16[512,2,128]{2,1,0:T(2,128)(2,1)S(1)}, u32[]{:S(2)}, u32[]{:S(2)}) %all-to-all-start) | async-done | bytes 262176 | tf_op jit(solution)/shard_map/all_to_all | solution.py:453
  44.1 0.0 copy-done.3
  44.1 2.5 %weights.1 = (bf16[1024,128]{1,0:T(8,128)(2,1)S(1)}, bf16[16,64,128]{2,1,0:T(8,128)(2,1)S(1)}) custom-call(s16[16,64,128]{2,1,0:T(8,128)(2,1)S(1)} %bitcast.10, f32[1024,128]{1,0:T(8,128)S(1)} %get-tuple-element.17.logits_ref, bf16[32,2,16,128]{3,2,1,0:T(8,128)(2,1)S(1)} %get-tuple-element.18.bins_wide_ref, ...), custom_call_target="tpu_custom_call" | custom-call | tf_op jit(solution)/shard_map/weights/pallas_call | solution.py:393
  46.7 0.0 copy-start.5
  46.7 0.7 copy-done.5
  47.4 0.0 copy-start.4
  47.4 3.8 %all-to-all-start.1 = ((bf16[16,64,128]{2,1,0:T(8,128)(2,1)}), bf16[16,64,128]{2,1,0:T(8,128)(2,1)S(1)}, u32[]{:S(2)}, u32[]{:S(2)}) async-start(bf16[16,64,128]{2,1,0:T(8,128)(2,1)} %copy-done.5), calls=%async_computation.1 | async-start | bytes 524288 | tf_op jit(solution)/shard_map/all_to_all | solution.py:466
  51.2 4.3 %pair.1 = bf16[2,32,32,128]{3,2,1,0:T(8,128)(2,1)} custom-call(bf16[1024,128]{1,0:T(8,128)(2,1)S(1)} %get-tuple-element.23.d_logit_ref, bf16[2048,512]{1,0:T(8,128)(2,1)} %copy-done, bf16[2,32,32,128]{3,2,1,0:T(8,128)(2,1)} %bitcast.21, bf16[128,512]{1,0:T(8,128)(2,1)} %w_in_ref.5, bf16[512,128]{1,0:T(8,128)(2,1)} %w_out_ref.5, bf16[64,128]{1,0:T(8,128)(2,1)} %bitcast.13), custom_call_target="tpu_custom_call" | custom-call | flops 536870912 | bytes 5242880 | tf_op jit(solution)/shard_map/pair/pallas_call | solution.py:412
  55.6 5.9 %all-to-all-done.1.recv_ref = bf16[16,64,128]{2,1,0:T(8,128)(2,1)S(1)} async-done(((bf16[16,64,128]{2,1,0:T(8,128)(2,1)}), bf16[16,64,128]{2,1,0:T(8,128)(2,1)S(1)}, u32[]{:S(2)}, u32[]{:S(2)}) %all-to-all-start.1) | async-done | bytes 262176 | tf_op jit(solution)/shard_map/all_to_all | solution.py:466
  61.5 0.0 copy-done.4
  61.5 0.3 sum_rows.1
  61.8 16.1 %all_to_all.15 = bf16[32,4,128]{2,1,0:T(4,128)(2,1)S(1)} all-to-all(bf16[32,4,128]{2,1,0:T(4,128)(2,1)S(1)} %bitcast.16), channel_id=1, replica_groups=mesh['row'=16,'col'=32] {'col'}, dimensions={0} | all-to-all | bytes 65536 | tf_op jit(solution)/shard_map/all_to_all | solution.py:471
  77.9 0.7 sum_columns.1
Async XLA Ops:
  0.6 43.5 %copy-start.3 = (bf16[128,64]{0,1:T(8,128)(2,1)S(1)}, bf16[128,64]{0,1:T(8,128)(2,1)}, u32[]{:S(2)}) copy-start(bf16[128,64]{0,1:T(8,128)(2,1)} %param.9) | copy-start | bytes 49156
  4.7 39.5 %all-to-all-start = ((s16[512,2,128]{2,1,0:T(2,128)(2,1)}), s16[512,2,128]{2,1,0:T(2,128)(2,1)S(1)}, u32[]{:S(2)}, u32[]{:S(2)}) async-start(s16[512,2,128]{2,1,0:T(2,128)(2,1)} %bitcast.22), calls=%async_computation | async-start | bytes 524288 | tf_op jit(solution)/shard_map/all_to_all | solution.py:453
  31.3 1.3 %copy-start = (bf16[2048,512]{1,0:T(8,128)(2,1)}, bf16[2048,512]{1,0:T(8,128)(2,1)S(1)}, u32[]{:S(2)}) copy-start(bf16[2048,512]{1,0:T(8,128)(2,1)S(1)} %get-tuple-element.24.hidden_ref) | copy-start | bytes 6291460
  32.6 0.8 %copy-start.1 = (bf16[128,2048]{1,0:T(8,128)(2,1)}, bf16[128,2048]{1,0:T(8,128)(2,1)S(1)}, u32[]{:S(2)}) copy-start(bf16[128,2048]{1,0:T(8,128)(2,1)S(1)} %get-tuple-element.21.normed_t_hbm) | copy-start | bytes 1572868
  33.4 0.8 %copy-start.2 = (bf16[128,2048]{1,0:T(8,128)(2,1)}, bf16[128,2048]{1,0:T(8,128)(2,1)S(1)}, u32[]{:S(2)}) copy-start(bf16[128,2048]{1,0:T(8,128)(2,1)S(1)} %get-tuple-element.22.residual_t_hbm) | copy-start | bytes 1572868
  46.7 0.7 copy-start.5
  47.4 14.1 %copy-start.4 = (bf16[128,64]{0,1:T(8,128)(2,1)S(1)}, bf16[128,64]{0,1:T(8,128)(2,1)}, u32[]{:S(2)}) copy-start(bf16[128,64]{0,1:T(8,128)(2,1)} %param.9) | copy-start | bytes 49156
  47.4 14.1 %all-to-all-start.1 = ((bf16[16,64,128]{2,1,0:T(8,128)(2,1)}), bf16[16,64,128]{2,1,0:T(8,128)(2,1)S(1)}, u32[]{:S(2)}, u32[]{:S(2)}) async-start(bf16[16,64,128]{2,1,0:T(8,128)(2,1)} %copy-done.5), calls=%async_computation.1 | async-start | bytes 524288 | tf_op jit(solution)/shard_map/all_to_all | solution.py:466

commit v8 on v7

--- a/solution.py
+++ b/solution.py
@@ -14,6 +14,8 @@
 code_steps = 2350.0
 
 CYCLES = 2
+
+ACROSS = 4
 
 
 def dot(first, second):
@@ -197,15 +199,16 @@
     long = tiles * rows
     paired = jnp.concatenate([g_mid, jnp.roll(g_mid, -long // 2, axis=1)], axis=0).T
     for r in range(n_row):
+        slot = r % ACROSS * (n_row // ACROSS) + r // ACROSS
         mine = g_in[r * rows : (r + 1) * rows, :]
-        part_ref[r, 0:long, :] = jnp.concatenate(
+        part_ref[slot, 0:long, :] = jnp.concatenate(
             [mine[:, t * channels : (t + 1) * channels] for t in range(tiles)], axis=0
         ).astype(bf16)
-        part_ref[r, long : long + long // 2, :] = paired[
+        part_ref[slot, long : long + long // 2, :] = paired[
             r * long : r * long + long // 2, :
         ].astype(bf16)
         mine = g_head[r * rows : (r + 1) * rows, :]
-        part_ref[r, long + long // 2 :, :] = jnp.concatenate(
+        part_ref[slot, long + long // 2 :, :] = jnp.concatenate(
             [mine, jnp.zeros_like(mine)], axis=0
         ).astype(bf16)
 
@@ -253,10 +256,18 @@
 
 
 def middle_kernel(recv_ref, w_head_t_ref, out_ref, rows_ref, send_ref):
-    n_col = out_ref.shape[0] // 4
-    total = recv_ref[0].astype(f32)
-    for r in range(1, recv_ref.shape[0]):
-        total = total + recv_ref[r].astype(f32)
+    n_far = recv_ref.shape[0] // ACROSS
+    for far in range(n_far):
+        total = recv_ref[far].astype(f32)
+        for x in range(1, ACROSS):
+            total = total + recv_ref[x * n_far + far].astype(f32)
+        pack(total, w_head_t_ref[...], rows_ref.at[far], send_ref, far)
+    out_ref[...] = send_ref[...].astype(bf16)
+
+
+def pack(total, w_head_t, rows_ref, send_ref, far):
+    n_col = total.shape[0] // 2
+    base = far * n_col * 4
     rows, tiles = 8, 4
     mine = total[: rows * tiles]
     group = lanes_of((1, rows, 128), 2) // 16 == lanes_of((1, rows, 128), 1)
@@ -265,33 +276,31 @@
     folded = folded.reshape(tiles, rows, rows, 128)
     slot = lanes_of((1, rows, 1, 128), 3) // 16 == (8 - lanes_of((1, rows, 1, 128), 1)) % 8
     part_in = jnp.sum(jnp.where(slot, folded, 0.0), axis=1).reshape(n_col, 128)
-    send_ref[pl.ds(0, n_col, stride=4), :] = part_in
+    send_ref[pl.ds(base + 0, n_col, stride=4), :] = part_in
     lane = lanes_of((1, 128), 1)
     mid = total[32:48]
     mid = jnp.concatenate([jnp.where(lane < 64, mid, 0.0), jnp.where(lane < 64, 0.0, mid)], axis=0)
-    w_head_t = w_head_t_ref[...]
     twice = jnp.concatenate([w_head_t, w_head_t], axis=0)
     high = mid.astype(bf16)
     low = (mid - high.astype(f32)).astype(bf16)
     mine = dot(high, twice) + dot(low, twice)
-    rows_ref[...] = jnp.concatenate([mine] * 4, axis=0).T
-    part_out = rows_ref[pl.ds(0, n_col, stride=4), :]
+    rows_ref[0] = jnp.concatenate([mine] * 4, axis=0).T
+    part_out = rows_ref[0, pl.ds(0, n_col, stride=4), :]
     for j in range(1, 4):
         part_out = jnp.where(
-            lane // 32 == 4 - j, rows_ref[pl.ds(j, n_col, stride=4), :], part_out
+            lane // 32 == 4 - j, rows_ref[0, pl.ds(j, n_col, stride=4), :], part_out
         )
-    send_ref[pl.ds(1, n_col, stride=4), :] = part_out
+    send_ref[pl.ds(base + 1, n_col, stride=4), :] = part_out
     mine = total[48:56]
     mine = mine + pltpu.roll(mine, 64, 1)
-    rows_ref[...] = jnp.concatenate([mine] * 16, axis=0).T
+    rows_ref[1] = jnp.concatenate([mine] * 16, axis=0).T
     part_head = jnp.where(
         lane // 8 == 15,
-        rows_ref[pl.ds(1, n_col, stride=2), :],
-        rows_ref[pl.ds(0, n_col, stride=2), :],
-    )
-    send_ref[pl.ds(2, n_col, stride=4), :] = part_head
-    send_ref[pl.ds(3, n_col, stride=4), :] = jnp.zeros_like(part_head)
-    out_ref[...] = send_ref[...].astype(bf16)
+        rows_ref[1, pl.ds(1, n_col, stride=2), :],
+        rows_ref[1, pl.ds(0, n_col, stride=2), :],
+    )
+    send_ref[pl.ds(base + 2, n_col, stride=4), :] = part_head
+    send_ref[pl.ds(base + 3, n_col, stride=4), :] = jnp.zeros_like(part_head)
 
 
 def final_kernel(scale, recv_ref, in_ref, out_t_ref, head_t_ref):
@@ -421,14 +430,15 @@
     )(d_logit, *[in_hbm(x) for x in (hidden, cycled, w_in, w_out, w_head_t)])
 
 
-def middle_call(part, w_head_t, done, n_col):
-    part, _ = lax.optimization_barrier((part, done))
+def middle_call(part, w_head_t, n_col):
+    n_far = part.shape[0] // ACROSS
+    shape = (n_far * n_col * 4, part.shape[-1])
     return pl.pallas_call(
         middle_kernel,
-        out_shape=jax.ShapeDtypeStruct((4 * n_col, part.shape[-1]), bf16),
-        scratch_shapes=[pltpu.VMEM((128, 128), f32), pltpu.VMEM((4 * n_col, part.shape[-1]), f32)],
+        out_shape=jax.ShapeDtypeStruct(shape, bf16),
+        scratch_shapes=[pltpu.VMEM((n_far, 2, 128, 128), f32), pltpu.VMEM(shape, f32)],
         compiler_params=params(ROOM),
-        name="sum_rows",
+        name="sum_x",
     )(part, w_head_t)
 
 
@@ -437,7 +447,7 @@
         functools.partial(final_kernel, scale),
         out_shape=[jax.ShapeDtypeStruct(shape, f32) for shape in shapes],
         compiler_params=params(ROOM),
-        name="sum_columns",
+        name="sum_rest",
     )(share)
 
 
@@ -463,14 +473,28 @@
     d_logit, part = weights_call(
         recv, (logits, bins_wide, hidden, w_out_t), normed_t, residual_t, w_head_t
     )
-    part = lax.all_to_all(part, "row", split_axis=0, concat_axis=0, tiled=True)
-    d_pair = pair_call(
-        d_logit, hidden_far, pair_rep, w_in, w_out, w_head_t, n_row, n_col
-    )
-    share = middle_call(part, w_head_t, d_pair, n_col)
+    n_far = n_row // ACROSS
+    part = lax.all_to_all(
+        part,
+        "row",
+        split_axis=0,
+        concat_axis=0,
+        tiled=True,
+        axis_index_groups=[[far * ACROSS + x for x in range(ACROSS)] for far in range(n_far)],
+    )
+    share = middle_call(part, w_head_t, n_col)
     share = lax.all_to_all(
-        share.reshape(n_col, 4, channels), "col", split_axis=0, concat_axis=0, tiled=True
-    ).reshape(4 * n_col, channels)
+        share.reshape(n_far * n_col, 4, channels),
+        ("row", "col"),
+        split_axis=0,
+        concat_axis=0,
+        tiled=True,
+        axis_index_groups=[
+            [(far * ACROSS + x) * n_col + c for far in range(n_far) for c in range(n_col)]
+            for x in range(ACROSS)
+        ],
+    ).reshape(n_far * n_col * 4, channels)
+    d_pair = pair_call(d_logit, hidden_far, pair_rep, w_in, w_out, w_head_t, n_row, n_col)
     grad_in, grad_out_t, grad_head_t = final_call(
         share,
         1.0 / (row_count * n_row),

time: 79 us -> 78.4 us (level)
  blocking collectives: 16.1 us -> 8.81 us
  starting transfers between devices: 26 us -> 30.1 us
  waiting for transfers between devices: 15.9 us -> 18.3 us
  Pallas kernels: 15.5 us -> 16.3 us
    all_to_all x1, blocking collectives: 16.1 us -> 8.81 us  [shards(): lax.all_to_all(part, 'row', split_axis=0, concat_axis=0, tiled=True, axis...]
    all_to_all x1, starting transfers between devices: 3.84 us -> 7.97 us  [shards(): lax.all_to_all(share.reshape(n_far * n_col, 4, channels), ('row', 'col'),...]
    all_to_all x1, waiting for transfers between devices: 5.94 us -> 8.43 us  [shards(): lax.all_to_all(share.reshape(n_far * n_col, 4, channels), ('row', 'col'),...]
    unnamed x13 -> x9, local copies, waits for them, and re-layouts: 4.41 us -> 3.73 us
where the time goes in v8:
time: 78.4 us; the launch traced here: 78 us
  starting transfers between devices  30.1 us (38%)
  waiting for transfers between devices  18.3 us (23%)
  Pallas kernels  16.3 us (21%)
  blocking collectives  8.81 us (11%)
  local copies, waits for them, and re-layouts  3.73 us (5%)
    all_to_all x1, starting transfers between devices, shards(): lax.all_to_all(send.reshape(n_row * n_col, CYCLES, channels), ('row', 'co...  22.2 us
    all_to_all x1, waiting for transfers between devices, shards(): lax.all_to_all(send.reshape(n_row * n_col, CYCLES, channels), ('row', 'co...  9.91 us
    all_to_all x1, blocking collectives, shards(): lax.all_to_all(part, 'row', split_axis=0, concat_axis=0, tiled=True, axis...  8.81 us
    all_to_all x1, waiting for transfers between devices, shards(): lax.all_to_all(share.reshape(n_far * n_col, 4, channels), ('row', 'col'),...  8.43 us
    all_to_all x1, starting transfers between devices, shards(): lax.all_to_all(share.reshape(n_far * n_col, 4, channels), ('row', 'col'),...  7.97 us
    pallas_call x1, Pallas kernels, pair_call(): pl.pallas_call(pair_kernel, out_shape=jax.ShapeDtypeStruct(cycled.shape,...  4.32 us
    pallas_call x1, Pallas kernels, forward_call(): pl.pallas_call(send_kernel, out_shape=jax.ShapeDtypeStruct((n_row, CYCLES...  4.04 us
    unnamed x9, local copies, waits for them, and re-layouts  3.73 us
  transfers between devices with their start and end apart: 2, of which 2 were waited for; matrix products, arithmetic and copies ran while one was open for 1% of the time, Pallas kernels for 10%

profile of v8, /device:TPU:1, one launch (start us, length us, event | category | flops | bytes accessed | tf_op | source)
XLA Modules:
  0.0 78.0 jit_solution(6825272488790301931)
XLA Ops:
  0.6 0.0 copy-start.3
  0.6 4.0 %forward.1 = s16[16,64,128]{2,1,0:T(8,128)(2,1)} custom-call(bf16[2,32,32,128]{3,2,1,0:T(8,128)(2,1)} %bitcast.18, bf16[128,512]{1,0:T(8,128)(2,1)} %w_in_ref.5, bf16[512,128]{1,0:T(8,128)(2,1)} %w_out_ref.5, bf16[64,128]{1,0:T(8,128)(2,1)} %bitcast.12), custom_call_target="tpu_custom_call" | custom-call | tf_op jit(solution)/shard_map/forward/pallas_call | solution.py:342
  4.7 22.2 %all-to-all-start = ((s16[512,2,128]{2,1,0:T(2,128)(2,1)}), s16[512,2,128]{2,1,0:T(2,128)(2,1)S(1)}, u32[]{:S(2)}, u32[]{:S(2)}) async-start(s16[512,2,128]{2,1,0:T(2,128)(2,1)} %bitcast.21), calls=%async_computation | async-start | bytes 524288 | tf_op jit(solution)/shard_map/all_to_all | solution.py:463
  26.8 0.8 %copy.9 = s32[64,32]{1,0:T(8,128)S(1)} copy(s32[64,32]{0,1:T(8,128)} %param.6) | data formatting | bytes 16384 | tf_op args[1]
  27.6 3.6 %prepare.1 = (bf16[2048,512]{1,0:T(8,128)(2,1)S(1)}, f32[1024,128]{1,0:T(8,128)S(1)}, bf16[32,2,16,128]{3,2,1,0:T(8,128)(2,1)S(1)}, bf16[128,512]{1,0:T(8,128)(2...) custom-call(bf16[2,32,32,128]{3,2,1,0:T(8,128)(2,1)} %bitcast.19, ...), custom_call_target="tpu_custom_call" | custom-call | flops 536870912 | bytes 8388608 | tf_op jit(solution)/shard_map/prepare/pallas_call | solution.py:364
  31.3 0.0 copy-start
  31.3 1.3 %copy-done = bf16[2048,512]{1,0:T(8,128)(2,1)} copy-done((bf16[2048,512]{1,0:T(8,128)(2,1)}, bf16[2048,512]{1,0:T(8,128)(2,1)S(1)}, u32[]{:S(2)}) %copy-start) | copy-done | bytes 2097176
  32.6 0.0 copy-start.1
  32.6 0.8 %copy-done.1 = bf16[128,2048]{1,0:T(8,128)(2,1)} copy-done((bf16[128,2048]{1,0:T(8,128)(2,1)}, bf16[128,2048]{1,0:T(8,128)(2,1)S(1)}, u32[]{:S(2)}) %copy-start.1) | copy-done | bytes 524312
  33.4 0.0 copy-start.2
  33.4 0.8 %copy-done.2 = bf16[128,2048]{1,0:T(8,128)(2,1)} copy-done((bf16[128,2048]{1,0:T(8,128)(2,1)}, bf16[128,2048]{1,0:T(8,128)(2,1)S(1)}, u32[]{:S(2)}) %copy-start.2) | copy-done | bytes 524312
  34.2 9.9 %all-to-all-done = s16[512,2,128]{2,1,0:T(2,128)(2,1)S(1)} async-done(((s16[512,2,128]{2,1,0:T(2,128)(2,1)}), s16[512,2,128]{2,1,0:T(2,128)(2,1)S(1)}, u32[]{:S(2)}, u32[]{:S(2)}) %all-to-all-start) | async-done | bytes 262176 | tf_op jit(solution)/shard_map/all_to_all | solution.py:463
  44.1 0.0 copy-done.3
  44.1 2.5 %weights.1 = (bf16[1024,128]{1,0:T(8,128)(2,1)S(1)}, bf16[16,64,128]{2,1,0:T(8,128)(2,1)S(1)}) custom-call(s16[16,64,128]{2,1,0:T(8,128)(2,1)S(1)} %bitcast.10, f32[1024,128]{1,0:T(8,128)S(1)} %get-tuple-element.16.logits_ref, bf16[32,2,16,128]{3,2,1,0:T(8,128)(2,1)S(1)} %get-tuple-element.17.bins_wide_ref, ...), custom_call_target="tpu_custom_call" | custom-call | tf_op jit(solution)/shard_map/weights/pallas_call | solution.py:402
  46.7 8.8 %all_to_all.15.recv_ref = bf16[16,64,128]{2,1,0:T(8,128)(2,1)S(1)} all-to-all(bf16[16,64,128]{2,1,0:T(8,128)(2,1)S(1)} %get-tuple-element.24), channel_id=1, replica_groups={{0,32,64,96},{128,160,192,224},{256,288,320,352},{384,416,448,480},{1,3..., dimensions={0} | all-to-all | bytes 524288 | tf_op jit(solution)/shard_map/all_to_all | solution.py:477
  55.5 1.1 %sum_x.1 = bf16[512,128]{1,0:T(8,128)(2,1)} custom-call(bf16[16,64,128]{2,1,0:T(8,128)(2,1)S(1)} %all_to_all.15.recv_ref, bf16[64,128]{1,0:T(8,128)(2,1)S(1)} %bitcast.16), custom_call_target="tpu_custom_call" | custom-call | tf_op jit(solution)/shard_map/sum_x/pallas_call | solution.py:436
  56.5 8.0 %all-to-all-start.2 = ((bf16[128,4,128]{2,1,0:T(4,128)(2,1)}), bf16[128,4,128]{2,1,0:T(4,128)(2,1)S(1)}, u32[]{:S(2)}, u32[]{:S(2)}) async-start(bf16[128,4,128]{2,1,0:T(4,128)(2,1)} %bitcast.6), calls=%async_computation.2 | async-start | bytes 262144 | tf_op jit(solution)/shard_map/all_to_all | solution.py:486
  64.5 4.3 %pair.1 = bf16[2,32,32,128]{3,2,1,0:T(8,128)(2,1)} custom-call(bf16[1024,128]{1,0:T(8,128)(2,1)S(1)} %get-tuple-element.22.d_logit_ref, bf16[2048,512]{1,0:T(8,128)(2,1)} %copy-done, bf16[2,32,32,128]{3,2,1,0:T(8,128)(2,1)} %bitcast.20, bf16[128,512]{1,0:T(8,128)(2,1)} %w_in_ref.5, bf16[512,128]{1,0:T(8,128)(2,1)} %w_out_ref.5, bf16[64,128]{1,0:T(8,128)(2,1)} %bitcast.14), custom_call_target="tpu_custom_call" | custom-call | flops 536870912 | bytes 5242880 | tf_op jit(solution)/shard_map/pair/pallas_call | solution.py:421
  68.8 8.4 %all-to-all-done.2 = bf16[128,4,128]{2,1,0:T(4,128)(2,1)S(1)} async-done(((bf16[128,4,128]{2,1,0:T(4,128)(2,1)}), bf16[128,4,128]{2,1,0:T(4,128)(2,1)S(1)}, u32[]{:S(2)}, u32[]{:S(2)}) %all-to-all-start.2) | async-done | bytes 131104 | tf_op jit(solution)/shard_map/all_to_all | solution.py:486
  77.3 0.7 sum_rest.1
Async XLA Ops:
  0.6 43.5 %copy-start.3 = (bf16[128,64]{0,1:T(8,128)(2,1)S(1)}, bf16[128,64]{0,1:T(8,128)(2,1)}, u32[]{:S(2)}) copy-start(bf16[128,64]{0,1:T(8,128)(2,1)} %param.9) | copy-start | bytes 49156
  4.7 39.4 %all-to-all-start = ((s16[512,2,128]{2,1,0:T(2,128)(2,1)}), s16[512,2,128]{2,1,0:T(2,128)(2,1)S(1)}, u32[]{:S(2)}, u32[]{:S(2)}) async-start(s16[512,2,128]{2,1,0:T(2,128)(2,1)} %bitcast.21), calls=%async_computation | async-start | bytes 524288 | tf_op jit(solution)/shard_map/all_to_all | solution.py:463
  31.3 1.3 %copy-start = (bf16[2048,512]{1,0:T(8,128)(2,1)}, bf16[2048,512]{1,0:T(8,128)(2,1)S(1)}, u32[]{:S(2)}) copy-start(bf16[2048,512]{1,0:T(8,128)(2,1)S(1)} %get-tuple-element.23.hidden_ref) | copy-start | bytes 6291460
  32.6 0.8 %copy-start.1 = (bf16[128,2048]{1,0:T(8,128)(2,1)}, bf16[128,2048]{1,0:T(8,128)(2,1)S(1)}, u32[]{:S(2)}) copy-start(bf16[128,2048]{1,0:T(8,128)(2,1)S(1)} %get-tuple-element.20.normed_t_hbm) | copy-start | bytes 1572868
  33.4 0.8 %copy-start.2 = (bf16[128,2048]{1,0:T(8,128)(2,1)}, bf16[128,2048]{1,0:T(8,128)(2,1)S(1)}, u32[]{:S(2)}) copy-start(bf16[128,2048]{1,0:T(8,128)(2,1)S(1)} %get-tuple-element.21.residual_t_hbm) | copy-start | bytes 1572868
  56.5 20.7 %all-to-all-start.2 = ((bf16[128,4,128]{2,1,0:T(4,128)(2,1)}), bf16[128,4,128]{2,1,0:T(4,128)(2,1)S(1)}, u32[]{:S(2)}, u32[]{:S(2)}) async-start(bf16[128,4,128]{2,1,0:T(4,128)(2,1)} %bitcast.6), calls=%async_computation.2 | async-start | bytes 262144 | tf_op jit(solution)/shard_map/all_to_all | solution.py:486

commit v9 on v8

--- a/solution.py
+++ b/solution.py
@@ -430,7 +430,8 @@
     )(d_logit, *[in_hbm(x) for x in (hidden, cycled, w_in, w_out, w_head_t)])
 
 
-def middle_call(part, w_head_t, n_col):
+def middle_call(part, w_head_t, done, n_col):
+    part, _ = lax.optimization_barrier((part, done))
     n_far = part.shape[0] // ACROSS
     shape = (n_far * n_col * 4, part.shape[-1])
     return pl.pallas_call(
@@ -482,7 +483,8 @@
         tiled=True,
         axis_index_groups=[[far * ACROSS + x for x in range(ACROSS)] for far in range(n_far)],
     )
-    share = middle_call(part, w_head_t, n_col)
+    d_pair = pair_call(d_logit, hidden_far, pair_rep, w_in, w_out, w_head_t, n_row, n_col)
+    share = middle_call(part, w_head_t, d_pair, n_col)
     share = lax.all_to_all(
         share.reshape(n_far * n_col, 4, channels),
         ("row", "col"),
@@ -494,7 +496,6 @@
             for x in range(ACROSS)
         ],
     ).reshape(n_far * n_col * 4, channels)
-    d_pair = pair_call(d_logit, hidden_far, pair_rep, w_in, w_out, w_head_t, n_row, n_col)
     grad_in, grad_out_t, grad_head_t = final_call(
         share,
         1.0 / (row_count * n_row),

time: 78.4 us -> 78.6 us (level)
  blocking collectives: 8.81 us -> 19.4 us
  waiting for transfers between devices: 18.3 us -> 12.3 us
  starting transfers between devices: 30.1 us -> 25.7 us
    all_to_all x1, blocking collectives: 8.81 us -> 19.4 us  [shards(): lax.all_to_all(share.reshape(n_far * n_col, 4, channels), ('row', 'col'),...]
    all_to_all x1, waiting for transfers between devices: 8.43 us -> 2.4 us  [shards(): lax.all_to_all(part, 'row', split_axis=0, concat_axis=0, tiled=True, axis...]
    all_to_all x1, starting transfers between devices: 7.97 us -> 3.54 us  [shards(): lax.all_to_all(part, 'row', split_axis=0, concat_axis=0, tiled=True, axis...]
    unnamed x9 -> x13, local copies, waits for them, and re-layouts: 3.73 us -> 4.41 us
where the time goes in v9:
time: 78.6 us; the launch traced here: 78.2 us
  starting transfers between devices  25.7 us (33%)
  blocking collectives  19.4 us (25%)
  Pallas kernels  15.7 us (20%)
  waiting for transfers between devices  12.3 us (16%)
  local copies, waits for them, and re-layouts  4.41 us (6%)
    all_to_all x1, starting transfers between devices, shards(): lax.all_to_all(send.reshape(n_row * n_col, CYCLES, channels), ('row', 'co...  22.2 us
    all_to_all x1, blocking collectives, shards(): lax.all_to_all(share.reshape(n_far * n_col, 4, channels), ('row', 'col'),...  19.4 us
    all_to_all x1, waiting for transfers between devices, shards(): lax.all_to_all(send.reshape(n_row * n_col, CYCLES, channels), ('row', 'co...  9.92 us
    unnamed x13, local copies, waits for them, and re-layouts  4.41 us
    pallas_call x1, Pallas kernels, pair_call(): pl.pallas_call(pair_kernel, out_shape=jax.ShapeDtypeStruct(cycled.shape,...  4.32 us
    pallas_call x1, Pallas kernels, forward_call(): pl.pallas_call(send_kernel, out_shape=jax.ShapeDtypeStruct((n_row, CYCLES...  4.05 us
    pallas_call x1, Pallas kernels, prepare_call(): pl.pallas_call(prepare_kernel, in_specs=[HERE] * 5, out_specs=[HERE] * 4...  3.63 us
    all_to_all x1, starting transfers between devices, shards(): lax.all_to_all(part, 'row', split_axis=0, concat_axis=0, tiled=True, axis...  3.54 us
  transfers between devices with their start and end apart: 2, of which 2 were waited for; matrix products, arithmetic and copies ran while one was open for 1% of the time, Pallas kernels for 10%

profile of v9, /device:TPU:1, one launch (start us, length us, event | category | flops | bytes accessed | tf_op | source)
XLA Modules:
  0.0 78.2 jit_solution(12499370931140441230)
XLA Ops:
  0.6 0.0 copy-start.3
  0.6 4.0 %forward.1 = s16[16,64,128]{2,1,0:T(8,128)(2,1)} custom-call(bf16[2,32,32,128]{3,2,1,0:T(8,128)(2,1)} %bitcast.19, bf16[128,512]{1,0:T(8,128)(2,1)} %w_in_ref.5, bf16[512,128]{1,0:T(8,128)(2,1)} %w_out_ref.5, bf16[64,128]{1,0:T(8,128)(2,1)} %bitcast.13), custom_call_target="tpu_custom_call" | custom-call | tf_op jit(solution)/shard_map/forward/pallas_call | solution.py:342
  4.7 22.2 %all-to-all-start = ((s16[512,2,128]{2,1,0:T(2,128)(2,1)}), s16[512,2,128]{2,1,0:T(2,128)(2,1)S(1)}, u32[]{:S(2)}, u32[]{:S(2)}) async-start(s16[512,2,128]{2,1,0:T(2,128)(2,1)} %bitcast.22), calls=%async_computation | async-start | bytes 524288 | tf_op jit(solution)/shard_map/all_to_all | solution.py:464
  26.9 0.8 %copy.9 = s32[64,32]{1,0:T(8,128)S(1)} copy(s32[64,32]{0,1:T(8,128)} %param.6) | data formatting | bytes 16384 | tf_op args[1]
  27.7 3.6 %prepare.1 = (bf16[2048,512]{1,0:T(8,128)(2,1)S(1)}, f32[1024,128]{1,0:T(8,128)S(1)}, bf16[32,2,16,128]{3,2,1,0:T(8,128)(2,1)S(1)}, bf16[128,512]{1,0:T(8,128)(2...) custom-call(bf16[2,32,32,128]{3,2,1,0:T(8,128)(2,1)} %bitcast.20, ...), custom_call_target="tpu_custom_call" | custom-call | flops 536870912 | bytes 8388608 | tf_op jit(solution)/shard_map/prepare/pallas_call | solution.py:364
  31.3 0.0 copy-start
  31.3 1.3 %copy-done = bf16[2048,512]{1,0:T(8,128)(2,1)} copy-done((bf16[2048,512]{1,0:T(8,128)(2,1)}, bf16[2048,512]{1,0:T(8,128)(2,1)S(1)}, u32[]{:S(2)}) %copy-start) | copy-done | bytes 2097176
  32.6 0.0 copy-start.1
  32.6 0.8 %copy-done.1 = bf16[128,2048]{1,0:T(8,128)(2,1)} copy-done((bf16[128,2048]{1,0:T(8,128)(2,1)}, bf16[128,2048]{1,0:T(8,128)(2,1)S(1)}, u32[]{:S(2)}) %copy-start.1) | copy-done | bytes 524312
  33.4 0.0 copy-start.2
  33.4 0.8 %copy-done.2 = bf16[128,2048]{1,0:T(8,128)(2,1)} copy-done((bf16[128,2048]{1,0:T(8,128)(2,1)}, bf16[128,2048]{1,0:T(8,128)(2,1)S(1)}, u32[]{:S(2)}) %copy-start.2) | copy-done | bytes 524312
  34.2 9.9 %all-to-all-done = s16[512,2,128]{2,1,0:T(2,128)(2,1)S(1)} async-done(((s16[512,2,128]{2,1,0:T(2,128)(2,1)}), s16[512,2,128]{2,1,0:T(2,128)(2,1)S(1)}, u32[]{:S(2)}, u32[]{:S(2)}) %all-to-all-start) | async-done | bytes 262176 | tf_op jit(solution)/shard_map/all_to_all | solution.py:464
  44.1 0.0 copy-done.3
  44.1 2.5 %weights.1 = (bf16[1024,128]{1,0:T(8,128)(2,1)S(1)}, bf16[16,64,128]{2,1,0:T(8,128)(2,1)S(1)}) custom-call(s16[16,64,128]{2,1,0:T(8,128)(2,1)S(1)} %bitcast.10, f32[1024,128]{1,0:T(8,128)S(1)} %get-tuple-element.17.logits_ref, bf16[32,2,16,128]{3,2,1,0:T(8,128)(2,1)S(1)} %get-tuple-element.18.bins_wide_ref, ...), custom_call_target="tpu_custom_call" | custom-call | tf_op jit(solution)/shard_map/weights/pallas_call | solution.py:402
  46.7 0.0 copy-start.5
  46.7 0.7 copy-done.5
  47.4 0.0 copy-start.4
  47.4 3.5 %all-to-all-start.1 = ((bf16[16,64,128]{2,1,0:T(8,128)(2,1)}), bf16[16,64,128]{2,1,0:T(8,128)(2,1)S(1)}, u32[]{:S(2)}, u32[]{:S(2)}) async-start(bf16[16,64,128]{2,1,0:T(8,128)(2,1)} %copy-done.5), calls=%async_computation.1 | async-start | bytes 524288 | tf_op jit(solution)/shard_map/all_to_all | solution.py:478
  50.9 4.3 %pair.1 = bf16[2,32,32,128]{3,2,1,0:T(8,128)(2,1)} custom-call(bf16[1024,128]{1,0:T(8,128)(2,1)S(1)} %get-tuple-element.23.d_logit_ref, bf16[2048,512]{1,0:T(8,128)(2,1)} %copy-done, bf16[2,32,32,128]{3,2,1,0:T(8,128)(2,1)} %bitcast.21, bf16[128,512]{1,0:T(8,128)(2,1)} %w_in_ref.5, bf16[512,128]{1,0:T(8,128)(2,1)} %w_out_ref.5, bf16[64,128]{1,0:T(8,128)(2,1)} %bitcast.15), custom_call_target="tpu_custom_call" | custom-call | flops 536870912 | bytes 5242880 | tf_op jit(solution)/shard_map/pair/pallas_call | solution.py:421
  55.2 2.4 %all-to-all-done.1.recv_ref = bf16[16,64,128]{2,1,0:T(8,128)(2,1)S(1)} async-done(((bf16[16,64,128]{2,1,0:T(8,128)(2,1)}), bf16[16,64,128]{2,1,0:T(8,128)(2,1)S(1)}, u32[]{:S(2)}, u32[]{:S(2)}) %all-to-all-start.1) | async-done | bytes 262176 | tf_op jit(solution)/shard_map/all_to_all | solution.py:478
  57.6 0.0 copy-done.4
  57.7 0.4 sum_x.1
  58.1 19.4 %all_to_all.15 = bf16[128,4,128]{2,1,0:T(4,128)(2,1)S(1)} all-to-all(bf16[128,4,128]{2,1,0:T(4,128)(2,1)S(1)} %bitcast.11), channel_id=1, replica_groups={{0,1,2,3,4,5,6,7,8,9,10,11,12,13,14,15,16,17,18,19,20,21,22,23,24,25,26..., dimensions={0} | all-to-all | bytes 262144 | tf_op jit(solution)/shard_map/all_to_all | solution.py:488
  77.4 0.7 sum_rest.1
Async XLA Ops:
  0.6 43.5 %copy-start.3 = (bf16[128,64]{0,1:T(8,128)(2,1)S(1)}, bf16[128,64]{0,1:T(8,128)(2,1)}, u32[]{:S(2)}) copy-start(bf16[128,64]{0,1:T(8,128)(2,1)} %param.9) | copy-start | bytes 49156
  4.7 39.5 %all-to-all-start = ((s16[512,2,128]{2,1,0:T(2,128)(2,1)}), s16[512,2,128]{2,1,0:T(2,128)(2,1)S(1)}, u32[]{:S(2)}, u32[]{:S(2)}) async-start(s16[512,2,128]{2,1,0:T(2,128)(2,1)} %bitcast.22), calls=%async_computation | async-start | bytes 524288 | tf_op jit(solution)/shard_map/all_to_all | solution.py:464
  31.3 1.3 %copy-start = (bf16[2048,512]{1,0:T(8,128)(2,1)}, bf16[2048,512]{1,0:T(8,128)(2,1)S(1)}, u32[]{:S(2)}) copy-start(bf16[2048,512]{1,0:T(8,128)(2,1)S(1)} %get-tuple-element.24.hidden_ref) | copy-start | bytes 6291460
  32.6 0.8 %copy-start.1 = (bf16[128,2048]{1,0:T(8,128)(2,1)}, bf16[128,2048]{1,0:T(8,128)(2,1)S(1)}, u32[]{:S(2)}) copy-start(bf16[128,2048]{1,0:T(8,128)(2,1)S(1)} %get-tuple-element.21.normed_t_hbm) | copy-start | bytes 1572868
  33.4 0.8 %copy-start.2 = (bf16[128,2048]{1,0:T(8,128)(2,1)}, bf16[128,2048]{1,0:T(8,128)(2,1)S(1)}, u32[]{:S(2)}) copy-start(bf16[128,2048]{1,0:T(8,128)(2,1)S(1)} %get-tuple-element.22.residual_t_hbm) | copy-start | bytes 1572868
  46.7 0.7 copy-start.5
  47.4 10.3 %copy-start.4 = (bf16[128,64]{0,1:T(8,128)(2,1)S(1)}, bf16[128,64]{0,1:T(8,128)(2,1)}, u32[]{:S(2)}) copy-start(bf16[128,64]{0,1:T(8,128)(2,1)} %param.9) | copy-start | bytes 49156
  47.4 10.3 %all-to-all-start.1 = ((bf16[16,64,128]{2,1,0:T(8,128)(2,1)}), bf16[16,64,128]{2,1,0:T(8,128)(2,1)S(1)}, u32[]{:S(2)}, u32[]{:S(2)}) async-start(bf16[16,64,128]{2,1,0:T(8,128)(2,1)} %copy-done.5), calls=%async_computation.1 | async-start | bytes 524288 | tf_op jit(solution)/shard_map/all_to_all | solution.py:478

commit v10 on v9

--- a/solution.py
+++ b/solution.py
@@ -80,7 +80,6 @@
     logits_ref,
     bins_wide_ref,
     w_out_t_ref,
-    hidden_hbm,
     normed_t_hbm,
     residual_t_hbm,
     normed_t_ref,
@@ -89,7 +88,6 @@
     sems,
 ):
     kept = (
-        (hidden_ref, hidden_hbm),
         (normed_t_ref, normed_t_hbm),
         (residual_t_ref, residual_t_hbm),
     )
@@ -357,14 +355,13 @@
     pairs = row_count * col_count
     hidden_count = w_in.shape[1]
     away = [
-        jax.ShapeDtypeStruct((pairs, hidden_count), bf16),
         jax.ShapeDtypeStruct((channels, pairs), bf16),
         jax.ShapeDtypeStruct((channels, pairs), bf16),
     ]
     results = pl.pallas_call(
         prepare_kernel,
         in_specs=[HERE] * 5,
-        out_specs=[HERE] * 4 + [pl.BlockSpec(memory_space=pltpu.HBM)] * 3,
+        out_specs=[HERE] * 4 + [pl.BlockSpec(memory_space=pltpu.HBM)] * 2,
         out_shape=[
             jax.ShapeDtypeStruct((pairs, hidden_count), bf16),
             jax.ShapeDtypeStruct((pairs // CYCLES, channels), f32),
@@ -372,7 +369,7 @@
             jax.ShapeDtypeStruct((channels, hidden_count), bf16),
             *away,
         ],
-        scratch_shapes=[pltpu.VMEM(x.shape, x.dtype) for x in away[1:]]
+        scratch_shapes=[pltpu.VMEM(x.shape, x.dtype) for x in away]
         + [
             pltpu.VMEM((CYCLES, n_col, CYCLES, n_row, channels), f32),
             pltpu.SemaphoreType.DMA((len(away),)),
@@ -427,7 +424,7 @@
             flops=2 * pairs * 2 * channels * hidden_count, bytes_accessed=5 * 2**20, transcendentals=0
         ),
         name="pair",
-    )(d_logit, *[in_hbm(x) for x in (hidden, cycled, w_in, w_out, w_head_t)])
+    )(d_logit, hidden, *[in_hbm(x) for x in (cycled, w_in, w_out, w_head_t)])
 
 
 def middle_call(part, w_head_t, done, n_col):
@@ -468,7 +465,7 @@
         concat_axis=0,
         tiled=True,
     ).reshape(n_row, CYCLES * n_col, channels)
-    (hidden, logits, bins_wide, w_out_t), (hidden_far, normed_t, residual_t) = (
+    (hidden, logits, bins_wide, w_out_t), (normed_t, residual_t) = (
         prepare_call(pair_rep, true_bins, w_in, w_out, w_head_t, n_row, n_col)
     )
     d_logit, part = weights_call(
@@ -483,7 +480,7 @@
         tiled=True,
         axis_index_groups=[[far * ACROSS + x for x in range(ACROSS)] for far in range(n_far)],
     )
-    d_pair = pair_call(d_logit, hidden_far, pair_rep, w_in, w_out, w_head_t, n_row, n_col)
+    d_pair = pair_call(d_logit, hidden, pair_rep, w_in, w_out, w_head_t, n_row, n_col)
     share = middle_call(part, w_head_t, d_pair, n_col)
     share = lax.all_to_all(
         share.reshape(n_far * n_col, 4, channels),

time: 78.6 us -> 77.9 us (level)
  waiting for transfers between devices: 12.3 us -> 14.5 us
  local copies, waits for them, and re-layouts: 4.41 us -> 3.08 us
  Pallas kernels: 15.7 us -> 14.8 us
  blocking collectives: 19.4 us -> 18.6 us
    all_to_all x1, waiting for transfers between devices: 9.92 us -> 11.4 us  [shards(): lax.all_to_all(send.reshape(n_row * n_col, CYCLES, channels), ('row', 'co...]
    unnamed x13 -> x11, local copies, waits for them, and re-layouts: 4.41 us -> 3.08 us
  transfers between devices with their start and end apart: 2 -> 2, of which waited for: 2 -> 2; matrix products, arithmetic and copies ran while one was open for 1% -> 1% of each run, Pallas kernels for 10% -> 9%
where the time goes in v10:
time: 77.9 us; the launch traced here: 77.4 us
  starting transfers between devices  25.7 us (33%)
  blocking collectives  18.6 us (24%)
  Pallas kernels  14.8 us (19%)
  waiting for transfers between devices  14.5 us (19%)
  local copies, waits for them, and re-layouts  3.08 us (4%)
    all_to_all x1, starting transfers between devices, shards(): lax.all_to_all(send.reshape(n_row * n_col, CYCLES, channels), ('row', 'co...  22.2 us
    all_to_all x1, blocking collectives, shards(): lax.all_to_all(share.reshape(n_far * n_col, 4, channels), ('row', 'col'),...  18.6 us
    all_to_all x1, waiting for transfers between devices, shards(): lax.all_to_all(send.reshape(n_row * n_col, CYCLES, channels), ('row', 'co...  11.4 us
    pallas_call x1, Pallas kernels, forward_call(): pl.pallas_call(send_kernel, out_shape=jax.ShapeDtypeStruct((n_row, CYCLES...  4.04 us
    pallas_call x1, Pallas kernels, pair_call(): pl.pallas_call(pair_kernel, out_shape=jax.ShapeDtypeStruct(cycled.shape,...  3.65 us
    all_to_all x1, starting transfers between devices, shards(): lax.all_to_all(part, 'row', split_axis=0, concat_axis=0, tiled=True, axis...  3.54 us
    pallas_call x1, Pallas kernels, prepare_call(): pl.pallas_call(prepare_kernel, in_specs=[HERE] * 5, out_specs=[HERE] * 4...  3.48 us
    all_to_all x1, waiting for transfers between devices, shards(): lax.all_to_all(part, 'row', split_axis=0, concat_axis=0, tiled=True, axis...  3.09 us
  transfers between devices with their start and end apart: 2, of which 2 were waited for; matrix products, arithmetic and copies ran while one was open for 1% of the time, Pallas kernels for 9%

profile of v10, /device:TPU:1, one launch (start us, length us, event | category | flops | bytes accessed | tf_op | source)
XLA Modules:
  0.0 77.4 jit_solution(8004169491323832264)
XLA Ops:
  0.6 0.0 copy-start.2
  0.6 4.0 %forward.1 = s16[16,64,128]{2,1,0:T(8,128)(2,1)} custom-call(bf16[2,32,32,128]{3,2,1,0:T(8,128)(2,1)} %bitcast.19, bf16[128,512]{1,0:T(8,128)(2,1)} %w_in_ref.5, bf16[512,128]{1,0:T(8,128)(2,1)} %w_out_ref.5, bf16[64,128]{1,0:T(8,128)(2,1)} %bitcast.13), custom_call_target="tpu_custom_call" | custom-call | tf_op jit(solution)/shard_map/forward/pallas_call | solution.py:340
  4.7 22.2 %all-to-all-start = ((s16[512,2,128]{2,1,0:T(2,128)(2,1)}), s16[512,2,128]{2,1,0:T(2,128)(2,1)S(1)}, u32[]{:S(2)}, u32[]{:S(2)}) async-start(s16[512,2,128]{2,1,0:T(2,128)(2,1)} %bitcast.22), calls=%async_computation | async-start | bytes 524288 | tf_op jit(solution)/shard_map/all_to_all | solution.py:461
  26.8 0.8 %copy.9 = s32[64,32]{1,0:T(8,128)S(1)} copy(s32[64,32]{0,1:T(8,128)} %param.6) | data formatting | bytes 16384 | tf_op args[1]
  27.6 3.5 %prepare.1 = (bf16[2048,512]{1,0:T(8,128)(2,1)S(1)}, f32[1024,128]{1,0:T(8,128)S(1)}, bf16[32,2,16,128]{3,2,1,0:T(8,128)(2,1)S(1)}, bf16[128,512]{1,0:T(8,128)(2...) custom-call(bf16[2,32,32,128]{3,2,1,0:T(8,128)(2,1)} %bitcast.20, s32[2,32,32]{2,1,0:T(8,128)S(1)} %bitcast.18, ...), custom_call_target="tpu_custom_call" | custom-call | flops 536870912 | bytes 8388608 | tf_op jit(solution)/shard_map/prepare/pallas_call | solution.py:361
  31.1 0.0 copy-start
  31.1 0.8 %copy-done = bf16[128,2048]{1,0:T(8,128)(2,1)} copy-done((bf16[128,2048]{1,0:T(8,128)(2,1)}, bf16[128,2048]{1,0:T(8,128)(2,1)S(1)}, u32[]{:S(2)}) %copy-start) | copy-done | bytes 524312
  31.9 0.0 copy-start.1
  31.9 0.8 %copy-done.1 = bf16[128,2048]{1,0:T(8,128)(2,1)} copy-done((bf16[128,2048]{1,0:T(8,128)(2,1)}, bf16[128,2048]{1,0:T(8,128)(2,1)S(1)}, u32[]{:S(2)}) %copy-start.1) | copy-done | bytes 524312
  32.7 11.4 %all-to-all-done = s16[512,2,128]{2,1,0:T(2,128)(2,1)S(1)} async-done(((s16[512,2,128]{2,1,0:T(2,128)(2,1)}), s16[512,2,128]{2,1,0:T(2,128)(2,1)S(1)}, u32[]{:S(2)}, u32[]{:S(2)}) %all-to-all-start) | async-done | bytes 262176 | tf_op jit(solution)/shard_map/all_to_all | solution.py:461
  44.1 0.0 copy-done.2
  44.1 2.5 %weights.1 = (bf16[1024,128]{1,0:T(8,128)(2,1)S(1)}, bf16[16,64,128]{2,1,0:T(8,128)(2,1)S(1)}) custom-call(s16[16,64,128]{2,1,0:T(8,128)(2,1)S(1)} %bitcast.10, f32[1024,128]{1,0:T(8,128)S(1)} %get-tuple-element.16.logits_ref, bf16[32,2,16,128]{3,2,1,0:T(8,128)(2,1)S(1)} %get-tuple-element.17.bins_wide_ref, ...), custom_call_target="tpu_custom_call" | custom-call | tf_op jit(solution)/shard_map/weights/pallas_call | solution.py:399
  46.7 0.0 copy-start.4
  46.7 0.7 copy-done.4
  47.4 0.0 copy-start.3
  47.4 3.5 %all-to-all-start.1 = ((bf16[16,64,128]{2,1,0:T(8,128)(2,1)}), bf16[16,64,128]{2,1,0:T(8,128)(2,1)S(1)}, u32[]{:S(2)}, u32[]{:S(2)}) async-start(bf16[16,64,128]{2,1,0:T(8,128)(2,1)} %copy-done.4), calls=%async_computation.1 | async-start | bytes 524288 | tf_op jit(solution)/shard_map/all_to_all | solution.py:475
  50.9 3.6 %pair.1 = bf16[2,32,32,128]{3,2,1,0:T(8,128)(2,1)} custom-call(bf16[1024,128]{1,0:T(8,128)(2,1)S(1)} %get-tuple-element.22.d_logit_ref, bf16[2048,512]{1,0:T(8,128)(2,1)S(1)} %get-tuple-element.18.hidden_ref, bf16[2,32,32,128]{3,2,1,0:T(8,128)(2,1)} %bitcast.21, bf16[128,512]{1,0:T(8,128)(2,1)} %w_in_ref.5, bf16[512,128]{1,0:T(8,128)(2,1)} %w_out_ref.5, ...), custom_call_target="tpu_custom_call" | custom-call | flops 536870912 | bytes 5242880 | tf_op jit(solution)/shard_map/pair/pallas_call | solution.py:418
  54.6 3.1 %all-to-all-done.1.recv_ref = bf16[16,64,128]{2,1,0:T(8,128)(2,1)S(1)} async-done(((bf16[16,64,128]{2,1,0:T(8,128)(2,1)}), bf16[16,64,128]{2,1,0:T(8,128)(2,1)S(1)}, u32[]{:S(2)}, u32[]{:S(2)}) %all-to-all-start.1) | async-done | bytes 262176 | tf_op jit(solution)/shard_map/all_to_all | solution.py:475
  57.7 0.0 copy-done.3
  57.7 0.4 sum_x.1
  58.1 18.6 %all_to_all.15 = bf16[128,4,128]{2,1,0:T(4,128)(2,1)S(1)} all-to-all(bf16[128,4,128]{2,1,0:T(4,128)(2,1)S(1)} %bitcast.11), channel_id=1, replica_groups={{0,1,2,3,4,5,6,7,8,9,10,11,12,13,14,15,16,17,18,19,20,21,22,23,24,25,26..., dimensions={0} | all-to-all | bytes 262144 | tf_op jit(solution)/shard_map/all_to_all | solution.py:485
  76.7 0.7 sum_rest.1
Async XLA Ops:
  0.6 43.5 %copy-start.2 = (bf16[128,64]{0,1:T(8,128)(2,1)S(1)}, bf16[128,64]{0,1:T(8,128)(2,1)}, u32[]{:S(2)}) copy-start(bf16[128,64]{0,1:T(8,128)(2,1)} %param.9) | copy-start | bytes 49156
  4.7 39.4 %all-to-all-start = ((s16[512,2,128]{2,1,0:T(2,128)(2,1)}), s16[512,2,128]{2,1,0:T(2,128)(2,1)S(1)}, u32[]{:S(2)}, u32[]{:S(2)}) async-start(s16[512,2,128]{2,1,0:T(2,128)(2,1)} %bitcast.22), calls=%async_computation | async-start | bytes 524288 | tf_op jit(solution)/shard_map/all_to_all | solution.py:461
  31.1 0.8 %copy-start = (bf16[128,2048]{1,0:T(8,128)(2,1)}, bf16[128,2048]{1,0:T(8,128)(2,1)S(1)}, u32[]{:S(2)}) copy-start(bf16[128,2048]{1,0:T(8,128)(2,1)S(1)} %get-tuple-element.20.normed_t_hbm) | copy-start | bytes 1572868
  31.9 0.8 %copy-start.1 = (bf16[128,2048]{1,0:T(8,128)(2,1)}, bf16[128,2048]{1,0:T(8,128)(2,1)S(1)}, u32[]{:S(2)}) copy-start(bf16[128,2048]{1,0:T(8,128)(2,1)S(1)} %get-tuple-element.21.residual_t_hbm) | copy-start | bytes 1572868
  46.7 0.7 copy-start.4
  47.4 10.3 %copy-start.3 = (bf16[128,64]{0,1:T(8,128)(2,1)S(1)}, bf16[128,64]{0,1:T(8,128)(2,1)}, u32[]{:S(2)}) copy-start(bf16[128,64]{0,1:T(8,128)(2,1)} %param.9) | copy-start | bytes 49156
  47.4 10.3 %all-to-all-start.1 = ((bf16[16,64,128]{2,1,0:T(8,128)(2,1)}), bf16[16,64,128]{2,1,0:T(8,128)(2,1)S(1)}, u32[]{:S(2)}, u32[]{:S(2)}) async-start(bf16[16,64,128]{2,1,0:T(8,128)(2,1)} %copy-done.4), calls=%async_computation.1 | async-start | bytes 524288 | tf_op jit(solution)/shard_map/all_to_all | solution.py:475

commit v11 on v10

--- a/solution.py
+++ b/solution.py
@@ -16,6 +16,7 @@
 CYCLES = 2
 
 ACROSS = 4
+HALVES = 2
 
 
 def dot(first, second):
@@ -192,23 +193,41 @@
     g_mid = (
         dot(d_logit_t, hidden[:half])[:bins_count] + dot(d_logit_t, hidden[half:])[bins_count:]
     )
+    high = g_mid.astype(bf16)
+    rest = (g_mid - high.astype(f32)).astype(bf16)
+    w_head = w_head_t_ref[...].T
+    g_out = (dot(w_head, high) + dot(w_head, rest)).T
+    g_out_turned = pltpu.roll(g_out, bins_count, 1)
+    g_head = g_head + pltpu.roll(g_head, bins_count, 1)
+    g_head_turned = pltpu.roll(g_head, channels - bins_count // HALVES, 1)
     rows = channels // n_row
-    tiles = hidden.shape[1] // channels
-    long = tiles * rows
-    paired = jnp.concatenate([g_mid, jnp.roll(g_mid, -long // 2, axis=1)], axis=0).T
-    for r in range(n_row):
-        slot = r % ACROSS * (n_row // ACROSS) + r // ACROSS
-        mine = g_in[r * rows : (r + 1) * rows, :]
-        part_ref[slot, 0:long, :] = jnp.concatenate(
-            [mine[:, t * channels : (t + 1) * channels] for t in range(tiles)], axis=0
-        ).astype(bf16)
-        part_ref[slot, long : long + long // 2, :] = paired[
-            r * long : r * long + long // 2, :
-        ].astype(bf16)
-        mine = g_head[r * rows : (r + 1) * rows, :]
-        part_ref[slot, long + long // 2 :, :] = jnp.concatenate(
-            [mine, jnp.zeros_like(mine)], axis=0
-        ).astype(bf16)
+    tiles = hidden.shape[1] // channels // HALVES
+    wide = tiles * rows
+    long = g_out.shape[0] // n_row
+    n_far = n_row // ACROSS
+    for z in range(HALVES):
+        for x in range(ACROSS):
+            slot = z * ACROSS + x
+            heads = []
+            for far in range(n_far):
+                r = far * ACROSS + x
+                base = far * (wide + long // 2)
+                mine = g_in[r * rows : (r + 1) * rows, :]
+                part_ref[slot, base : base + wide, :] = jnp.concatenate(
+                    [mine[:, t * channels : (t + 1) * channels] for t in range(z * tiles, (z + 1) * tiles)],
+                    axis=0,
+                ).astype(bf16)
+                first = slice(r * long, r * long + long // 2)
+                second = slice(r * long + long // 2, (r + 1) * long)
+                part_ref[slot, base + wide : base + wide + long // 2, :] = jnp.where(
+                    left,
+                    (g_out if z == 0 else g_out_turned)[first],
+                    (g_out_turned if z == 0 else g_out)[second],
+                ).astype(bf16)
+                heads.append((g_head if z == 0 else g_head_turned)[r * rows : (r + 1) * rows])
+            part_ref[slot, n_far * (wide + long // 2) :, :] = jnp.concatenate(heads, axis=0).astype(
+                bf16
+            )
 
 
 def pair_gradient(d_logit, w_head_t):
@@ -253,52 +272,50 @@
     return (lanes_of(shape, 0) % width == lanes_of(shape, 1) % width).astype(f32).astype(kind)
 
 
-def middle_kernel(recv_ref, w_head_t_ref, out_ref, rows_ref, send_ref):
-    n_far = recv_ref.shape[0] // ACROSS
+def middle_kernel(recv_ref, out_ref, rows_ref, send_ref):
+    total = recv_ref[0].astype(f32)
+    for source in range(1, recv_ref.shape[0]):
+        total = total + recv_ref[source].astype(f32)
+    n_far = rows_ref.shape[0]
     for far in range(n_far):
-        total = recv_ref[far].astype(f32)
-        for x in range(1, ACROSS):
-            total = total + recv_ref[x * n_far + far].astype(f32)
-        pack(total, w_head_t_ref[...], rows_ref.at[far], send_ref, far)
+        pack(
+            total[far * 32 : far * 32 + 16],
+            total[far * 32 + 16 : far * 32 + 32],
+            total[n_far * 32 + far * 8 : n_far * 32 + far * 8 + 8],
+            rows_ref.at[far],
+            send_ref,
+            far * 64,
+        )
     out_ref[...] = send_ref[...].astype(bf16)
 
 
-def pack(total, w_head_t, rows_ref, send_ref, far):
-    n_col = total.shape[0] // 2
-    base = far * n_col * 4
-    rows, tiles = 8, 4
-    mine = total[: rows * tiles]
+def pack(wide, long, head, rows_ref, send_ref, base):
+    count = 16
+    rows, tiles = 8, 2
     group = lanes_of((1, rows, 128), 2) // 16 == lanes_of((1, rows, 128), 1)
-    spread = jnp.where(group, jnp.broadcast_to(mine[:, None, :], (rows * tiles, rows, 128)), 0.0)
+    spread = jnp.where(group, jnp.broadcast_to(wide[:, None, :], (rows * tiles, rows, 128)), 0.0)
     folded = dot(spread.reshape(-1, 128).astype(bf16), fold_matrix(16, bf16))
     folded = folded.reshape(tiles, rows, rows, 128)
     slot = lanes_of((1, rows, 1, 128), 3) // 16 == (8 - lanes_of((1, rows, 1, 128), 1)) % 8
-    part_in = jnp.sum(jnp.where(slot, folded, 0.0), axis=1).reshape(n_col, 128)
-    send_ref[pl.ds(base + 0, n_col, stride=4), :] = part_in
+    part_in = jnp.sum(jnp.where(slot, folded, 0.0), axis=1).reshape(count, 128)
+    send_ref[pl.ds(base, count, stride=4), :] = part_in
     lane = lanes_of((1, 128), 1)
-    mid = total[32:48]
-    mid = jnp.concatenate([jnp.where(lane < 64, mid, 0.0), jnp.where(lane < 64, 0.0, mid)], axis=0)
-    twice = jnp.concatenate([w_head_t, w_head_t], axis=0)
-    high = mid.astype(bf16)
-    low = (mid - high.astype(f32)).astype(bf16)
-    mine = dot(high, twice) + dot(low, twice)
+    mine = jnp.concatenate([long, pltpu.roll(long, 64, 1)], axis=0)
     rows_ref[0] = jnp.concatenate([mine] * 4, axis=0).T
-    part_out = rows_ref[0, pl.ds(0, n_col, stride=4), :]
+    part_out = rows_ref[0, pl.ds(0, count, stride=4), :]
     for j in range(1, 4):
         part_out = jnp.where(
-            lane // 32 == 4 - j, rows_ref[0, pl.ds(j, n_col, stride=4), :], part_out
+            lane // 32 == 4 - j, rows_ref[0, pl.ds(j, count, stride=4), :], part_out
         )
-    send_ref[pl.ds(base + 1, n_col, stride=4), :] = part_out
-    mine = total[48:56]
-    mine = mine + pltpu.roll(mine, 64, 1)
-    rows_ref[1] = jnp.concatenate([mine] * 16, axis=0).T
+    send_ref[pl.ds(base + 1, count, stride=4), :] = part_out
+    rows_ref[1] = jnp.concatenate([head] * 16, axis=0).T
     part_head = jnp.where(
         lane // 8 == 15,
-        rows_ref[1, pl.ds(1, n_col, stride=2), :],
-        rows_ref[1, pl.ds(0, n_col, stride=2), :],
-    )
-    send_ref[pl.ds(base + 2, n_col, stride=4), :] = part_head
-    send_ref[pl.ds(base + 3, n_col, stride=4), :] = jnp.zeros_like(part_head)
+        rows_ref[1, pl.ds(1, count, stride=2), :],
+        rows_ref[1, pl.ds(0, count, stride=2), :],
+    )
+    send_ref[pl.ds(base + 2, count, stride=4), :] = part_head
+    send_ref[pl.ds(base + 3, count, stride=4), :] = jnp.zeros_like(part_head)
 
 
 def final_kernel(scale, recv_ref, in_ref, out_t_ref, head_t_ref):
@@ -393,14 +410,15 @@
     logits, bins_wide, hidden, w_out_t = near
     n_row, span, channels = recv.shape
     pairs, hidden_count = hidden.shape
-    part_rows = 2 * (hidden_count // n_row)
+    far_rows = hidden_count // n_row // 2 + channels // n_row * (hidden_count // channels) // HALVES
+    part_rows = n_row // ACROSS * (far_rows + channels // n_row)
     d_logit = jax.ShapeDtypeStruct((pairs // CYCLES, channels), bf16)
     late = (normed_t, residual_t)
     return pl.pallas_call(
         weights_kernel,
         in_specs=[HERE] * 5 + [THERE] * 2 + [HERE],
         out_specs=[HERE, HERE],
-        out_shape=[d_logit, jax.ShapeDtypeStruct((n_row, part_rows, channels), bf16)],
+        out_shape=[d_logit, jax.ShapeDtypeStruct((HALVES * ACROSS, part_rows, channels), bf16)],
         scratch_shapes=[pltpu.VMEM(x.shape, x.dtype) for x in late]
         + [
             pltpu.VMEM((pairs // CYCLES, channels), f32),
@@ -427,17 +445,17 @@
     )(d_logit, hidden, *[in_hbm(x) for x in (cycled, w_in, w_out, w_head_t)])
 
 
-def middle_call(part, w_head_t, done, n_col):
+def middle_call(part, done, n_row, n_col):
     part, _ = lax.optimization_barrier((part, done))
-    n_far = part.shape[0] // ACROSS
-    shape = (n_far * n_col * 4, part.shape[-1])
+    n_far = n_row // ACROSS
+    shape = (n_far * (n_col // HALVES) * 4, part.shape[-1])
     return pl.pallas_call(
         middle_kernel,
         out_shape=jax.ShapeDtypeStruct(shape, bf16),
         scratch_shapes=[pltpu.VMEM((n_far, 2, 128, 128), f32), pltpu.VMEM(shape, f32)],
         compiler_params=params(ROOM),
-        name="sum_x",
-    )(part, w_head_t)
+        name="sum_near",
+    )(part)
 
 
 def final_call(share, scale, shapes):
@@ -471,28 +489,41 @@
     d_logit, part = weights_call(
         recv, (logits, bins_wide, hidden, w_out_t), normed_t, residual_t, w_head_t
     )
-    n_far = n_row // ACROSS
+    n_far, n_half = n_row // ACROSS, n_col // HALVES
     part = lax.all_to_all(
         part,
-        "row",
-        split_axis=0,
-        concat_axis=0,
-        tiled=True,
-        axis_index_groups=[[far * ACROSS + x for x in range(ACROSS)] for far in range(n_far)],
-    )
-    d_pair = pair_call(d_logit, hidden, pair_rep, w_in, w_out, w_head_t, n_row, n_col)
-    share = middle_call(part, w_head_t, d_pair, n_col)
-    share = lax.all_to_all(
-        share.reshape(n_far * n_col, 4, channels),
         ("row", "col"),
         split_axis=0,
         concat_axis=0,
         tiled=True,
         axis_index_groups=[
-            [(far * ACROSS + x) * n_col + c for far in range(n_far) for c in range(n_col)]
+            [
+                (far * ACROSS + x) * n_col + z * n_half + c
+                for z in range(HALVES)
+                for x in range(ACROSS)
+            ]
+            for far in range(n_far)
+            for c in range(n_half)
+        ],
+    )
+    d_pair = pair_call(d_logit, hidden, pair_rep, w_in, w_out, w_head_t, n_row, n_col)
+    share = middle_call(part, d_pair, n_row, n_col)
+    share = lax.all_to_all(
+        share.reshape(n_far * n_half, 4, channels),
+        ("row", "col"),
+        split_axis=0,
+        concat_axis=0,
+        tiled=True,
+        axis_index_groups=[
+            [
+                (far * ACROSS + x) * n_col + z * n_half + c
+                for far in range(n_far)
+                for c in range(n_half)
+            ]
+            for z in range(HALVES)
             for x in range(ACROSS)
         ],
-    ).reshape(n_far * n_col * 4, channels)
+    ).reshape(n_far * n_half * 4, channels)
     grad_in, grad_out_t, grad_head_t = final_call(
         share,
         1.0 / (row_count * n_row),

time: 77.9 us -> 77.5 us (level)
  blocking collectives: 18.6 us -> 17.8 us
  Pallas kernels: 14.8 us -> 15.6 us
    pallas_call x1, Pallas kernels: 2.54 us -> 3.46 us  [weights_call(): pl.pallas_call(weights_kernel, in_specs=[HERE] * 5 + [THERE] * 2 + [HERE]...]
    all_to_all x1, blocking collectives: 18.6 us -> 17.8 us  [shards(): lax.all_to_all(share.reshape(n_far * n_half, 4, channels), ('row', 'col')...]
    unnamed x11 -> x7, local copies, waits for them, and re-layouts: 3.08 us -> 2.39 us
where the time goes in v11:
time: 77.5 us; the launch traced here: 77.1 us
  starting transfers between devices  25.6 us (33%)
  blocking collectives  17.8 us (23%)
  Pallas kernels  15.6 us (20%)
  waiting for transfers between devices  14.9 us (19%)
  local copies, waits for them, and re-layouts  2.39 us (3%)
    all_to_all x1, starting transfers between devices, shards(): lax.all_to_all(send.reshape(n_row * n_col, CYCLES, channels), ('row', 'co...  22.2 us
    all_to_all x1, blocking collectives, shards(): lax.all_to_all(share.reshape(n_far * n_half, 4, channels), ('row', 'col')...  17.8 us
    all_to_all x1, waiting for transfers between devices, shards(): lax.all_to_all(send.reshape(n_row * n_col, CYCLES, channels), ('row', 'co...  11.4 us
    pallas_call x1, Pallas kernels, forward_call(): pl.pallas_call(send_kernel, out_shape=jax.ShapeDtypeStruct((n_row, CYCLES...  4.05 us
    pallas_call x1, Pallas kernels, pair_call(): pl.pallas_call(pair_kernel, out_shape=jax.ShapeDtypeStruct(cycled.shape,...  3.65 us
    all_to_all x1, waiting for transfers between devices, shards(): lax.all_to_all(part, ('row', 'col'), split_axis=0, concat_axis=0, tiled=T...  3.54 us
    pallas_call x1, Pallas kernels, prepare_call(): pl.pallas_call(prepare_kernel, in_specs=[HERE] * 5, out_specs=[HERE] * 4...  3.48 us
    pallas_call x1, Pallas kernels, weights_call(): pl.pallas_call(weights_kernel, in_specs=[HERE] * 5 + [THERE] * 2 + [HERE]...  3.46 us
  transfers between devices with their start and end apart: 2, of which 2 were waited for; matrix products, arithmetic and copies ran while one was open for 1% of the time, Pallas kernels for 9%

profile of v11, /device:TPU:1, one launch (start us, length us, event | category | flops | bytes accessed | tf_op | source)
XLA Modules:
  0.0 77.1 jit_solution(3087578974087412597)
XLA Ops:
  0.6 0.0 copy-start.2
  0.6 4.0 %forward.1 = s16[16,64,128]{2,1,0:T(8,128)(2,1)} custom-call(bf16[2,32,32,128]{3,2,1,0:T(8,128)(2,1)} %bitcast.18, bf16[128,512]{1,0:T(8,128)(2,1)} %w_in_ref.5, bf16[512,128]{1,0:T(8,128)(2,1)} %w_out_ref.5, bf16[64,128]{1,0:T(8,128)(2,1)} %bitcast.13), custom_call_target="tpu_custom_call" | custom-call | tf_op jit(solution)/shard_map/forward/pallas_call | solution.py:357
  4.7 22.2 %all-to-all-start = ((s16[512,2,128]{2,1,0:T(2,128)(2,1)}), s16[512,2,128]{2,1,0:T(2,128)(2,1)S(1)}, u32[]{:S(2)}, u32[]{:S(2)}) async-start(s16[512,2,128]{2,1,0:T(2,128)(2,1)} %bitcast.21), calls=%async_computation | async-start | bytes 524288 | tf_op jit(solution)/shard_map/all_to_all | solution.py:479
  26.9 0.8 %copy.9 = s32[64,32]{1,0:T(8,128)S(1)} copy(s32[64,32]{0,1:T(8,128)} %param.6) | data formatting | bytes 16384 | tf_op args[1]
  27.7 3.5 %prepare.1 = (bf16[2048,512]{1,0:T(8,128)(2,1)S(1)}, f32[1024,128]{1,0:T(8,128)S(1)}, bf16[32,2,16,128]{3,2,1,0:T(8,128)(2,1)S(1)}, bf16[128,512]{1,0:T(8,128)(2...) custom-call(bf16[2,32,32,128]{3,2,1,0:T(8,128)(2,1)} %bitcast.19, s32[2,32,32]{2,1,0:T(8,128)S(1)} %bitcast.17, ...), custom_call_target="tpu_custom_call" | custom-call | flops 536870912 | bytes 8388608 | tf_op jit(solution)/shard_map/prepare/pallas_call | solution.py:378
  31.1 0.0 copy-start
  31.1 0.8 %copy-done = bf16[128,2048]{1,0:T(8,128)(2,1)} copy-done((bf16[128,2048]{1,0:T(8,128)(2,1)}, bf16[128,2048]{1,0:T(8,128)(2,1)S(1)}, u32[]{:S(2)}) %copy-start) | copy-done | bytes 524312
  31.9 0.0 copy-start.1
  31.9 0.8 %copy-done.1 = bf16[128,2048]{1,0:T(8,128)(2,1)} copy-done((bf16[128,2048]{1,0:T(8,128)(2,1)}, bf16[128,2048]{1,0:T(8,128)(2,1)S(1)}, u32[]{:S(2)}) %copy-start.1) | copy-done | bytes 524312
  32.7 11.4 %all-to-all-done = s16[512,2,128]{2,1,0:T(2,128)(2,1)S(1)} async-done(((s16[512,2,128]{2,1,0:T(2,128)(2,1)}), s16[512,2,128]{2,1,0:T(2,128)(2,1)S(1)}, u32[]{:S(2)}, u32[]{:S(2)}) %all-to-all-start) | async-done | bytes 262176 | tf_op jit(solution)/shard_map/all_to_all | solution.py:479
  44.1 0.0 copy-done.2
  44.1 3.5 %weights.1 = (bf16[1024,128]{1,0:T(8,128)(2,1)S(1)}, bf16[8,160,128]{2,1,0:T(8,128)(2,1)}) custom-call(s16[16,64,128]{2,1,0:T(8,128)(2,1)S(1)} %bitcast.10, f32[1024,128]{1,0:T(8,128)S(1)} %get-tuple-element.16.logits_ref, bf16[32,2,16,128]{3,2,1,0:T(8,128)(2,1)S(1)} %get-tuple-element.17.bins_wide_ref, bf16[2048,512]{1,0:T(8,128)(2,1)S(1)} %get-tuple-element.18.hidden_ref, ...), custom_call_target="tpu_custom_call" | custom-call | tf_op jit(solution)/shard_map/weights/pallas_call | solution.py:417
  47.6 3.4 %all-to-all-start.1 = ((bf16[8,160,128]{2,1,0:T(8,128)(2,1)}), bf16[8,160,128]{2,1,0:T(8,128)(2,1)S(1)}, u32[]{:S(2)}, u32[]{:S(2)}) async-start(bf16[8,160,128]{2,1,0:T(8,128)(2,1)} %get-tuple-element.23), calls=%async_computation.1 | async-start | bytes 655360 | tf_op jit(solution)/shard_map/all_to_all | solution.py:493
  51.0 3.6 %pair.1 = bf16[2,32,32,128]{3,2,1,0:T(8,128)(2,1)} custom-call(bf16[1024,128]{1,0:T(8,128)(2,1)S(1)} %get-tuple-element.22.d_logit_ref, bf16[2048,512]{1,0:T(8,128)(2,1)S(1)} %get-tuple-element.18.hidden_ref, bf16[2,32,32,128]{3,2,1,0:T(8,128)(2,1)} %bitcast.20, bf16[128,512]{1,0:T(8,128)(2,1)} %w_in_ref.5, bf16[512,128]{1,0:T(8,128)(2,1)} %w_out_ref.5, ...), custom_call_target="tpu_custom_call" | custom-call | flops 536870912 | bytes 5242880 | tf_op jit(solution)/shard_map/pair/pallas_call | solution.py:436
  54.7 3.5 %all-to-all-done.1.recv_ref = bf16[8,160,128]{2,1,0:T(8,128)(2,1)S(1)} async-done(((bf16[8,160,128]{2,1,0:T(8,128)(2,1)}), bf16[8,160,128]{2,1,0:T(8,128)(2,1)S(1)}, u32[]{:S(2)}, u32[]{:S(2)}) %all-to-all-start.1) | async-done | bytes 327712 | tf_op jit(solution)/shard_map/all_to_all | solution.py:493
  58.2 0.3 sum_near.1
  58.5 17.8 %all_to_all.15 = bf16[64,4,128]{2,1,0:T(4,128)(2,1)S(1)} all-to-all(bf16[64,4,128]{2,1,0:T(4,128)(2,1)S(1)} %bitcast.12), channel_id=1, replica_groups={{0,1,2,3,4,5,6,7,8,9,10,11,12,13,14,15,128,129,130,131,132,133,134,135,..., dimensions={0} | all-to-all | bytes 131072 | tf_op jit(solution)/shard_map/all_to_all | solution.py:511
  76.4 0.7 sum_rest.1
Async XLA Ops:
  0.6 43.5 %copy-start.2 = (bf16[128,64]{0,1:T(8,128)(2,1)S(1)}, bf16[128,64]{0,1:T(8,128)(2,1)}, u32[]{:S(2)}) copy-start(bf16[128,64]{0,1:T(8,128)(2,1)} %param.9) | copy-start | bytes 49156
  4.7 39.4 %all-to-all-start = ((s16[512,2,128]{2,1,0:T(2,128)(2,1)}), s16[512,2,128]{2,1,0:T(2,128)(2,1)S(1)}, u32[]{:S(2)}, u32[]{:S(2)}) async-start(s16[512,2,128]{2,1,0:T(2,128)(2,1)} %bitcast.21), calls=%async_computation | async-start | bytes 524288 | tf_op jit(solution)/shard_map/all_to_all | solution.py:479
  31.1 0.8 %copy-start = (bf16[128,2048]{1,0:T(8,128)(2,1)}, bf16[128,2048]{1,0:T(8,128)(2,1)S(1)}, u32[]{:S(2)}) copy-start(bf16[128,2048]{1,0:T(8,128)(2,1)S(1)} %get-tuple-element.20.normed_t_hbm) | copy-start | bytes 1572868
  31.9 0.8 %copy-start.1 = (bf16[128,2048]{1,0:T(8,128)(2,1)}, bf16[128,2048]{1,0:T(8,128)(2,1)S(1)}, u32[]{:S(2)}) copy-start(bf16[128,2048]{1,0:T(8,128)(2,1)S(1)} %get-tuple-element.21.residual_t_hbm) | copy-start | bytes 1572868
  47.6 10.6 %all-to-all-start.1 = ((bf16[8,160,128]{2,1,0:T(8,128)(2,1)}), bf16[8,160,128]{2,1,0:T(8,128)(2,1)S(1)}, u32[]{:S(2)}, u32[]{:S(2)}) async-start(bf16[8,160,128]{2,1,0:T(8,128)(2,1)} %get-tuple-element.23), calls=%async_computation.1 | async-start | bytes 655360 | tf_op jit(solution)/shard_map/all_to_all | solution.py:493

commit v12 on v11

--- a/solution.py
+++ b/solution.py
@@ -445,8 +445,7 @@
     )(d_logit, hidden, *[in_hbm(x) for x in (cycled, w_in, w_out, w_head_t)])
 
 
-def middle_call(part, done, n_row, n_col):
-    part, _ = lax.optimization_barrier((part, done))
+def middle_call(part, n_row, n_col):
     n_far = n_row // ACROSS
     shape = (n_far * (n_col // HALVES) * 4, part.shape[-1])
     return pl.pallas_call(
@@ -506,8 +505,7 @@
             for c in range(n_half)
         ],
     )
-    d_pair = pair_call(d_logit, hidden, pair_rep, w_in, w_out, w_head_t, n_row, n_col)
-    share = middle_call(part, d_pair, n_row, n_col)
+    share = middle_call(part, n_row, n_col)
     share = lax.all_to_all(
         share.reshape(n_far * n_half, 4, channels),
         ("row", "col"),
@@ -524,6 +522,7 @@
             for x in range(ACROSS)
         ],
     ).reshape(n_far * n_half * 4, channels)
+    d_pair = pair_call(d_logit, hidden, pair_rep, w_in, w_out, w_head_t, n_row, n_col)
     grad_in, grad_out_t, grad_head_t = final_call(
         share,
         1.0 / (row_count * n_row),

time: 77.5 us -> 77.5 us (level)
  blocking collectives: 17.8 us -> 10.1 us
  waiting for transfers between devices: 14.9 us -> 19.9 us
  starting transfers between devices: 25.6 us -> 28.6 us
    all_to_all x1, blocking collectives: 17.8 us -> 10.1 us  [shards(): lax.all_to_all(part, ('row', 'col'), split_axis=0, concat_axis=0, tiled=T...]
    all_to_all x1, waiting for transfers between devices: 3.54 us -> 8.54 us  [shards(): lax.all_to_all(share.reshape(n_far * n_half, 4, channels), ('row', 'col')...]
    all_to_all x1, starting transfers between devices: 3.44 us -> 6.4 us  [shards(): lax.all_to_all(share.reshape(n_far * n_half, 4, channels), ('row', 'col')...]
where the time goes in v12:
time: 77.5 us; the launch traced here: 77.1 us
  starting transfers between devices  28.6 us (37%)
  waiting for transfers between devices  19.9 us (26%)
  Pallas kernels  15.5 us (20%)
  blocking collectives  10.1 us (13%)
  local copies, waits for them, and re-layouts  2.39 us (3%)
    all_to_all x1, starting transfers between devices, shards(): lax.all_to_all(send.reshape(n_row * n_col, CYCLES, channels), ('row', 'co...  22.2 us
    all_to_all x1, waiting for transfers between devices, shards(): lax.all_to_all(send.reshape(n_row * n_col, CYCLES, channels), ('row', 'co...  11.4 us
    all_to_all x1, blocking collectives, shards(): lax.all_to_all(part, ('row', 'col'), split_axis=0, concat_axis=0, tiled=T...  10.1 us
    all_to_all x1, waiting for transfers between devices, shards(): lax.all_to_all(share.reshape(n_far * n_half, 4, channels), ('row', 'col')...  8.54 us
    all_to_all x1, starting transfers between devices, shards(): lax.all_to_all(share.reshape(n_far * n_half, 4, channels), ('row', 'col')...  6.4 us
    pallas_call x1, Pallas kernels, forward_call(): pl.pallas_call(send_kernel, out_shape=jax.ShapeDtypeStruct((n_row, CYCLES...  4.05 us
    pallas_call x1, Pallas kernels, pair_call(): pl.pallas_call(pair_kernel, out_shape=jax.ShapeDtypeStruct(cycled.shape,...  3.64 us
    pallas_call x1, Pallas kernels, prepare_call(): pl.pallas_call(prepare_kernel, in_specs=[HERE] * 5, out_specs=[HERE] * 4...  3.48 us
  transfers between devices with their start and end apart: 2, of which 2 were waited for; matrix products, arithmetic and copies ran while one was open for 1% of the time, Pallas kernels for 9%

profile of v12, /device:TPU:1, one launch (start us, length us, event | category | flops | bytes accessed | tf_op | source)
XLA Modules:
  0.0 77.1 jit_solution(12300542275734464916)
XLA Ops:
  0.6 0.0 copy-start.2
  0.6 4.0 %forward.1 = s16[16,64,128]{2,1,0:T(8,128)(2,1)} custom-call(bf16[2,32,32,128]{3,2,1,0:T(8,128)(2,1)} %bitcast.17, bf16[128,512]{1,0:T(8,128)(2,1)} %w_in_ref.5, bf16[512,128]{1,0:T(8,128)(2,1)} %w_out_ref.5, bf16[64,128]{1,0:T(8,128)(2,1)} %bitcast.12), custom_call_target="tpu_custom_call" | custom-call | tf_op jit(solution)/shard_map/forward/pallas_call | solution.py:357
  4.7 22.2 %all-to-all-start = ((s16[512,2,128]{2,1,0:T(2,128)(2,1)}), s16[512,2,128]{2,1,0:T(2,128)(2,1)S(1)}, u32[]{:S(2)}, u32[]{:S(2)}) async-start(s16[512,2,128]{2,1,0:T(2,128)(2,1)} %bitcast.20), calls=%async_computation | async-start | bytes 524288 | tf_op jit(solution)/shard_map/all_to_all | solution.py:478
  26.9 0.8 %copy.9 = s32[64,32]{1,0:T(8,128)S(1)} copy(s32[64,32]{0,1:T(8,128)} %param.6) | data formatting | bytes 16384 | tf_op args[1]
  27.7 3.5 %prepare.1 = (bf16[2048,512]{1,0:T(8,128)(2,1)S(1)}, f32[1024,128]{1,0:T(8,128)S(1)}, bf16[32,2,16,128]{3,2,1,0:T(8,128)(2,1)S(1)}, bf16[128,512]{1,0:T(8,128)(2...) custom-call(bf16[2,32,32,128]{3,2,1,0:T(8,128)(2,1)} %bitcast.18, s32[2,32,32]{2,1,0:T(8,128)S(1)} %bitcast.16, ...), custom_call_target="tpu_custom_call" | custom-call | flops 536870912 | bytes 8388608 | tf_op jit(solution)/shard_map/prepare/pallas_call | solution.py:378
  31.1 0.0 copy-start
  31.1 0.8 %copy-done = bf16[128,2048]{1,0:T(8,128)(2,1)} copy-done((bf16[128,2048]{1,0:T(8,128)(2,1)}, bf16[128,2048]{1,0:T(8,128)(2,1)S(1)}, u32[]{:S(2)}) %copy-start) | copy-done | bytes 524312
  31.9 0.0 copy-start.1
  31.9 0.8 %copy-done.1 = bf16[128,2048]{1,0:T(8,128)(2,1)} copy-done((bf16[128,2048]{1,0:T(8,128)(2,1)}, bf16[128,2048]{1,0:T(8,128)(2,1)S(1)}, u32[]{:S(2)}) %copy-start.1) | copy-done | bytes 524312
  32.7 11.4 %all-to-all-done = s16[512,2,128]{2,1,0:T(2,128)(2,1)S(1)} async-done(((s16[512,2,128]{2,1,0:T(2,128)(2,1)}), s16[512,2,128]{2,1,0:T(2,128)(2,1)S(1)}, u32[]{:S(2)}, u32[]{:S(2)}) %all-to-all-start) | async-done | bytes 262176 | tf_op jit(solution)/shard_map/all_to_all | solution.py:478
  44.1 0.0 copy-done.2
  44.1 2.7 %weights.1 = (bf16[1024,128]{1,0:T(8,128)(2,1)S(1)}, bf16[8,160,128]{2,1,0:T(8,128)(2,1)S(1)}) custom-call(s16[16,64,128]{2,1,0:T(8,128)(2,1)S(1)} %bitcast.10, f32[1024,128]{1,0:T(8,128)S(1)} %get-tuple-element.15.logits_ref, bf16[32,2,16,128]{3,2,1,0:T(8,128)(2,1)S(1)} %get-tuple-element.16.bins_wide_ref, ...), custom_call_target="tpu_custom_call" | custom-call | tf_op jit(solution)/shard_map/weights/pallas_call | solution.py:417
  46.9 10.1 %all_to_all.15.recv_ref = bf16[8,160,128]{2,1,0:T(8,128)(2,1)S(1)} all-to-all(bf16[8,160,128]{2,1,0:T(8,128)(2,1)S(1)} %get-tuple-element.22), channel_id=1, replica_groups={{0,32,64,96,16,48,80,112},{1,33,65,97,17,49,81,113},{2,34,66,98,18,50,8..., dimensions={0} | all-to-all | bytes 655360 | tf_op jit(solution)/shard_map/all_to_all | solution.py:492
  56.9 0.9 %sum_near.1 = bf16[256,128]{1,0:T(8,128)(2,1)} custom-call(bf16[8,160,128]{2,1,0:T(8,128)(2,1)S(1)} %all_to_all.15.recv_ref), custom_call_target="tpu_custom_call" | custom-call | tf_op jit(solution)/shard_map/sum_near/pallas_call | solution.py:451
  57.9 6.4 %all-to-all-start.2 = ((bf16[64,4,128]{2,1,0:T(4,128)(2,1)}), bf16[64,4,128]{2,1,0:T(4,128)(2,1)S(1)}, u32[]{:S(2)}, u32[]{:S(2)}) async-start(bf16[64,4,128]{2,1,0:T(4,128)(2,1)} %bitcast.6), calls=%async_computation.2 | async-start | bytes 131072 | tf_op jit(solution)/shard_map/all_to_all | solution.py:509
  64.3 3.6 %pair.1 = bf16[2,32,32,128]{3,2,1,0:T(8,128)(2,1)} custom-call(bf16[1024,128]{1,0:T(8,128)(2,1)S(1)} %get-tuple-element.21.d_logit_ref, bf16[2048,512]{1,0:T(8,128)(2,1)S(1)} %get-tuple-element.17.hidden_ref, bf16[2,32,32,128]{3,2,1,0:T(8,128)(2,1)} %bitcast.19, bf16[128,512]{1,0:T(8,128)(2,1)} %w_in_ref.5, bf16[512,128]{1,0:T(8,128)(2,1)} %w_out_ref.5, ...), custom_call_target="tpu_custom_call" | custom-call | flops 536870912 | bytes 5242880 | tf_op jit(solution)/shard_map/pair/pallas_call | solution.py:436
  67.9 8.5 %all-to-all-done.2 = bf16[64,4,128]{2,1,0:T(4,128)(2,1)S(1)} async-done(((bf16[64,4,128]{2,1,0:T(4,128)(2,1)}), bf16[64,4,128]{2,1,0:T(4,128)(2,1)S(1)}, u32[]{:S(2)}, u32[]{:S(2)}) %all-to-all-start.2) | async-done | bytes 65568 | tf_op jit(solution)/shard_map/all_to_all | solution.py:509
  76.4 0.7 sum_rest.1
Async XLA Ops:
  0.6 43.5 %copy-start.2 = (bf16[128,64]{0,1:T(8,128)(2,1)S(1)}, bf16[128,64]{0,1:T(8,128)(2,1)}, u32[]{:S(2)}) copy-start(bf16[128,64]{0,1:T(8,128)(2,1)} %param.9) | copy-start | bytes 49156
  4.7 39.4 %all-to-all-start = ((s16[512,2,128]{2,1,0:T(2,128)(2,1)}), s16[512,2,128]{2,1,0:T(2,128)(2,1)S(1)}, u32[]{:S(2)}, u32[]{:S(2)}) async-start(s16[512,2,128]{2,1,0:T(2,128)(2,1)} %bitcast.20), calls=%async_computation | async-start | bytes 524288 | tf_op jit(solution)/shard_map/all_to_all | solution.py:478
  31.1 0.8 %copy-start = (bf16[128,2048]{1,0:T(8,128)(2,1)}, bf16[128,2048]{1,0:T(8,128)(2,1)S(1)}, u32[]{:S(2)}) copy-start(bf16[128,2048]{1,0:T(8,128)(2,1)S(1)} %get-tuple-element.19.normed_t_hbm) | copy-start | bytes 1572868
  31.9 0.8 %copy-start.1 = (bf16[128,2048]{1,0:T(8,128)(2,1)}, bf16[128,2048]{1,0:T(8,128)(2,1)S(1)}, u32[]{:S(2)}) copy-start(bf16[128,2048]{1,0:T(8,128)(2,1)S(1)} %get-tuple-element.20.residual_t_hbm) | copy-start | bytes 1572868
  57.9 18.6 %all-to-all-start.2 = ((bf16[64,4,128]{2,1,0:T(4,128)(2,1)}), bf16[64,4,128]{2,1,0:T(4,128)(2,1)S(1)}, u32[]{:S(2)}, u32[]{:S(2)}) async-start(bf16[64,4,128]{2,1,0:T(4,128)(2,1)} %bitcast.6), calls=%async_computation.2 | async-start | bytes 131072 | tf_op jit(solution)/shard_map/all_to_all | solution.py:509

commit v13 on v12

--- a/solution.py
+++ b/solution.py
@@ -14,6 +14,7 @@
 code_steps = 2350.0
 
 CYCLES = 2
+CHUNKS = 2
 
 ACROSS = 4
 HALVES = 2
@@ -60,13 +61,16 @@
     n_row = send_ref.shape[0]
     span = send_ref.shape[1]
     channels = pair_ref.shape[-1]
-    values = pair_ref[...].reshape(-1, channels).astype(f32)
-    half = values.shape[0] // CYCLES
-    x_hat, _ = normalize(values)
-    hidden = jnp.maximum(dot(x_hat.astype(bf16), w_in_ref[...]), 0.0).astype(bf16)
-    residual = (values + dot(hidden, w_out_ref[...])).astype(bf16)
-    wide = jnp.concatenate([residual[:half], residual[half:]], axis=1)
-    rows_ref[...] = encode(dot_t(wide, widen(w_head_t_ref[...])))
+    count = pair_ref.shape[1] // CHUNKS
+    half = count * pair_ref.shape[2]
+    w_wide = widen(w_head_t_ref[...])
+    for g in range(CHUNKS):
+        values = pair_ref[:, g * count : (g + 1) * count].reshape(-1, channels).astype(f32)
+        x_hat, _ = normalize(values)
+        hidden = jnp.maximum(dot(x_hat.astype(bf16), w_in_ref[...]), 0.0).astype(bf16)
+        residual = (values + dot(hidden, w_out_ref[...])).astype(bf16)
+        wide = jnp.concatenate([residual[:half], residual[half:]], axis=1)
+        rows_ref[g * half : (g + 1) * half] = encode(dot_t(wide, w_wide))
     for r in range(n_row):
         send_ref[r] = rows_ref[pl.ds(r, span, stride=n_row), :].astype(jnp.int16)
 
@@ -188,11 +192,11 @@
         dot(residual_t_ref[:, :half], d_logit),
         dot(residual_t_ref[:, half:], d_logit),
     )
-    g_in = dot(normed_t_ref[...], d_hidden)
     d_logit_t = d_logit.T
     g_mid = (
         dot(d_logit_t, hidden[:half])[:bins_count] + dot(d_logit_t, hidden[half:])[bins_count:]
     )
+    g_in = dot(normed_t_ref[...], d_hidden)
     high = g_mid.astype(bf16)
     rest = (g_mid - high.astype(f32)).astype(bf16)
     w_head = w_head_t_ref[...].T

time: 77.5 us -> 77.3 us (level)
  no operation moved by 1% of the time
where the time goes in v13:
time: 77.3 us; the launch traced here: 76.9 us
  starting transfers between devices  28.6 us (37%)
  waiting for transfers between devices  19.9 us (26%)
  Pallas kernels  15.3 us (20%)
  blocking collectives  10.1 us (13%)
  local copies, waits for them, and re-layouts  2.39 us (3%)
    all_to_all x1, starting transfers between devices, shards(): lax.all_to_all(send.reshape(n_row * n_col, CYCLES, channels), ('row', 'co...  22.2 us
    all_to_all x1, waiting for transfers between devices, shards(): lax.all_to_all(send.reshape(n_row * n_col, CYCLES, channels), ('row', 'co...  11.4 us
    all_to_all x1, blocking collectives, shards(): lax.all_to_all(part, ('row', 'col'), split_axis=0, concat_axis=0, tiled=T...  10.1 us
    all_to_all x1, waiting for transfers between devices, shards(): lax.all_to_all(share.reshape(n_far * n_half, 4, channels), ('row', 'col')...  8.54 us
    all_to_all x1, starting transfers between devices, shards(): lax.all_to_all(share.reshape(n_far * n_half, 4, channels), ('row', 'col')...  6.4 us
    pallas_call x1, Pallas kernels, forward_call(): pl.pallas_call(send_kernel, out_shape=jax.ShapeDtypeStruct((n_row, CYCLES...  3.96 us
    pallas_call x1, Pallas kernels, pair_call(): pl.pallas_call(pair_kernel, out_shape=jax.ShapeDtypeStruct(cycled.shape,...  3.64 us
    pallas_call x1, Pallas kernels, prepare_call(): pl.pallas_call(prepare_kernel, in_specs=[HERE] * 5, out_specs=[HERE] * 4...  3.48 us
  transfers between devices with their start and end apart: 2, of which 2 were waited for; matrix products, arithmetic and copies ran while one was open for 1% of the time, Pallas kernels for 9%

profile of v13, /device:TPU:1, one launch (start us, length us, event | category | flops | bytes accessed | tf_op | source)
XLA Modules:
  0.0 76.9 jit_solution(1435839999050451203)
XLA Ops:
  0.6 0.0 copy-start.2
  0.6 4.0 %forward.1 = s16[16,64,128]{2,1,0:T(8,128)(2,1)} custom-call(bf16[2,32,32,128]{3,2,1,0:T(8,128)(2,1)} %bitcast.17, bf16[128,512]{1,0:T(8,128)(2,1)} %w_in_ref.5, bf16[512,128]{1,0:T(8,128)(2,1)} %w_out_ref.5, bf16[64,128]{1,0:T(8,128)(2,1)} %bitcast.12), custom_call_target="tpu_custom_call" | custom-call | tf_op jit(solution)/shard_map/forward/pallas_call | solution.py:361
  4.6 22.2 %all-to-all-start = ((s16[512,2,128]{2,1,0:T(2,128)(2,1)}), s16[512,2,128]{2,1,0:T(2,128)(2,1)S(1)}, u32[]{:S(2)}, u32[]{:S(2)}) async-start(s16[512,2,128]{2,1,0:T(2,128)(2,1)} %bitcast.20), calls=%async_computation | async-start | bytes 524288 | tf_op jit(solution)/shard_map/all_to_all | solution.py:482
  26.8 0.8 %copy.9 = s32[64,32]{1,0:T(8,128)S(1)} copy(s32[64,32]{0,1:T(8,128)} %param.6) | data formatting | bytes 16384 | tf_op args[1]
  27.6 3.5 %prepare.1 = (bf16[2048,512]{1,0:T(8,128)(2,1)S(1)}, f32[1024,128]{1,0:T(8,128)S(1)}, bf16[32,2,16,128]{3,2,1,0:T(8,128)(2,1)S(1)}, bf16[128,512]{1,0:T(8,128)(2...) custom-call(bf16[2,32,32,128]{3,2,1,0:T(8,128)(2,1)} %bitcast.18, s32[2,32,32]{2,1,0:T(8,128)S(1)} %bitcast.16, ...), custom_call_target="tpu_custom_call" | custom-call | flops 536870912 | bytes 8388608 | tf_op jit(solution)/shard_map/prepare/pallas_call | solution.py:382
  31.1 0.0 copy-start
  31.1 0.8 %copy-done = bf16[128,2048]{1,0:T(8,128)(2,1)} copy-done((bf16[128,2048]{1,0:T(8,128)(2,1)}, bf16[128,2048]{1,0:T(8,128)(2,1)S(1)}, u32[]{:S(2)}) %copy-start) | copy-done | bytes 524312
  31.8 0.0 copy-start.1
  31.9 0.8 %copy-done.1 = bf16[128,2048]{1,0:T(8,128)(2,1)} copy-done((bf16[128,2048]{1,0:T(8,128)(2,1)}, bf16[128,2048]{1,0:T(8,128)(2,1)S(1)}, u32[]{:S(2)}) %copy-start.1) | copy-done | bytes 524312
  32.6 11.4 %all-to-all-done = s16[512,2,128]{2,1,0:T(2,128)(2,1)S(1)} async-done(((s16[512,2,128]{2,1,0:T(2,128)(2,1)}), s16[512,2,128]{2,1,0:T(2,128)(2,1)S(1)}, u32[]{:S(2)}, u32[]{:S(2)}) %all-to-all-start) | async-done | bytes 262176 | tf_op jit(solution)/shard_map/all_to_all | solution.py:482
  44.0 0.0 copy-done.2
  44.0 2.6 %weights.1 = (bf16[1024,128]{1,0:T(8,128)(2,1)S(1)}, bf16[8,160,128]{2,1,0:T(8,128)(2,1)S(1)}) custom-call(s16[16,64,128]{2,1,0:T(8,128)(2,1)S(1)} %bitcast.10, f32[1024,128]{1,0:T(8,128)S(1)} %get-tuple-element.15.logits_ref, bf16[32,2,16,128]{3,2,1,0:T(8,128)(2,1)S(1)} %get-tuple-element.16.bins_wide_ref, ...), custom_call_target="tpu_custom_call" | custom-call | tf_op jit(solution)/shard_map/weights/pallas_call | solution.py:421
  46.7 10.1 %all_to_all.15.recv_ref = bf16[8,160,128]{2,1,0:T(8,128)(2,1)S(1)} all-to-all(bf16[8,160,128]{2,1,0:T(8,128)(2,1)S(1)} %get-tuple-element.22), channel_id=1, replica_groups={{0,32,64,96,16,48,80,112},{1,33,65,97,17,49,81,113},{2,34,66,98,18,50,8..., dimensions={0} | all-to-all | bytes 655360 | tf_op jit(solution)/shard_map/all_to_all | solution.py:496
  56.7 0.9 %sum_near.1 = bf16[256,128]{1,0:T(8,128)(2,1)} custom-call(bf16[8,160,128]{2,1,0:T(8,128)(2,1)S(1)} %all_to_all.15.recv_ref), custom_call_target="tpu_custom_call" | custom-call | tf_op jit(solution)/shard_map/sum_near/pallas_call | solution.py:455
  57.7 6.4 %all-to-all-start.2 = ((bf16[64,4,128]{2,1,0:T(4,128)(2,1)}), bf16[64,4,128]{2,1,0:T(4,128)(2,1)S(1)}, u32[]{:S(2)}, u32[]{:S(2)}) async-start(bf16[64,4,128]{2,1,0:T(4,128)(2,1)} %bitcast.6), calls=%async_computation.2 | async-start | bytes 131072 | tf_op jit(solution)/shard_map/all_to_all | solution.py:513
  64.1 3.6 %pair.1 = bf16[2,32,32,128]{3,2,1,0:T(8,128)(2,1)} custom-call(bf16[1024,128]{1,0:T(8,128)(2,1)S(1)} %get-tuple-element.21.d_logit_ref, bf16[2048,512]{1,0:T(8,128)(2,1)S(1)} %get-tuple-element.17.hidden_ref, bf16[2,32,32,128]{3,2,1,0:T(8,128)(2,1)} %bitcast.19, bf16[128,512]{1,0:T(8,128)(2,1)} %w_in_ref.5, bf16[512,128]{1,0:T(8,128)(2,1)} %w_out_ref.5, ...), custom_call_target="tpu_custom_call" | custom-call | flops 536870912 | bytes 5242880 | tf_op jit(solution)/shard_map/pair/pallas_call | solution.py:440
  67.7 8.5 %all-to-all-done.2 = bf16[64,4,128]{2,1,0:T(4,128)(2,1)S(1)} async-done(((bf16[64,4,128]{2,1,0:T(4,128)(2,1)}), bf16[64,4,128]{2,1,0:T(4,128)(2,1)S(1)}, u32[]{:S(2)}, u32[]{:S(2)}) %all-to-all-start.2) | async-done | bytes 65568 | tf_op jit(solution)/shard_map/all_to_all | solution.py:513
  76.2 0.7 sum_rest.1
Async XLA Ops:
  0.6 43.4 %copy-start.2 = (bf16[128,64]{0,1:T(8,128)(2,1)S(1)}, bf16[128,64]{0,1:T(8,128)(2,1)}, u32[]{:S(2)}) copy-start(bf16[128,64]{0,1:T(8,128)(2,1)} %param.9) | copy-start | bytes 49156
  4.6 39.4 %all-to-all-start = ((s16[512,2,128]{2,1,0:T(2,128)(2,1)}), s16[512,2,128]{2,1,0:T(2,128)(2,1)S(1)}, u32[]{:S(2)}, u32[]{:S(2)}) async-start(s16[512,2,128]{2,1,0:T(2,128)(2,1)} %bitcast.20), calls=%async_computation | async-start | bytes 524288 | tf_op jit(solution)/shard_map/all_to_all | solution.py:482
  31.1 0.8 %copy-start = (bf16[128,2048]{1,0:T(8,128)(2,1)}, bf16[128,2048]{1,0:T(8,128)(2,1)S(1)}, u32[]{:S(2)}) copy-start(bf16[128,2048]{1,0:T(8,128)(2,1)S(1)} %get-tuple-element.19.normed_t_hbm) | copy-start | bytes 1572868
  31.8 0.8 %copy-start.1 = (bf16[128,2048]{1,0:T(8,128)(2,1)}, bf16[128,2048]{1,0:T(8,128)(2,1)S(1)}, u32[]{:S(2)}) copy-start(bf16[128,2048]{1,0:T(8,128)(2,1)S(1)} %get-tuple-element.20.residual_t_hbm) | copy-start | bytes 1572868
  57.7 18.6 %all-to-all-start.2 = ((bf16[64,4,128]{2,1,0:T(4,128)(2,1)}), bf16[64,4,128]{2,1,0:T(4,128)(2,1)S(1)}, u32[]{:S(2)}, u32[]{:S(2)}) async-start(bf16[64,4,128]{2,1,0:T(4,128)(2,1)} %bitcast.6), calls=%async_computation.2 | async-start | bytes 131072 | tf_op jit(solution)/shard_map/all_to_all | solution.py:513

commit v14 on v13

--- a/solution.py
+++ b/solution.py
@@ -167,7 +167,7 @@
 
     for r in range(n_row):
         rows_ref[pl.ds(r, span, stride=n_row), :] = decode(recv_ref[r])
-    sym = logits_ref[...] + rows_ref[...]
+    sym = logits_ref[...] + rows_ref[0:half, :]
     lane = lax.broadcasted_iota(jnp.int32, (1, channels), 1)
     left = lane < bins_count
     low = jnp.max(jnp.where(left, sym, -jnp.inf), axis=-1, keepdims=True)
@@ -290,7 +290,7 @@
             send_ref,
             far * 64,
         )
-    out_ref[...] = send_ref[...].astype(bf16)
+    out_ref[...] = send_ref[0 : out_ref.shape[0], :].astype(bf16)
 
 
 def pack(wide, long, head, rows_ref, send_ref, base):
@@ -361,7 +361,7 @@
     return pl.pallas_call(
         send_kernel,
         out_shape=jax.ShapeDtypeStruct((n_row, CYCLES * n_col, channels), jnp.int16),
-        scratch_shapes=[pltpu.VMEM((CYCLES * n_col * n_row, channels), jnp.int32)],
+        scratch_shapes=[pltpu.VMEM((CYCLES * n_col * n_row + n_row, channels), jnp.int32)],
         compiler_params=params(),
         name="forward",
     )(pair_rep.reshape(CYCLES, n_col, col_count, channels), w_in, w_out, w_head_t)
@@ -425,7 +425,7 @@
         out_shape=[d_logit, jax.ShapeDtypeStruct((HALVES * ACROSS, part_rows, channels), bf16)],
         scratch_shapes=[pltpu.VMEM(x.shape, x.dtype) for x in late]
         + [
-            pltpu.VMEM((pairs // CYCLES, channels), f32),
+            pltpu.VMEM((pairs // CYCLES + n_row, channels), f32),
             pltpu.SemaphoreType.DMA((len(late),)),
         ],
         compiler_params=params(ROOM),
@@ -455,7 +455,10 @@
     return pl.pallas_call(
         middle_kernel,
         out_shape=jax.ShapeDtypeStruct(shape, bf16),
-        scratch_shapes=[pltpu.VMEM((n_far, 2, 128, 128), f32), pltpu.VMEM(shape, f32)],
+        scratch_shapes=[
+            pltpu.VMEM((n_far, 2, 128, 128), f32),
+            pltpu.VMEM((shape[0] + 8, shape[1]), f32),
+        ],
         compiler_params=params(ROOM),
         name="sum_near",
     )(part)

time: 77.3 us -> 77.3 us (level)
  no operation moved by 1% of the time
where the time goes in v14:
time: 77.3 us; the launch traced here: 76.9 us
  starting transfers between devices  28.6 us (37%)
  waiting for transfers between devices  19.9 us (26%)
  Pallas kernels  15.3 us (20%)
  blocking collectives  10.1 us (13%)
  local copies, waits for them, and re-layouts  2.39 us (3%)
    all_to_all x1, starting transfers between devices, shards(): lax.all_to_all(send.reshape(n_row * n_col, CYCLES, channels), ('row', 'co...  22.2 us
    all_to_all x1, waiting for transfers between devices, shards(): lax.all_to_all(send.reshape(n_row * n_col, CYCLES, channels), ('row', 'co...  11.4 us
    all_to_all x1, blocking collectives, shards(): lax.all_to_all(part, ('row', 'col'), split_axis=0, concat_axis=0, tiled=T...  10.1 us
    all_to_all x1, waiting for transfers between devices, shards(): lax.all_to_all(share.reshape(n_far * n_half, 4, channels), ('row', 'col')...  8.54 us
    all_to_all x1, starting transfers between devices, shards(): lax.all_to_all(share.reshape(n_far * n_half, 4, channels), ('row', 'col')...  6.4 us
    pallas_call x1, Pallas kernels, forward_call(): pl.pallas_call(send_kernel, out_shape=jax.ShapeDtypeStruct((n_row, CYCLES...  3.96 us
    pallas_call x1, Pallas kernels, pair_call(): pl.pallas_call(pair_kernel, out_shape=jax.ShapeDtypeStruct(cycled.shape,...  3.64 us
    pallas_call x1, Pallas kernels, prepare_call(): pl.pallas_call(prepare_kernel, in_specs=[HERE] * 5, out_specs=[HERE] * 4...  3.48 us
  transfers between devices with their start and end apart: 2, of which 2 were waited for; matrix products, arithmetic and copies ran while one was open for 1% of the time, Pallas kernels for 9%

profile of v14, /device:TPU:1, one launch (start us, length us, event | category | flops | bytes accessed | tf_op | source)
XLA Modules:
  0.0 76.9 jit_solution(17877711343089976233)
XLA Ops:
  0.6 0.0 copy-start.2
  0.6 4.0 %forward.1 = s16[16,64,128]{2,1,0:T(8,128)(2,1)} custom-call(bf16[2,32,32,128]{3,2,1,0:T(8,128)(2,1)} %bitcast.17, bf16[128,512]{1,0:T(8,128)(2,1)} %w_in_ref.5, bf16[512,128]{1,0:T(8,128)(2,1)} %w_out_ref.5, bf16[64,128]{1,0:T(8,128)(2,1)} %bitcast.12), custom_call_target="tpu_custom_call" | custom-call | tf_op jit(solution)/shard_map/forward/pallas_call | solution.py:361
  4.6 22.2 %all-to-all-start = ((s16[512,2,128]{2,1,0:T(2,128)(2,1)}), s16[512,2,128]{2,1,0:T(2,128)(2,1)S(1)}, u32[]{:S(2)}, u32[]{:S(2)}) async-start(s16[512,2,128]{2,1,0:T(2,128)(2,1)} %bitcast.20), calls=%async_computation | async-start | bytes 524288 | tf_op jit(solution)/shard_map/all_to_all | solution.py:485
  26.8 0.8 %copy.9 = s32[64,32]{1,0:T(8,128)S(1)} copy(s32[64,32]{0,1:T(8,128)} %param.6) | data formatting | bytes 16384 | tf_op args[1]
  27.6 3.5 %prepare.1 = (bf16[2048,512]{1,0:T(8,128)(2,1)S(1)}, f32[1024,128]{1,0:T(8,128)S(1)}, bf16[32,2,16,128]{3,2,1,0:T(8,128)(2,1)S(1)}, bf16[128,512]{1,0:T(8,128)(2...) custom-call(bf16[2,32,32,128]{3,2,1,0:T(8,128)(2,1)} %bitcast.18, s32[2,32,32]{2,1,0:T(8,128)S(1)} %bitcast.16, ...), custom_call_target="tpu_custom_call" | custom-call | flops 536870912 | bytes 8388608 | tf_op jit(solution)/shard_map/prepare/pallas_call | solution.py:382
  31.1 0.0 copy-start
  31.1 0.8 %copy-done = bf16[128,2048]{1,0:T(8,128)(2,1)} copy-done((bf16[128,2048]{1,0:T(8,128)(2,1)}, bf16[128,2048]{1,0:T(8,128)(2,1)S(1)}, u32[]{:S(2)}) %copy-start) | copy-done | bytes 524312
  31.8 0.0 copy-start.1
  31.9 0.8 %copy-done.1 = bf16[128,2048]{1,0:T(8,128)(2,1)} copy-done((bf16[128,2048]{1,0:T(8,128)(2,1)}, bf16[128,2048]{1,0:T(8,128)(2,1)S(1)}, u32[]{:S(2)}) %copy-start.1) | copy-done | bytes 524312
  32.6 11.4 %all-to-all-done = s16[512,2,128]{2,1,0:T(2,128)(2,1)S(1)} async-done(((s16[512,2,128]{2,1,0:T(2,128)(2,1)}), s16[512,2,128]{2,1,0:T(2,128)(2,1)S(1)}, u32[]{:S(2)}, u32[]{:S(2)}) %all-to-all-start) | async-done | bytes 262176 | tf_op jit(solution)/shard_map/all_to_all | solution.py:485
  44.0 0.0 copy-done.2
  44.0 2.6 %weights.1 = (bf16[1024,128]{1,0:T(8,128)(2,1)S(1)}, bf16[8,160,128]{2,1,0:T(8,128)(2,1)S(1)}) custom-call(s16[16,64,128]{2,1,0:T(8,128)(2,1)S(1)} %bitcast.10, f32[1024,128]{1,0:T(8,128)S(1)} %get-tuple-element.15.logits_ref, bf16[32,2,16,128]{3,2,1,0:T(8,128)(2,1)S(1)} %get-tuple-element.16.bins_wide_ref, ...), custom_call_target="tpu_custom_call" | custom-call | tf_op jit(solution)/shard_map/weights/pallas_call | solution.py:421
  46.7 10.1 %all_to_all.15.recv_ref = bf16[8,160,128]{2,1,0:T(8,128)(2,1)S(1)} all-to-all(bf16[8,160,128]{2,1,0:T(8,128)(2,1)S(1)} %get-tuple-element.22), channel_id=1, replica_groups={{0,32,64,96,16,48,80,112},{1,33,65,97,17,49,81,113},{2,34,66,98,18,50,8..., dimensions={0} | all-to-all | bytes 655360 | tf_op jit(solution)/shard_map/all_to_all | solution.py:499
  56.7 0.9 %sum_near.1 = bf16[256,128]{1,0:T(8,128)(2,1)} custom-call(bf16[8,160,128]{2,1,0:T(8,128)(2,1)S(1)} %all_to_all.15.recv_ref), custom_call_target="tpu_custom_call" | custom-call | tf_op jit(solution)/shard_map/sum_near/pallas_call | solution.py:455
  57.7 6.4 %all-to-all-start.2 = ((bf16[64,4,128]{2,1,0:T(4,128)(2,1)}), bf16[64,4,128]{2,1,0:T(4,128)(2,1)S(1)}, u32[]{:S(2)}, u32[]{:S(2)}) async-start(bf16[64,4,128]{2,1,0:T(4,128)(2,1)} %bitcast.6), calls=%async_computation.2 | async-start | bytes 131072 | tf_op jit(solution)/shard_map/all_to_all | solution.py:516
  64.1 3.6 %pair.1 = bf16[2,32,32,128]{3,2,1,0:T(8,128)(2,1)} custom-call(bf16[1024,128]{1,0:T(8,128)(2,1)S(1)} %get-tuple-element.21.d_logit_ref, bf16[2048,512]{1,0:T(8,128)(2,1)S(1)} %get-tuple-element.17.hidden_ref, bf16[2,32,32,128]{3,2,1,0:T(8,128)(2,1)} %bitcast.19, bf16[128,512]{1,0:T(8,128)(2,1)} %w_in_ref.5, bf16[512,128]{1,0:T(8,128)(2,1)} %w_out_ref.5, ...), custom_call_target="tpu_custom_call" | custom-call | flops 536870912 | bytes 5242880 | tf_op jit(solution)/shard_map/pair/pallas_call | solution.py:440
  67.7 8.5 %all-to-all-done.2 = bf16[64,4,128]{2,1,0:T(4,128)(2,1)S(1)} async-done(((bf16[64,4,128]{2,1,0:T(4,128)(2,1)}), bf16[64,4,128]{2,1,0:T(4,128)(2,1)S(1)}, u32[]{:S(2)}, u32[]{:S(2)}) %all-to-all-start.2) | async-done | bytes 65568 | tf_op jit(solution)/shard_map/all_to_all | solution.py:516
  76.2 0.7 sum_rest.1
Async XLA Ops:
  0.6 43.4 %copy-start.2 = (bf16[128,64]{0,1:T(8,128)(2,1)S(1)}, bf16[128,64]{0,1:T(8,128)(2,1)}, u32[]{:S(2)}) copy-start(bf16[128,64]{0,1:T(8,128)(2,1)} %param.9) | copy-start | bytes 49156
  4.6 39.4 %all-to-all-start = ((s16[512,2,128]{2,1,0:T(2,128)(2,1)}), s16[512,2,128]{2,1,0:T(2,128)(2,1)S(1)}, u32[]{:S(2)}, u32[]{:S(2)}) async-start(s16[512,2,128]{2,1,0:T(2,128)(2,1)} %bitcast.20), calls=%async_computation | async-start | bytes 524288 | tf_op jit(solution)/shard_map/all_to_all | solution.py:485
  31.1 0.8 %copy-start = (bf16[128,2048]{1,0:T(8,128)(2,1)}, bf16[128,2048]{1,0:T(8,128)(2,1)S(1)}, u32[]{:S(2)}) copy-start(bf16[128,2048]{1,0:T(8,128)(2,1)S(1)} %get-tuple-element.19.normed_t_hbm) | copy-start | bytes 1572868
  31.8 0.8 %copy-start.1 = (bf16[128,2048]{1,0:T(8,128)(2,1)}, bf16[128,2048]{1,0:T(8,128)(2,1)S(1)}, u32[]{:S(2)}) copy-start(bf16[128,2048]{1,0:T(8,128)(2,1)S(1)} %get-tuple-element.20.residual_t_hbm) | copy-start | bytes 1572868
  57.7 18.6 %all-to-all-start.2 = ((bf16[64,4,128]{2,1,0:T(4,128)(2,1)}), bf16[64,4,128]{2,1,0:T(4,128)(2,1)S(1)}, u32[]{:S(2)}, u32[]{:S(2)}) async-start(bf16[64,4,128]{2,1,0:T(4,128)(2,1)} %bitcast.6), calls=%async_computation.2 | async-start | bytes 131072 | tf_op jit(solution)/shard_map/all_to_all | solution.py:516
